TPU v7x, 256 devices: a whole 4x4x8 slice. The times are simulated.
256 devices in a mesh: row: 32 (over y, z), ka: 8 (over x, core).
Axes of the slice: x: 4, y: 4, z: 8, core: 2. Of those that a mesh axis runs over, the one named last changes fastest.
Arguments:
- pair_table: int32 [8], replicated, may hold values from 0 to 7, as said below
- cholesky: bfloat16 [8, 3000, 3072], P('ka', None, 'row'), may hold values from -0.875 to 0.875
- amplitudes: bfloat16 [8, 3072, 3072], P('ka', 'row'), may hold values from -0.109375 to 0.109375
- denominators: float32 [8, 3072, 3072], P('ka', 'row'), may hold values from 1 to 6
Outputs:
- new_amplitudes: bfloat16 [8, 3072, 3072], P('ka', 'row')
Inputs may be any that keep to these rules, and one draw needn't show every extreme that they name: `pair_table`: blocks may couple to any block, to themselves too, and several blocks may couple to the same one.
All inputs are finite; a program needn't handle non-finite values.
Results may differ from a plain program's by a relative error of at most 0.0046.
Values may be sent and summed in bfloat16 or wider, within the bound.
No kernel may reach another device: no remote copies, remote signals or barrier semaphores. Data moves between devices by JAX's collectives and lax.ppermute only.
A program may use at most 192 MiB of HBM per device.

v0:
```python
import jax
import jax.numpy as jnp
from jax import lax
from jax.sharding import PartitionSpec as P


def shards(pair_table, cholesky, amplitudes, denominators):
    wanted = pair_table[lax.axis_index("ka")]
    amps = amplitudes[0]
    denom = denominators[0]
    piece = lax.all_gather(cholesky, "ka", axis=0, tiled=True)
    ids = jnp.arange(piece.shape[0], dtype=jnp.int32)
    onehot = (ids == wanted).astype(jnp.float32)
    chosen = jnp.einsum("k,kln->ln", onehot, piece.astype(jnp.float32))
    chol_local = chosen.astype(jnp.bfloat16)
    chol_full = lax.all_gather(chol_local, "row", axis=1, tiled=True)
    tx = lax.dot_general(
        amps, chol_full, (((1,), (1,)), ((), ())), preferred_element_type=jnp.float32
    )
    columns = lax.all_to_all(amps, "row", split_axis=1, concat_axis=0, tiled=True)
    cycle = jnp.dot(chol_full, columns, preferred_element_type=jnp.float32)
    left = (jnp.transpose(chol_local.astype(jnp.float32)) + tx).astype(jnp.bfloat16)
    right = (chol_local.astype(jnp.float32) + cycle).astype(jnp.bfloat16)
    prod = jnp.dot(
        left, lax.all_gather(right, "row", axis=1, tiled=True), preferred_element_type=jnp.float32
    )
    return (-prod / denom).astype(jnp.bfloat16)[None]


def solution(mesh):
    in_specs = (P(), P("ka", None, "row"), P("ka", "row", None), P("ka", "row", None))
    out_specs = P("ka", "row", None)
    return jax.shard_map(shards, mesh=mesh, in_specs=in_specs, out_specs=out_specs, check_vma=False)
```

profile of v0, /device:TPU:2, one launch (start us, length us, event | category | flops | bytes accessed | tf_op | source)
XLA Modules:
  0.0 483.3 jit_solution(227682376947074820)
XLA Ops:
  6.5 0.0 all-gather.4.cloned.1.call-start
  6.5 0.7 all-gather.4.cloned.1.call-update
  7.3 0.0 all-gather.6.cloned.1.call-start
  7.3 1.2 dynamic_slice.3
  8.5 39.5 %all-gather.4.cloned.1.call-done = bf16[8,3000,96]{1,2,0:T(8,128)(2,1)} async-done(((bf16[1,3000,96]{1,2,0:T(8,128)(2,1)}), bf16[8,3000,96]{1,2,0:T(8,128)(2,1)}) %all-gather.4.cloned.1.call-update) | async-done | bytes 4608016 | tf_op jit(solution)/shard_map/all_gather | solution.py:11
  48.0 35.5 %fusion = bf16[1,3000,96]{0,1,2:T(8,128)(2,1)} fusion(bf16[8,3000,96]{1,2,0:T(8,128)(2,1)} %all-gather.4.cloned.1.call-done, s32[]{:T(128)} %bitcast), kind=kOutput, calls=%fused_computation | convolution fusion | flops 4608008 | bytes 5184004 | tf_op jit(solution)/shard_map/k,kln->ln/dot_general | solution.py:14
  83.5 0.0 copy-start.1
  83.5 56.4 %copy.9 = bf16[1,3000,96]{1,2,0:T(8,128)(2,1)} copy(bf16[1,3000,96]{0,1,2:T(8,128)(2,1)} %fusion) | data formatting | bytes 1152000 | tf_op jit(solution)/shard_map/k,kln->ln/dot_general | solution.py:14
  139.9 0.0 copy-start
  139.9 0.0 all-gather.6.cloned.1.call-update
  139.9 0.0 all-gather.8.cloned.1.call-start
  140.0 0.0 copy-done.1
  140.0 0.4 copy.6
  140.4 37.3 %all_to_all.19 = bf16[96,32,96]{0,2,1:T(8,128)(2,1)S(1)} all-to-all(bf16[96,32,96]{0,2,1:T(8,128)(2,1)S(1)} %bitcast.32), channel_id=1, replica_groups=mesh['row'=32,'ka'=8] {'row'}, dimensions={1} | all-to-all | bytes 1179648 | tf_op jit(solution)/shard_map/all_to_all | solution.py:20
  177.7 0.3 copy.7
  178.0 1.1 all_to_all.17
  179.0 0.0 copy-start.2
  179.1 123.0 %all-gather.6.cloned.1.call-done = bf16[3000,3072]{0,1:T(8,128)(2,1)} async-done(((bf16[3000,96]{0,1:T(8,128)(2,1)}), bf16[3000,3072]{0,1:T(8,128)(2,1)}) %all-gather.6.cloned.1.call-update) | async-done | bytes 18432016 | tf_op jit(solution)/shard_map/all_gather | solution.py:16
  302.0 0.0 copy-done
  302.0 10.3 %fusion.3 = bf16[3000,96]{0,1:T(8,128)(2,1)} fusion(bf16[3000,3072]{0,1:T(8,128)(2,1)} %all-gather.6.cloned.1.call-done, bf16[3072,96]{0,1:T(8,128)(2,1)S(1)} %all_to_all.17, bf16[1,3000,96]{1,2,0:T(8,128)(2,1)S(1)} %copy-done), kind=kOutput, calls=%fused_computation.6 | convolution fusion | flops 1770336000 | bytes 20173824 | tf_op jit(solution)/shard_map/dot_general | solution.py:21
  312.3 0.0 all-gather.8.cloned.1.call-update
  312.3 148.0 %all-gather.8.cloned.1.call-done = bf16[3000,3072]{0,1:T(8,128)(2,1)} async-done(((bf16[3000,96]{0,1:T(8,128)(2,1)}), bf16[3000,3072]{0,1:T(8,128)(2,1)}) %all-gather.8.cloned.1.call-update) | async-done | bytes 18432016 | tf_op jit(solution)/shard_map/all_gather | solution.py:25
  460.3 0.0 copy-done.2
  460.3 16.4 %fusion.6 = bf16[1,96,3072]{2,1,0:T(8,128)(2,1)} fusion(bf16[3000,3072]{0,1:T(8,128)(2,1)} %all-gather.8.cloned.1.call-done, bf16[3000,3072]{0,1:T(8,128)(2,1)} %all-gather.6.cloned.1.call-done, f32[1,96,3072]{2,1,0:T(8,128)S(1)} %copy-done.2, bf16[1,96,3072]{2,1,0:T(8,128)(2,1)S(1)} %copy-done.1, bf16[1,3000,96]{1,2,0:T(8,128)(2,1)S(1)} %copy-done), kind=kOutput, calls=%fused_computation.9 | convolution fusion | flops 3540692736 | bytes 39799296 | tf_op jit(solution)/shard_map/dot_general | solution.py:24
Async XLA Ops:
  6.5 41.5 %all-gather.4.cloned.1.call-start = ((), (), s32[]{:S(2)}) async-start(), calls=%async_computation.1 | async-start | bytes 5308416 | tf_op jit(solution)/shard_map/all_gather | solution.py:11
  7.3 294.8 %all-gather.6.cloned.1.call-start = ((), (), s32[]{:S(2)}) async-start(), calls=%async_computation.2 | async-start | bytes 19464192 | tf_op jit(solution)/shard_map/all_gather | solution.py:16
  83.5 56.5 %copy-start.1 = (bf16[1,96,3072]{2,1,0:T(8,128)(2,1)S(1)}, bf16[1,96,3072]{2,1,0:T(8,128)(2,1)}, u32[]{:S(2)}) copy-start(bf16[1,96,3072]{2,1,0:T(8,128)(2,1)} %param.6) | copy-start | bytes 1769476
  139.9 162.1 %copy-start = (bf16[1,3000,96]{1,2,0:T(8,128)(2,1)S(1)}, bf16[1,3000,96]{1,2,0:T(8,128)(2,1)}, u32[]{:S(2)}) copy-start(bf16[1,3000,96]{1,2,0:T(8,128)(2,1)} %copy.9) | copy-start | bytes 1728004
  139.9 320.4 %all-gather.8.cloned.1.call-start = ((), (), s32[]{:S(2)}) async-start(), calls=%async_computation.3 | async-start | bytes 19464192 | tf_op jit(solution)/shard_map/all_gather | solution.py:25
  179.0 281.3 %copy-start.2 = (f32[1,96,3072]{2,1,0:T(8,128)S(1)}, f32[1,96,3072]{2,1,0:T(8,128)}, u32[]{:S(2)}) copy-start(f32[1,96,3072]{2,1,0:T(8,128)} %param.7) | copy-start | bytes 3538948
Sparse Core Ops, SparseCore 0:
  9.2 38.8 all-gather.3
  140.1 161.9 all-gather.5
  312.4 147.8 all-gather.7
where the time goes:
time: 485 us; the launch traced here: 483 us
  waiting for transfers between devices  311 us (64%)
  matrix products  62.1 us (13%)
  local copies, waits for them, and re-layouts  59.4 us (12%)
  blocking collectives  37.3 us (8%)
  between operations  13.1 us (3%)
    all_gather x1, waiting for transfers between devices, shards(): lax.all_gather(right, 'row', axis=1, tiled=True)  148 us
    all_gather x1, waiting for transfers between devices, shards(): chol_full = lax.all_gather(chol_local, 'row', axis=1, tiled=True)  123 us
    dot_general x1, local copies, waits for them, and re-layouts, shards(): chosen = jnp.einsum('k,kln->ln', onehot, piece.astype(jnp.float32))  56.4 us
    all_gather x1, waiting for transfers between devices, shards(): piece = lax.all_gather(cholesky, 'ka', axis=0, tiled=True)  39.5 us
    all_to_all x1, blocking collectives, shards(): lax.all_to_all(amps, 'row', split_axis=1, concat_axis=0, tiled=True)  37.3 us
    dot_general x1, matrix products, shards(): chosen = jnp.einsum('k,kln->ln', onehot, piece.astype(jnp.float32))  35.5 us
    dot_general x1, matrix products, shards(): jnp.dot(left, lax.all_gather(right, 'row', axis=1, tiled=True), preferred...  16.4 us
    dot_general x1, matrix products, shards(): cycle = jnp.dot(chol_full, columns, preferred_element_type=jnp.float32)  10.3 us
  transfers between devices with their start and end apart: 3, of which 3 were waited for; matrix products, arithmetic and copies ran while one was open for 0% of the time, Pallas kernels for 0%

commit v1 on v0

v1 whole, which is shorter than its diff:
```python
import jax
import jax.numpy as jnp
from jax import lax
from jax.sharding import Mesh
from jax.sharding import PartitionSpec as P

NY, NZ, NX, NC = 4, 8, 4, 2
BF, F32 = jnp.bfloat16, jnp.float32
SIZES = {"y": NY, "z": NZ, "x": NX, "c": NC}


def shift(block, axis, step):
    n = SIZES[axis]
    return lax.ppermute(block, axis, [(i, (i + step) % n) for i in range(n)])


def pick(blocks, index):
    return lax.select_n(index, *blocks)


def halves(block):
    h = block.shape[0] // 2
    return block[:h], block[h:]


def shards(pair_table, cholesky, amplitudes, denominators):
    y, x, c = lax.axis_index("y"), lax.axis_index("x"), lax.axis_index("c")
    q = x * NC + c
    amps = amplitudes[0]
    pairs, naux = amps.shape[0], cholesky.shape[1]
    aux = -(-naux // (128 * NY)) * 128
    width = NZ * pairs

    amps_i = lax.all_gather(amps, "z", axis=0, tiled=True)
    amps_j = lax.all_gather(amps, "y", axis=0, tiled=True)

    own = jnp.pad(jnp.transpose(cholesky[0]), ((0, 0), (0, NY * aux - naux)))
    slices = jnp.transpose(own.reshape(pairs, NY, aux), (1, 0, 2))
    mine = lax.all_to_all(slices, "y", split_axis=0, concat_axis=0, tiled=True).reshape(NY * pairs, aux)

    fore, back = shift(mine, "x", 1), shift(mine, "x", -1)
    low, high = halves(fore)[0], halves(back)[1]
    far = jnp.concatenate([shift(low, "x", 1), shift(high, "x", -1)], axis=0)
    blocks = [mine, back, far, fore]
    wanted, theirs = pair_table[q], pair_table[q + 1 - 2 * c]
    sent = shift(pick(blocks, (theirs // NC - x) % NX), "c", 1)
    chosen = jnp.where(wanted % NC == c, pick(blocks, (wanted // NC - x) % NX), sent)

    full = lax.all_gather(chosen.reshape(NY, pairs, aux), "z", axis=1, tiled=False)
    full = full.reshape(NY * width, aux)

    left = (chosen.astype(F32) + jnp.dot(amps_j, full, preferred_element_type=F32)).astype(BF)
    part = [
        lax.dot_general(left, full[i * width : (i + 1) * width], (((1,), (1,)), ((), ())), preferred_element_type=F32).astype(BF)
        for i in range(NY)
    ]
    part = lax.all_to_all(jnp.stack(part), "y", split_axis=0, concat_axis=0, tiled=True)
    total = jnp.sum(part.astype(F32), axis=0)
    prod = jnp.dot(total.astype(BF), amps_i, preferred_element_type=F32)
    place = lax.dynamic_update_slice(jnp.zeros_like(prod), total, (0, y * width))
    prod = (prod + place).astype(BF).reshape(NY, pairs, NY * width)
    prod = lax.all_to_all(prod, "y", split_axis=0, concat_axis=0, tiled=True)
    return (-jnp.sum(prod.astype(F32), axis=0) / denominators[0]).astype(BF)[None]


def solution(mesh):
    grid = Mesh(mesh.devices.reshape(NY, NZ, NX, NC), ("y", "z", "x", "c"))
    ka, row = ("x", "c"), ("y", "z")
    in_specs = (P(), P(ka, None, row), P(ka, row, None), P(ka, row, None))
    return jax.shard_map(shards, mesh=grid, in_specs=in_specs, out_specs=P(ka, row, None), check_vma=False)
```

time: 485 us -> 260 us (0.54)
  waiting for transfers between devices: 311 us -> 151 us
  matrix products: 62.1 us -> 13.3 us
  local copies, waits for them, and re-layouts: 59.4 us -> 12 us
  blocking collectives: 37.3 us -> 47.7 us
  starting transfers between devices: 0.08 us -> 8.33 us
  other arithmetic: 0 us -> 7.01 us
  between operations: 13.1 us -> 18.7 us
    all_gather x3, waiting for transfers between devices: 310 us -> 105 us  [the longest x1 59.6 us: shards(): lax.all_gather(chosen.reshape(NY, pairs, aux), 'z', axis=1, tiled=False)]
    dot_general x1 -> x0, local copies, waits for them, and re-layouts: 56.4 us -> none  [shards(): chosen = jnp.einsum('k,kln->ln', onehot, piece.astype(jnp.float32))]
    dot_general x3 -> x6, matrix products: 62.1 us -> 13.3 us  [the longest x1 5.85 us: shards(): jnp.dot(amps_j, full, preferred_element_type=F32)]
    all_to_all x0 -> x1, waiting for transfers between devices: none -> 29.4 us  [shards(): lax.all_to_all(jnp.stack(part), 'y', split_axis=0, concat_axis=0, tiled=T...]
    ppermute x0 -> x5, waiting for transfers between devices: none -> 15.7 us  [shift(): return lax.ppermute(block, axis, [(i, (i + step) % n) for i in range(n)])]
    all_to_all x1 -> x2, blocking collectives: 37.3 us -> 47.7 us  [the longest x1 33.2 us: shards(): prod = lax.all_to_all(prod, 'y', split_axis=0, concat_axis=0, tiled=True)]
    all_gather x0 -> x1, local copies, waits for them, and re-layouts: none -> 5.02 us  [shards(): lax.all_gather(chosen.reshape(NY, pairs, aux), 'z', axis=1, tiled=False)]
  transfers between devices with their start and end apart: 3 -> 9, of which waited for: 3 -> 7; matrix products, arithmetic and copies ran while one was open for 0% -> 7% of each run, Pallas kernels for 0% -> 0%
where the time goes in v1:
time: 260 us; the launch traced here: 259 us
  waiting for transfers between devices  151 us (58%)
  blocking collectives  47.7 us (18%)
  between operations  18.7 us (7%)
  matrix products  13.3 us (5%)
  local copies, waits for them, and re-layouts  12 us (5%)
  starting transfers between devices  8.33 us (3%)
  other arithmetic  7.01 us (3%)
    all_gather x1, waiting for transfers between devices, shards(): lax.all_gather(chosen.reshape(NY, pairs, aux), 'z', axis=1, tiled=False)  59.6 us
    all_to_all x1, blocking collectives, shards(): prod = lax.all_to_all(prod, 'y', split_axis=0, concat_axis=0, tiled=True)  33.2 us
    all_to_all x1, waiting for transfers between devices, shards(): lax.all_to_all(jnp.stack(part), 'y', split_axis=0, concat_axis=0, tiled=T...  29.4 us
    all_gather x1, waiting for transfers between devices, shards(): amps_j = lax.all_gather(amps, 'y', axis=0, tiled=True)  29.3 us
    all_gather x1, waiting for transfers between devices, shards(): amps_i = lax.all_gather(amps, 'z', axis=0, tiled=True)  16.2 us
    ppermute x5, waiting for transfers between devices, shift(): return lax.ppermute(block, axis, [(i, (i + step) % n) for i in range(n)])  15.7 us
    all_to_all x1, blocking collectives, shards(): lax.all_to_all(slices, 'y', split_axis=0, concat_axis=0, tiled=True)  14.4 us
    dot_general x1, matrix products, shards(): jnp.dot(amps_j, full, preferred_element_type=F32)  5.85 us
  transfers between devices with their start and end apart: 9, of which 7 were waited for; matrix products, arithmetic and copies ran while one was open for 7% of the time, Pallas kernels for 0%

profile of v1, /device:TPU:2, one launch (start us, length us, event | category | flops | bytes accessed | tf_op | source)
XLA Modules:
  0.0 258.5 jit_solution(16645464835616980149)
XLA Ops:
  6.5 0.0 all-gather.6.cloned.1.call-start
  6.5 1.1 pad.4
  7.6 0.4 reshape.24
  8.1 0.1 copy.19
  8.1 14.4 %all_to_all.15 = bf16[4,96,768]{2,1,0:T(8,128)(2,1)S(1)} all-to-all(bf16[4,96,768]{2,1,0:T(8,128)(2,1)S(1)} %copy.19), channel_id=1, replica_groups=mesh['y'=4,'z'=8,'x'=4,'c'=2] {'y'}, dimensions={0} | all-to-all | bytes 1179648 | tf_op jit(solution)/shard_map/all_to_all | solution.py:39
  22.6 0.3 copy.21
  22.9 1.6 collective-permute-start.1
  24.5 0.5 collective-permute-start
  25.0 11.6 %collective-permute-done.1 = bf16[384,768]{0,1:T(8,128)(2,1)S(1)} collective-permute-done((bf16[384,768]{0,1:T(8,128)(2,1)S(1)}, bf16[384,768]{0,1:T(8,128)(2,1)S(1)}, u32[]{:S(2)}, u32[]{:S(2)}) %collective-permute-start.1) | collective-permute-done | bytes 589856 | tf_op jit(solution)/shard_map/ppermute | solution.py:14
  36.6 1.6 collective-permute-start.2
  38.2 0.0 collective-permute-done
  38.2 0.2 slice.41
  38.3 0.6 collective-permute-start.3
  39.0 0.7 fusion.14
  42.4 2.7 %collective-permute-done.2 = bf16[192,768]{0,1:T(8,128)(2,1)S(1)} collective-permute-done((bf16[192,768]{0,1:T(8,128)(2,1)S(1)}, bf16[192,768]{0,1:T(8,128)(2,1)S(1)}, u32[]{:S(2)}, u32[]{:S(2)}) %collective-permute-start.2) | collective-permute-done | bytes 294944 | tf_op jit(solution)/shard_map/ppermute | solution.py:14
  45.1 1.5 collective-permute-done.3
  46.6 0.4 select_select_fusion
  47.0 0.1 collective-permute-start.4
  49.8 0.0 collective-permute-done.4
  49.8 1.6 select_select_fusion.1
  51.3 1.1 copy.24
  52.4 0.0 all-gather.6.cloned.1.call-update
  52.5 0.0 all-gather.8.cloned.1.call-start
  52.5 0.7 all-gather.8.cloned.1.call-update
  53.2 0.2 all-gather.10.cloned.1.call-start
  53.4 0.5 all-gather.10.cloned.1.call-update
  53.9 59.6 %all-gather.6.cloned.1.call-done = bf16[4,8,96,768]{3,2,0,1:T(8,128)(2,1)} async-done(((bf16[4,1,96,768]{3,2,0,1:T(8,128)(2,1)}), bf16[4,8,96,768]{3,2,0,1:T(8,128)(2,1)}) %all-gather.6.cloned.1.call-update) | async-done | bytes 4718608 | tf_op jit(solution)/shard_map/all_gather | solution.py:49
  113.6 5.0 %copy.25 = bf16[4,8,96,768]{3,2,1,0:T(8,128)(2,1)} copy(bf16[4,8,96,768]{3,2,0,1:T(8,128)(2,1)} %all-gather.6.cloned.1.call-done) | data formatting | bytes 9437184 | tf_op jit(solution)/shard_map/all_gather | solution.py:49
  118.6 1.7 fusion.13
  120.3 29.3 %all-gather.8.cloned.1.call-done = bf16[1,384,3072]{2,1,0:T(8,128)(2,1)} async-done(((bf16[1,96,3072]{2,1,0:T(8,128)(2,1)}), bf16[1,384,3072]{2,1,0:T(8,128)(2,1)}) %all-gather.8.cloned.1.call-update) | async-done | bytes 2359312 | tf_op jit(solution)/shard_map/all_gather | solution.py:35
  149.6 5.8 %add_convert_fusion = bf16[384,768]{0,1:T(8,128)(2,1)S(1)} fusion(bf16[384,768]{0,1:T(8,128)(2,1)S(1)} %select_select_fusion.1, bf16[3072,768]{1,0:T(8,128)(2,1)} %bitcast.48, bf16[1,384,3072]{2,1,0:T(8,128)(2,1)} %all-gather.8.cloned.1.call-done), kind=kOutput, calls=%fused_computation.19 | convolution fusion | flops 1812824064 | bytes 8257536 | tf_op jit(solution)/shard_map/dot_general | solution.py:52
  155.5 0.7 fusion.7
  156.1 0.6 copy-done.2
  156.7 0.7 fusion.8
  157.4 0.7 fusion.9
  158.1 0.7 fusion.10
  158.8 1.7 pad_maximum_fusion
  160.5 3.7 %all-to-all-start.1 = ((bf16[4,384,768]{2,1,0:T(8,128)(2,1)}), bf16[4,384,768]{2,1,0:T(8,128)(2,1)S(1)}, u32[]{:S(2)}, u32[]{:S(2)}) async-start(bf16[4,384,768]{2,1,0:T(8,128)(2,1)} %pad_maximum_fusion), calls=%async_computation.1 | async-start | bytes 4718592 | tf_op jit(solution)/shard_map/all_to_all | solution.py:57
  164.2 29.4 %all-to-all-done.1 = bf16[4,384,768]{2,1,0:T(8,128)(2,1)S(1)} async-done(((bf16[4,384,768]{2,1,0:T(8,128)(2,1)}), bf16[4,384,768]{2,1,0:T(8,128)(2,1)S(1)}, u32[]{:S(2)}, u32[]{:S(2)}) %all-to-all-start.1) | async-done | bytes 2359328 | tf_op jit(solution)/shard_map/all_to_all | solution.py:57
  193.6 1.3 convert_reduce_fusion.1
  195.0 16.2 %all-gather.10.cloned.1.call-done = bf16[1,768,3072]{2,1,0:T(8,128)(2,1)} async-done(((bf16[1,96,3072]{2,1,0:T(8,128)(2,1)}), bf16[1,768,3072]{2,1,0:T(8,128)(2,1)}) %all-gather.10.cloned.1.call-update) | async-done | bytes 4718608 | tf_op jit(solution)/shard_map/all_gather | solution.py:34
  211.2 4.7 %fusion = f32[384,3072]{1,0:T(8,128)S(1)} fusion(bf16[1,768,3072]{2,1,0:T(8,128)(2,1)} %all-gather.10.cloned.1.call-done, f32[384,768]{1,0:T(8,128)} %convert_reduce_fusion.1), kind=kOutput, calls=%fused_computation | convolution fusion | flops 1812234240 | bytes 10616832 | tf_op jit(solution)/shard_map/dot_general | solution.py:59
  215.9 0.2 add_dynamic-update-slice_fusion
  216.2 0.3 convert_element_type.44
  216.5 33.2 %all_to_all.16 = bf16[4,96,3072]{2,1,0:T(8,128)(2,1)S(1)} all-to-all(bf16[4,96,3072]{2,1,0:T(8,128)(2,1)S(1)} %bitcast.47), channel_id=1, replica_groups=mesh['y'=4,'z'=8,'x'=4,'c'=2] {'y'}, dimensions={0} | all-to-all | bytes 4718592 | tf_op jit(solution)/shard_map/all_to_all | solution.py:62
  249.7 0.4 convert_reduce_fusion
  250.1 0.9 copy-done.4
  251.0 1.0 fusion.11
  (11 shorter events, 0.0 us)
Async XLA Ops:
  6.5 107.0 %all-gather.6.cloned.1.call-start = ((), (), s32[]{:S(2)}) async-start(), calls=%async_computation.3 | async-start | bytes 5308416 | tf_op jit(solution)/shard_map/all_gather | solution.py:49
  22.6 16.4 %copy-start.5 = (s32[8]{0:T(128)S(1)}, s32[8]{0:T(128)}, u32[]{:S(2)}) copy-start(s32[8]{0:T(128)} %param.4) | copy-start | bytes 100
  22.9 13.7 %collective-permute-start.1 = (bf16[384,768]{0,1:T(8,128)(2,1)S(1)}, bf16[384,768]{0,1:T(8,128)(2,1)S(1)}, u32[]{:S(2)}, u32[]{:S(2)}) collective-permute-start(bf16[384,768]{0,1:T(8,128)(2,1)S(1)} %copy.21), channel_id=1, source_target_pairs={{0,2},{2,4},{4,6},{6,0},{1,3},{3,5},{5,7},{7,1},{8,10},{10,12},{12... | collective-permute-start | bytes 1769480 | tf_op jit(solution)/shard_map/ppermute | solution.py:14
  24.5 13.7 %collective-permute-start = (bf16[384,768]{0,1:T(8,128)(2,1)S(1)}, bf16[384,768]{0,1:T(8,128)(2,1)S(1)}, u32[]{:S(2)}, u32[]{:S(2)}) collective-permute-start(bf16[384,768]{0,1:T(8,128)(2,1)S(1)} %copy.21), channel_id=1, source_target_pairs={{0,6},{2,0},{4,2},{6,4},{1,7},{3,1},{5,3},{7,5},{8,14},{10,8},{12,... | collective-permute-start | bytes 1769480 | tf_op jit(solution)/shard_map/ppermute | solution.py:14
  36.6 8.5 %collective-permute-start.2 = (bf16[192,768]{0,1:T(8,128)(2,1)S(1)}, bf16[192,768]{0,1:T(8,128)(2,1)S(1)}, u32[]{:S(2)}, u32[]{:S(2)}) collective-permute-start(bf16[192,768]{0,1:T(8,128)(2,1)S(1)} %slice.40), channel_id=1, source_target_pairs={{0,2},{2,4},{4,6},{6,0},{1,3},{3,5},{5,7},{7,1},{8,10},{10,12},{12... | collective-permute-start | bytes 884744 | tf_op jit(solution)/shard_map/ppermute | solution.py:14
  38.3 8.2 %collective-permute-start.3 = (bf16[192,768]{0,1:T(8,128)(2,1)S(1)}, bf16[192,768]{0,1:T(8,128)(2,1)S(1)}, u32[]{:S(2)}, u32[]{:S(2)}) collective-permute-start(bf16[192,768]{0,1:T(8,128)(2,1)S(1)} %slice.41), channel_id=1, source_target_pairs={{0,6},{2,0},{4,2},{6,4},{1,7},{3,1},{5,3},{7,5},{8,14},{10,8},{12,... | collective-permute-start | bytes 884744 | tf_op jit(solution)/shard_map/ppermute | solution.py:14
  47.0 2.7 %collective-permute-start.4 = (bf16[384,768]{0,1:T(8,128)(2,1)S(1)}, bf16[384,768]{0,1:T(8,128)(2,1)}, u32[]{:S(2)}, u32[]{:S(2)}) collective-permute-start(bf16[384,768]{0,1:T(8,128)(2,1)S(1)} %select_select_fusion), channel_id=1, source_target_pairs={{0,1},{1,0},{2,3},{3,2},{4,5},{5,4},{6,7},{7,6},{8,9},{9,8},{10,11... | collective-permute-start | bytes 1769480 | tf_op jit(solution)/shard_map/ppermute | solution.py:14
  52.5 97.1 %all-gather.8.cloned.1.call-start = ((), (), s32[]{:S(2)}) async-start(), calls=%async_computation.4 | async-start | bytes 2949120 | tf_op jit(solution)/shard_map/all_gather | solution.py:35
  53.2 158.0 %all-gather.10.cloned.1.call-start = ((), (), s32[]{:S(2)}) async-start(), calls=%async_computation.5 | async-start | bytes 5308416 | tf_op jit(solution)/shard_map/all_gather | solution.py:34
  113.6 5.0 %copy-start = (bf16[4,8,96,768]{3,2,0,1:T(8,128)(2,1)S(1)}, bf16[4,8,96,768]{3,2,0,1:T(8,128)(2,1)}, u32[]{:S(2)}) copy-start(bf16[4,8,96,768]{3,2,0,1:T(8,128)(2,1)} %all-gather.6.cloned.1.call-done) | copy-start | bytes 14155780
  149.6 5.9 %copy-start.3 = (bf16[1,8,96,768]{3,2,1,0:T(8,128)(2,1)S(1)}, bf16[1,8,96,768]{3,2,1,0:T(8,128)(2,1)}, u32[]{:S(2)}) copy-start(bf16[1,8,96,768]{3,2,1,0:T(8,128)(2,1)} %get-tuple-element.5) | copy-start | bytes 3538948
  155.5 1.3 copy-start.2
  160.5 33.1 %all-to-all-start.1 = ((bf16[4,384,768]{2,1,0:T(8,128)(2,1)}), bf16[4,384,768]{2,1,0:T(8,128)(2,1)S(1)}, u32[]{:S(2)}, u32[]{:S(2)}) async-start(bf16[4,384,768]{2,1,0:T(8,128)(2,1)} %pad_maximum_fusion), calls=%async_computation.1 | async-start | bytes 4718592 | tf_op jit(solution)/shard_map/all_to_all | solution.py:57
  195.0 20.9 %copy-start.1 = (f32[384,768]{1,0:T(8,128)S(1)}, f32[384,768]{1,0:T(8,128)}, u32[]{:S(2)}) copy-start(f32[384,768]{1,0:T(8,128)} %convert_reduce_fusion.1) | copy-start | bytes 3538948
  249.7 1.3 copy-start.4
Sparse Core Ops, SparseCore 0:
  52.6 60.9 all-gather.5
  115.4 34.1 all-gather.7
  151.4 59.7 all-gather.9

commit v2 on v1

v2 whole, which is shorter than its diff:
```python
import functools

import jax
import jax.numpy as jnp
from jax import lax
from jax.experimental import pallas as pl
from jax.experimental.pallas import tpu as pltpu
from jax.sharding import Mesh
from jax.sharding import PartitionSpec as P

NY, NZ, NX, NC = 4, 8, 4, 2
BF, F32 = jnp.bfloat16, jnp.float32
SIZES = {"y": NY, "z": NZ, "x": NX, "c": NC}
ANY = pl.BlockSpec(memory_space=pl.ANY)
VMEM = pl.BlockSpec(memory_space=pltpu.VMEM)
SMEM = pl.BlockSpec(memory_space=pltpu.SMEM)


def params(mib):
    return pltpu.CompilerParams(vmem_limit_bytes=mib * 2**20)


def shift(block, axis, step):
    n = SIZES[axis]
    with jax.named_scope(f"{axis}{step}_{block.size * 2 // 1000}kB"):
        return lax.ppermute(block, axis, [(i, (i + step) % n) for i in range(n)])


def dot(a, b):
    return jnp.dot(a, b, preferred_element_type=F32)


def dot_t(a, b):
    return lax.dot_general(a, b, (((1,), (1,)), ((), ())), preferred_element_type=F32)


def cost(flops):
    return pl.CostEstimate(flops=flops, bytes_accessed=8 * 2**20, transcendentals=0)


def swap_kernel(place_ref, table_ref, held_ref, sent_ref, sems):
    c = place_ref[2]
    copies = []
    for k in range(NX):
        want = table_ref[k * NC + 1 - c]
        copies.append(pltpu.make_async_copy(held_ref.at[want >> 1], sent_ref.at[k], sems.at[k]))
        copies[-1].start()
    for copy in copies:
        copy.wait()


def mine_kernel(place_ref, table_ref, held_ref, sent_ref, amps_ref, mine_ref, out_ref, sems):
    c = place_ref[2]
    amps = pltpu.make_async_copy(amps_ref, out_ref, sems.at[NX])
    amps.start()
    for k in range(NX):
        want = table_ref[k * NC + c]
        here = (want & 1) == c

        @pl.when(here)
        def _():
            pltpu.make_async_copy(held_ref.at[want >> 1], mine_ref.at[k], sems.at[k]).start()

        @pl.when(jnp.logical_not(here))
        def _():
            pltpu.make_async_copy(sent_ref.at[k], mine_ref.at[k], sems.at[k]).start()

    for k in range(NX):
        pltpu.make_async_copy(sent_ref.at[k], mine_ref.at[k], sems.at[k]).wait()
    amps.wait()


def choose(kernel, results, place, table, *arrays):
    return pl.pallas_call(
        kernel,
        out_shape=[jax.ShapeDtypeStruct(a.shape, a.dtype) for a in results],
        in_specs=[SMEM, SMEM] + [ANY] * len(arrays),
        out_specs=[ANY] * len(results),
        scratch_shapes=[pltpu.SemaphoreType.DMA((NX + 1,))],
        compiler_params=params(2),
    )(place, table, *arrays)


def join_kernel(parts_ref, first_ref, chosen_ref, sems):
    copies = [pltpu.make_async_copy(parts_ref.at[k], chosen_ref.at[:, k], sems.at[k]) for k in range(NX)]
    for copy in copies:
        copy.start()
    for copy in copies:
        copy.wait()


def join(parts, first):
    nx, ny, third, aux = parts.shape
    return pl.pallas_call(
        join_kernel,
        out_shape=jax.ShapeDtypeStruct((ny, nx, third, aux), BF),
        in_specs=[ANY] * 2,
        out_specs=ANY,
        scratch_shapes=[pltpu.SemaphoreType.DMA((NX,))],
        compiler_params=params(2),
    )(parts, first)


def left_kernel(dist, place_ref, amps_ref, *refs):
    blocks, (left_ref, full_ref, sems) = refs[:-3], refs[-3:]
    z, rows = place_ref[1], blocks[0].shape[0]
    copies = []
    for n, d in enumerate(dist):
        copies.append(pltpu.make_async_copy(blocks[n], full_ref.at[(z + NZ + d) % NZ], sems.at[n]))
        copies[-1].start()
    for n, d in enumerate(dist):
        at = (z + NZ + d) % NZ
        copies[n].wait()
        block = full_ref[at]
        part = dot(amps_ref[:, pl.ds(pl.multiple_of(at * rows, 128), rows)], block)
        if n:
            left_ref[...] += part
        else:
            left_ref[...] = block.astype(F32) + part


def partial_kernel(pairs, place_ref, amps_ref, left_ref, full_ref, far_a_ref, far_b_ref, late_ref, own_ref, *refs):
    send_refs, (later_ref, left, sem) = refs[:-3], refs[-3:]
    later = pltpu.make_async_copy(late_ref, later_ref, sem)
    later.start()
    y, z, rows = place_ref[0], place_ref[1], left_ref.shape[0]
    last = (z + NZ // 2) % NZ
    amps = amps_ref[:, pl.ds(pl.multiple_of(last * rows, 128), rows)]
    h = far_a_ref.shape[1]
    for at, far in ((0, far_a_ref), (h, far_b_ref)):
        cols = pl.ds(at, h)
        left[:, cols] = (left_ref[:, cols] + dot(amps, far[...])).astype(BF)
    for n, d in enumerate((2, 1, 3, 0)):
        at = pl.ds(pl.multiple_of((y + d) % NY * pairs, 32), pairs)
        far = jnp.concatenate([far_a_ref[at], far_b_ref[at]], axis=1)
        block = jnp.concatenate([jnp.where(last == k, far, full_ref[k, at]) for k in range(NZ)], axis=0)
        part = dot_t(left[...], block)
        if d:
            send_refs[n][...] = part.astype(BF)
        else:
            own_ref[...] = part
    later.wait()


def out_kernel(pairs, first, place_ref, total_ref, amps_ref, own_ref, *refs):
    send_refs, (total, rows, amps, sems) = refs[:-4], refs[-4:]
    y = place_ref[0]
    width = total_ref.shape[1]
    step = amps.shape[2]
    copies = [
        pltpu.make_async_copy(amps_ref.at[:, pl.ds(k * step, step)], amps.at[k], sems.at[k])
        for k in range(amps.shape[0])
    ]
    for copy in copies:
        copy.start()
    for d in range(NY):
        block = total_ref[pl.ds(pl.multiple_of((y + d) % NY * pairs, 32), pairs)]
        total[d * pairs : (d + 1) * pairs] = block
        rows[d * pairs : (d + 1) * pairs] = block.astype(BF)
    for k, copy in enumerate(copies):
        n, part = divmod(first + k * step, width)
        cols = pl.ds(k * step, step)
        copy.wait()
        prod = dot(rows[...], amps[k])
        prod += jnp.where(y == n, total[:, part : part + step], 0.0)
        own_ref[:, cols] = prod[:pairs]
        for d in range(1, NY):
            send_refs[d - 1][:, cols] = prod[d * pairs : (d + 1) * pairs].astype(BF)


def out_products(place, total, amps_i, first, pairs):
    rows, cols = amps_i.shape
    step = total.shape[1] // 2
    return pl.pallas_call(
        functools.partial(out_kernel, pairs, first),
        out_shape=[jax.ShapeDtypeStruct((pairs, cols), F32)] + [jax.ShapeDtypeStruct((pairs, cols), BF)] * (NY - 1),
        in_specs=[SMEM, VMEM, ANY],
        out_specs=[VMEM] * NY,
        scratch_shapes=[
            pltpu.VMEM(total.shape, F32),
            pltpu.VMEM(total.shape, BF),
            pltpu.VMEM((cols // step, rows, step), BF),
            pltpu.SemaphoreType.DMA((cols // step,)),
        ],
        compiler_params=params(10),
        cost_estimate=cost(2 * total.size * cols),
    )(place, total, amps_i)


def shards(pair_table, cholesky, amplitudes, denominators):
    y, z, x, c = (lax.axis_index(a) for a in ("y", "z", "x", "c"))
    place = jnp.stack([y, z, c])
    amps = amplitudes[0]
    pairs, naux = amps.shape[0], cholesky.shape[1]
    aux = -(-naux // (128 * NY)) * 128
    width = NZ * pairs
    rows = NY * pairs
    third = pairs // NX

    early = 4 * NY * width // 8
    amps_i0 = lax.all_gather(amps[:, :early], "z", axis=0, tiled=True)
    by_z = jnp.transpose(amps.reshape(pairs, NY, NZ, pairs), (0, 2, 1, 3)).reshape(pairs, NY * width)

    own = jnp.pad(jnp.transpose(cholesky[0]), ((0, 0), (0, NY * aux - naux)))
    own = jnp.transpose(own.reshape(NX, third, NY, aux), (0, 2, 1, 3)).reshape(NX * NY, third, aux)
    held = lax.all_to_all(own, ("x", "y"), split_axis=0, concat_axis=0, tiled=True).reshape(NX, NY, third, aux)
    (sent,) = choose(swap_kernel, (held,), place, pair_table, held)
    mine, by_z = choose(mine_kernel, (held, by_z), place, pair_table, held, shift(sent, "c", 1), by_z)
    amps_j = lax.all_gather(by_z, "y", axis=0, tiled=True)
    parts = lax.all_to_all(mine, "x", split_axis=0, concat_axis=0, tiled=True)
    chosen = join(parts, amps_i0).reshape(rows, aux)

    dist, blocks = [0], [chosen]
    fore = back = chosen
    for s in range(1, NZ // 2):
        fore, back = shift(fore, "z", 1), shift(back, "z", -1)
        dist += [-s, s]
        blocks += [fore, back]
    h = aux // 2
    far_a, far_b = shift(fore[:, :h], "z", 1), shift(back[:, h:], "z", -1)

    left, full = pl.pallas_call(
        functools.partial(left_kernel, dist),
        out_shape=[
            jax.ShapeDtypeStruct((rows, aux), F32),
            jax.ShapeDtypeStruct((NZ, rows, aux), BF),
        ],
        in_specs=[SMEM, VMEM] + [ANY] * len(blocks),
        out_specs=[VMEM] * 2,
        scratch_shapes=[pltpu.SemaphoreType.DMA((len(blocks),))],
        compiler_params=params(8),
        cost_estimate=cost(2 * rows * aux * rows * len(blocks)),
    )(place, amps_j, *blocks)
    late = amps[:, early:]
    total, *send, later = pl.pallas_call(
        functools.partial(partial_kernel, pairs),
        out_shape=[jax.ShapeDtypeStruct((rows, width), F32)] + [jax.ShapeDtypeStruct((rows, width), BF)] * (NY - 1)
        + [jax.ShapeDtypeStruct(late.shape, BF)],
        in_specs=[SMEM] + [VMEM] * 5 + [ANY],
        out_specs=[VMEM] * NY + [ANY],
        scratch_shapes=[pltpu.VMEM((rows, aux), BF), pltpu.SemaphoreType.DMA],
        compiler_params=params(8),
        cost_estimate=cost(2 * rows * aux * (rows + NY * width)),
    )(place, amps_j, left, full, far_a, far_b, late)
    amps_i1 = lax.all_gather(later, "z", axis=0, tiled=True)
    parts = [shift(part, "y", d) for part, d in zip(send, (2, 1, 3))]
    for part in parts:
        total = total + part.astype(F32)

    outs = []
    for first, amps_i in ((0, amps_i0), (early, amps_i1)):
        out, *send = out_products(place, total, amps_i, first, pairs)
        for d in (2, 1, 3):
            out = out + shift(send[d - 1], "y", d).astype(F32)
        outs.append(out)
    return (-jnp.concatenate(outs, axis=1) / denominators[0]).astype(BF)[None]


def solution(mesh):
    grid = Mesh(mesh.devices.reshape(NY, NZ, NX, NC), ("y", "z", "x", "c"))
    ka, row = ("x", "c"), ("y", "z")
    in_specs = (P(), P(ka, None, row), P(ka, row, None), P(ka, row, None))
    return jax.shard_map(shards, mesh=grid, in_specs=in_specs, out_specs=P(ka, row, None), check_vma=False)
```

time: 260 us -> 180 us (0.69)
  waiting for transfers between devices: 151 us -> 79.1 us
  blocking collectives: 47.7 us -> 14 us
  starting transfers between devices: 8.33 us -> 36.1 us
  Pallas kernels: 0 us -> 16.9 us
  matrix products: 13.3 us -> 0 us
  local copies, waits for them, and re-layouts: 12 us -> 18.3 us
  other arithmetic: 7.01 us -> 1.56 us
  between operations: 18.7 us -> 13.3 us
    all_gather x3, waiting for transfers between devices: 105 us -> 10.4 us  [the longest x1 5.3 us: shards(): amps_i1 = lax.all_gather(later, 'z', axis=0, tiled=True)]
    ppermute x5 -> x18, waiting for transfers between devices: 15.7 us -> 58.8 us  [shift(): return lax.ppermute(block, axis, [(i, (i + step) % n) for i in range(n)])]
    all_to_all x2 -> x1, blocking collectives: 47.7 us -> 14 us  [shards(): parts = lax.all_to_all(mine, 'x', split_axis=0, concat_axis=0, tiled=True)]
    ppermute x5 -> x18, starting transfers between devices: 4.38 us -> 28.4 us  [shift(): return lax.ppermute(block, axis, [(i, (i + step) % n) for i in range(n)])]
    all_to_all x1, waiting for transfers between devices: 29.4 us -> 9.9 us  [shards(): lax.all_to_all(own, ('x', 'y'), split_axis=0, concat_axis=0, tiled=True)]
    pallas_call x0 -> x7, Pallas kernels: none -> 16.9 us  [the longest x2 5.59 us: out_products(): pl.pallas_call(functools.partial(out_kernel, pairs, first), out_shape=[ja...]
    dot_general x6 -> x0, matrix products: 13.3 us -> none  [the longest x1 5.85 us: shards(): jnp.dot(amps_j, full, preferred_element_type=F32)]
    unnamed x12 -> x26, local copies, waits for them, and re-layouts: 1.47 us -> 9.44 us
  transfers between devices with their start and end apart: 9 -> 22, of which waited for: 7 -> 9; matrix products, arithmetic and copies ran while one was open for 7% -> 4% of each run, Pallas kernels for 0% -> 8%
where the time goes in v2:
time: 180 us; the launch traced here: 179 us
  waiting for transfers between devices  79.1 us (44%)
  starting transfers between devices  36.1 us (20%)
  local copies, waits for them, and re-layouts  18.3 us (10%)
  Pallas kernels  16.9 us (9%)
  blocking collectives  14 us (8%)
  between operations  13.3 us (7%)
    ppermute x18, waiting for transfers between devices, shift(): return lax.ppermute(block, axis, [(i, (i + step) % n) for i in range(n)])  58.8 us
    ppermute x18, starting transfers between devices, shift(): return lax.ppermute(block, axis, [(i, (i + step) % n) for i in range(n)])  28.4 us
    all_to_all x1, blocking collectives, shards(): parts = lax.all_to_all(mine, 'x', split_axis=0, concat_axis=0, tiled=True)  14 us
    all_to_all x1, waiting for transfers between devices, shards(): lax.all_to_all(own, ('x', 'y'), split_axis=0, concat_axis=0, tiled=True)  9.9 us
    unnamed x26, local copies, waits for them, and re-layouts  9.44 us
    all_to_all x1, starting transfers between devices, shards(): lax.all_to_all(own, ('x', 'y'), split_axis=0, concat_axis=0, tiled=True)  7.61 us
    pallas_call x2, Pallas kernels, out_products(): pl.pallas_call(functools.partial(out_kernel, pairs, first), out_shape=[ja...  5.59 us
    all_gather x1, waiting for transfers between devices, shards(): amps_i1 = lax.all_gather(later, 'z', axis=0, tiled=True)  5.3 us
  transfers between devices with their start and end apart: 22, of which 9 were waited for; matrix products, arithmetic and copies ran while one was open for 4% of the time, Pallas kernels for 8%

profile of v2, /device:TPU:2, one launch (start us, length us, event | category | flops | bytes accessed | tf_op | source)
XLA Modules:
  0.0 179.4 jit_solution(12925710148883228899)
XLA Ops:
  6.5 1.9 %fusion.2 = (bf16[96,1536]{1,0:T(8,128)(2,1)S(1)}, bf16[96,1536]{1,0:T(8,128)(2,1)}) fusion(bf16[96,3072]{1,0:T(8,128)(2,1)} %bitcast.25), kind=kLoop, calls=%fused_computation.8 | loop fusion | bytes 1179648 | tf_op jit(solution)/shard_map/slice | solution.py:234
  8.5 0.4 reshape.44
  8.9 0.9 copy.5
  9.8 7.6 %all-to-all-start = ((bf16[16,24,768]{2,1,0:T(8,128)(2,1)}), bf16[16,24,768]{2,1,0:T(8,128)(2,1)S(1)}, u32[]{:S(2)}, u32[]{:S(2)}) async-start(bf16[16,24,768]{2,1,0:T(8,128)(2,1)} %bitcast.6), calls=%async_computation | async-start | bytes 1179648 | tf_op jit(solution)/shard_map/all_to_all | solution.py:206
  17.6 9.9 %all-to-all-done = bf16[16,24,768]{2,1,0:T(8,128)(2,1)S(1)} async-done(((bf16[16,24,768]{2,1,0:T(8,128)(2,1)}), bf16[16,24,768]{2,1,0:T(8,128)(2,1)S(1)}, u32[]{:S(2)}, u32[]{:S(2)}) %all-to-all-start) | async-done | bytes 589856 | tf_op jit(solution)/shard_map/all_to_all | solution.py:206
  27.5 1.4 shard_map.46
  29.0 1.6 reshape_squeeze.3
  30.6 1.5 copy.8
  32.1 1.1 reshape.47.amps_ref
  33.1 1.4 shard_map.47
  34.6 14.0 %all_to_all.10.parts_ref = bf16[4,4,24,768]{3,2,1,0:T(8,128)(2,1)S(1)} all-to-all(bf16[4,4,24,768]{3,2,1,0:T(8,128)(2,1)S(1)} %get-tuple-element.23), channel_id=1, replica_groups=mesh['y'=4,'z'=8,'x'=4,'c'=2] {'x'}, dimensions={0} | all-to-all | bytes 1179648 | tf_op jit(solution)/shard_map/all_to_all | solution.py:210
  48.6 5.1 %all-gather.6.cloned.1.call-done.first_ref.amps_ref = bf16[768,1536]{1,0:T(8,128)(2,1)} async-done(((bf16[96,1536]{1,0:T(8,128)(2,1)}), bf16[768,1536]{1,0:T(8,128)(2,1)}) %all-gather.6.cloned.1.call-update) | async-done | bytes 2359312 | tf_op jit(solution)/shard_map/all_gather | solution.py:201
  53.7 1.7 copy-done.2
  55.4 0.2 shard_map.48
  55.6 1.2 collective-permute-start.1
  56.8 2.1 %collective-permute-start.2 = (bf16[384,768]{1,0:T(8,128)(2,1)S(1)}, bf16[384,768]{1,0:T(8,128)(2,1)S(1)}, u32[]{:S(2)}, u32[]{:S(2)}) collective-permute-start(bf16[384,768]{1,0:T(8,128)(2,1)S(1)} %bitcast.21), channel_id=1, source_target_pairs={{0,56},{8,0},{16,8},{24,16},{32,24},{40,32},{48,40},{56,48},{1,57}... | collective-permute-start | bytes 1769480 | tf_op jit(solution)/shard_map/z-1_589kB/ppermute | solution.py:26
  58.9 10.8 %collective-permute-done.1.refs_1_ = bf16[384,768]{1,0:T(8,128)(2,1)S(1)} collective-permute-done((bf16[384,768]{1,0:T(8,128)(2,1)S(1)}, bf16[384,768]{1,0:T(8,128)(2,1)S(1)}, u32[]{:S(2)}, u32[]{:S(2)}) %collective-permute-start.1) | collective-permute-done | bytes 589856 | tf_op jit(solution)/shard_map/z1_589kB/ppermute | solution.py:26
  69.7 3.2 %collective-permute-start.4 = (bf16[384,768]{1,0:T(8,128)(2,1)S(1)}, bf16[384,768]{1,0:T(8,128)(2,1)S(1)}, u32[]{:S(2)}, u32[]{:S(2)}) collective-permute-start(bf16[384,768]{1,0:T(8,128)(2,1)S(1)} %collective-permute-done.2.refs_2_), channel_id=1, source_target_pairs={{0,56},{8,0},{16,8},{24,16},{32,24},{40,32},{48,40},{56,48},{1,57}... | collective-permute-start | bytes 1769480 | tf_op jit(solution)/shard_map/z-1_589kB/ppermute | solution.py:26
  73.0 10.1 %collective-permute-done.3.refs_3_ = bf16[384,768]{1,0:T(8,128)(2,1)S(1)} collective-permute-done((bf16[384,768]{1,0:T(8,128)(2,1)S(1)}, bf16[384,768]{1,0:T(8,128)(2,1)S(1)}, u32[]{:S(2)}, u32[]{:S(2)}) %collective-permute-start.3) | collective-permute-done | bytes 589856 | tf_op jit(solution)/shard_map/z1_589kB/ppermute | solution.py:26
  83.1 0.9 copy-done.5
  84.0 3.2 %collective-permute-start.6 = (bf16[384,768]{1,0:T(8,128)(2,1)S(1)}, bf16[384,768]{1,0:T(8,128)(2,1)S(1)}, u32[]{:S(2)}, u32[]{:S(2)}) collective-permute-start(bf16[384,768]{1,0:T(8,128)(2,1)S(1)} %collective-permute-done.4.refs_4_), channel_id=1, source_target_pairs={{0,56},{8,0},{16,8},{24,16},{32,24},{40,32},{48,40},{56,48},{1,57}... | collective-permute-start | bytes 1769480 | tf_op jit(solution)/shard_map/z-1_589kB/ppermute | solution.py:26
  87.2 8.4 %collective-permute-done.5.refs_5_ = bf16[384,768]{1,0:T(8,128)(2,1)S(1)} collective-permute-done((bf16[384,768]{1,0:T(8,128)(2,1)S(1)}, bf16[384,768]{1,0:T(8,128)(2,1)S(1)}, u32[]{:S(2)}, u32[]{:S(2)}) %collective-permute-start.5) | collective-permute-done | bytes 589856 | tf_op jit(solution)/shard_map/z1_589kB/ppermute | solution.py:26
  95.6 0.8 slice.17
  96.4 0.7 slice.18
  97.1 3.2 %collective-permute-start.8 = (bf16[384,384]{1,0:T(8,128)(2,1)}, bf16[384,384]{1,0:T(8,128)(2,1)}, u32[]{:S(2)}, u32[]{:S(2)}) collective-permute-start(bf16[384,384]{1,0:T(8,128)(2,1)} %slice.18), channel_id=1, source_target_pairs={{0,56},{8,0},{16,8},{24,16},{32,24},{40,32},{48,40},{56,48},{1,57}... | collective-permute-start | bytes 884744 | tf_op jit(solution)/shard_map/z-1_294kB/ppermute | solution.py:26
  100.4 1.7 copy-done
  102.0 1.1 copy-done.6
  103.1 1.1 copy-done.8
  104.2 5.0 %shard_map.49 = (f32[384,768]{1,0:T(8,128)S(1)}, bf16[8,384,768]{2,1,0:T(8,128)(2,1)S(1)}) custom-call(s32[3]{0:T(128)S(1)} %pad_add_fusion.place_ref, bf16[384,3072]{1,0:T(8,128)(2,1)S(1)} %copy-done, bf16[384,768]{1,0:T(8,128)(2,1)S(1)} %bitcast.22, bf16[384,768]{1,0:T(8,128)(2,1)S(1)} %collective-permute-done.1.refs_1_, ...), custom_call_target="tpu_custom_call" | custom-call | flops 1585446912 | bytes 8388608 | tf_op jit(solution)/shard_map/pallas_call | solution.py:222
  109.2 3.4 %shard_map.50 = (f32[384,768]{1,0:T(8,128)S(1)}, bf16[384,768]{1,0:T(8,128)(2,1)S(1)}, bf16[384,768]{1,0:T(8,128)(2,1)S(1)}, bf16[384,768]{1,0:T(8,128)(2,1)S(1)}, bf16[96,1536]{1,0:T(8,128)(2,1)}) custom-call(s32[3]{0:T(128)S(1)} %pad_add_fusion.place_ref, bf16[384,3072]{1,0:T(8,128)(2,1)S(1)} %copy-done.1, f32[384,768]{1,0:T(8,128)S(1)} %get-tuple-element.24.left_ref, ...), custom_call_target="tpu_custom_call" | custom-call | flops 2038431744 | bytes 8388608 | tf_op jit(solution)/shard_map/pallas_call | solution.py:235
  112.6 1.2 collective-permute-start.10
  113.8 2.1 %collective-permute-start.11 = (bf16[384,768]{1,0:T(8,128)(2,1)S(1)}, bf16[384,768]{1,0:T(8,128)(2,1)S(1)}, u32[]{:S(2)}, u32[]{:S(2)}) collective-permute-start(bf16[384,768]{1,0:T(8,128)(2,1)S(1)} %get-tuple-element.29), channel_id=1, source_target_pairs={{0,192},{64,0},{128,64},{192,128},{1,193},{65,1},{129,65},{193,129... | collective-permute-start | bytes 1769480 | tf_op jit(solution)/shard_map/y3_589kB/ppermute | solution.py:26
  115.9 1.5 collective-permute-start.9
  117.4 22.0 %collective-permute-done.10 = bf16[384,768]{1,0:T(8,128)(2,1)S(1)} collective-permute-done((bf16[384,768]{1,0:T(8,128)(2,1)S(1)}, bf16[384,768]{1,0:T(8,128)(2,1)S(1)}, u32[]{:S(2)}, u32[]{:S(2)}) %collective-permute-start.10) | collective-permute-done | bytes 589856 | tf_op jit(solution)/shard_map/y1_589kB/ppermute | solution.py:26
  139.4 0.3 convert_add_fusion.total_ref
  139.7 1.4 copy-done.3
  141.1 2.8 %shard_map.51 = (f32[96,1536]{1,0:T(8,128)S(1)}, bf16[96,1536]{1,0:T(8,128)(2,1)S(1)}, bf16[96,1536]{1,0:T(8,128)(2,1)S(1)}, bf16[96,1536]{1,0:T(8,128)(2,1)S(1)}) custom-call(s32[3]{0:T(128)S(1)} %pad_add_fusion.place_ref, f32[384,768]{1,0:T(8,128)S(1)} %convert_add_fusion.total_ref, bf16[768,1536]{1,0:T(8,128)(2,1)S(1)} %copy-done.3), custom_call_target="tpu_custom_call" | custom-call | flops 905969664 | bytes 8388608 | tf_op jit(solution)/shard_map/pallas_call | solution.py:174
  144.0 4.1 %collective-permute-start.13 = (bf16[96,1536]{1,0:T(8,128)(2,1)S(1)}, bf16[96,1536]{1,0:T(8,128)(2,1)S(1)}, u32[]{:S(2)}, u32[]{:S(2)}) collective-permute-start(bf16[96,1536]{1,0:T(8,128)(2,1)S(1)} %get-tuple-element.32), channel_id=1, source_target_pairs={{0,64},{64,128},{128,192},{192,0},{1,65},{65,129},{129,193},{193,1... | collective-permute-start | bytes 884744 | tf_op jit(solution)/shard_map/y1_294kB/ppermute | solution.py:26
  148.1 5.3 %all-gather.8.cloned.1.call-done.amps_ref = bf16[768,1536]{1,0:T(8,128)(2,1)} async-done(((bf16[96,1536]{1,0:T(8,128)(2,1)}), bf16[768,1536]{1,0:T(8,128)(2,1)}) %all-gather.8.cloned.1.call-update) | async-done | bytes 2359312 | tf_op jit(solution)/shard_map/all_gather | solution.py:245
  153.4 1.7 copy-done.4
  155.1 2.8 %shard_map.52 = (f32[96,1536]{1,0:T(8,128)S(1)}, bf16[96,1536]{1,0:T(8,128)(2,1)S(1)}, bf16[96,1536]{1,0:T(8,128)(2,1)S(1)}, bf16[96,1536]{1,0:T(8,128)(2,1)S(1)}) custom-call(s32[3]{0:T(128)S(1)} %pad_add_fusion.place_ref, f32[384,768]{1,0:T(8,128)S(1)} %convert_add_fusion.total_ref, bf16[768,1536]{1,0:T(8,128)(2,1)S(1)} %copy-done.4), custom_call_target="tpu_custom_call" | custom-call | flops 905969664 | bytes 8388608 | tf_op jit(solution)/shard_map/pallas_call | solution.py:174
  157.9 3.1 %collective-permute-start.15 = (bf16[96,1536]{1,0:T(8,128)(2,1)S(1)}, bf16[96,1536]{1,0:T(8,128)(2,1)S(1)}, u32[]{:S(2)}, u32[]{:S(2)}) collective-permute-start(bf16[96,1536]{1,0:T(8,128)(2,1)S(1)} %get-tuple-element.36), channel_id=1, source_target_pairs={{0,128},{64,192},{128,0},{192,64},{1,129},{65,193},{129,1},{193,65... | collective-permute-start | bytes 884744 | tf_op jit(solution)/shard_map/y2_294kB/ppermute | solution.py:26
  161.0 0.6 collective-permute-start.16
  161.6 2.6 %collective-permute-start.17 = (bf16[96,1536]{1,0:T(8,128)(2,1)S(1)}, bf16[96,1536]{1,0:T(8,128)(2,1)S(1)}, u32[]{:S(2)}, u32[]{:S(2)}) collective-permute-start(bf16[96,1536]{1,0:T(8,128)(2,1)S(1)} %get-tuple-element.38), channel_id=1, source_target_pairs={{0,192},{64,0},{128,64},{192,128},{1,193},{65,1},{129,65},{193,129... | collective-permute-start | bytes 884744 | tf_op jit(solution)/shard_map/y3_294kB/ppermute | solution.py:26
  164.3 4.3 %collective-permute-done.15 = bf16[96,1536]{1,0:T(8,128)(2,1)S(1)} collective-permute-done((bf16[96,1536]{1,0:T(8,128)(2,1)S(1)}, bf16[96,1536]{1,0:T(8,128)(2,1)S(1)}, u32[]{:S(2)}, u32[]{:S(2)}) %collective-permute-start.15) | collective-permute-done | bytes 294944 | tf_op jit(solution)/shard_map/y2_294kB/ppermute | solution.py:26
  168.6 3.1 %collective-permute-done.16 = bf16[96,1536]{1,0:T(8,128)(2,1)S(1)} collective-permute-done((bf16[96,1536]{1,0:T(8,128)(2,1)S(1)}, bf16[96,1536]{1,0:T(8,128)(2,1)S(1)}, u32[]{:S(2)}, u32[]{:S(2)}) %collective-permute-start.16) | collective-permute-done | bytes 294944 | tf_op jit(solution)/shard_map/y1_294kB/ppermute | solution.py:26
  171.7 0.1 add_bitcast_fusion
  171.8 1.0 fusion.1
  (47 shorter events, 0.6 us)
Async XLA Ops:
  6.5 1.9 %copy-start.12 = (bf16[1,3000,96]{1,2,0:T(8,128)(2,1)S(1)}, bf16[1,3000,96]{1,2,0:T(8,128)(2,1)}, u32[]{:S(2)}) copy-start(bf16[1,3000,96]{1,2,0:T(8,128)(2,1)} %param.5) | copy-start | bytes 1728004
  6.5 47.2 %all-gather.6.cloned.1.call-start = ((), (), s32[]{:S(2)}) async-start(), calls=%async_computation.3 | async-start | bytes 2654208 | tf_op jit(solution)/shard_map/all_gather | solution.py:201
  8.9 18.5 %copy-start.9 = (s32[8]{0:T(128)S(1)}, s32[8]{0:T(128)}, u32[]{:S(2)}) copy-start(s32[8]{0:T(128)} %table_ref.3) | copy-start | bytes 100
  9.8 19.1 %copy-start.10 = (bf16[1,96,3072]{2,1,0:T(8,128)(2,1)S(1)}, bf16[1,96,3072]{2,1,0:T(8,128)(2,1)}, u32[]{:S(2)}) copy-start(bf16[1,96,3072]{2,1,0:T(8,128)(2,1)} %param.6) | copy-start | bytes 1769476
  9.8 17.6 %all-to-all-start = ((bf16[16,24,768]{2,1,0:T(8,128)(2,1)}), bf16[16,24,768]{2,1,0:T(8,128)(2,1)S(1)}, u32[]{:S(2)}, u32[]{:S(2)}) async-start(bf16[16,24,768]{2,1,0:T(8,128)(2,1)} %bitcast.6), calls=%async_computation | async-start | bytes 1179648 | tf_op jit(solution)/shard_map/all_to_all | solution.py:206
  17.4 82.9 %all-gather.4.cloned.1.call-start = ((), (), s32[]{:S(2)}) async-start(), calls=%async_computation.2 | async-start | bytes 2949120 | tf_op jit(solution)/shard_map/all_gather | solution.py:209
  28.8 4.3 %collective-permute-start = (bf16[4,4,24,768]{3,2,1,0:T(8,128)(2,1)S(1)}, bf16[4,4,24,768]{3,2,1,0:T(8,128)(2,1)S(1)}, u32[]{:S(2)}, u32[]{:S(2)}) collective-permute-start(bf16[4,4,24,768]{3,2,1,0:T(8,128)(2,1)S(1)} %shard_map.46), channel_id=1, source_target_pairs={{0,1},{1,0},{2,3},{3,2},{4,5},{5,4},{6,7},{7,6},{8,9},{9,8},{10,11... | collective-permute-start | bytes 1769480 | tf_op jit(solution)/shard_map/c1_589kB/ppermute | solution.py:26
  34.6 118.8 %all-gather.8.cloned.1.call-start = ((), (), s32[]{:S(2)}) async-start(), calls=%async_computation.4 | async-start | bytes 2654208 | tf_op jit(solution)/shard_map/all_gather | solution.py:245
  53.7 1.7 copy-start.2
  55.6 14.1 %collective-permute-start.1 = (bf16[384,768]{1,0:T(8,128)(2,1)S(1)}, bf16[384,768]{1,0:T(8,128)(2,1)S(1)}, u32[]{:S(2)}, u32[]{:S(2)}) collective-permute-start(bf16[384,768]{1,0:T(8,128)(2,1)S(1)} %bitcast.20), channel_id=1, source_target_pairs={{0,8},{8,16},{16,24},{24,32},{32,40},{40,48},{48,56},{56,0},{1,9},... | collective-permute-start | bytes 1769480 | tf_op jit(solution)/shard_map/z1_589kB/ppermute | solution.py:26
  56.8 12.9 %collective-permute-start.2 = (bf16[384,768]{1,0:T(8,128)(2,1)S(1)}, bf16[384,768]{1,0:T(8,128)(2,1)S(1)}, u32[]{:S(2)}, u32[]{:S(2)}) collective-permute-start(bf16[384,768]{1,0:T(8,128)(2,1)S(1)} %bitcast.21), channel_id=1, source_target_pairs={{0,56},{8,0},{16,8},{24,16},{32,24},{40,32},{48,40},{56,48},{1,57}... | collective-permute-start | bytes 1769480 | tf_op jit(solution)/shard_map/z-1_589kB/ppermute | solution.py:26
  69.7 13.4 %collective-permute-start.3 = (bf16[384,768]{1,0:T(8,128)(2,1)S(1)}, bf16[384,768]{1,0:T(8,128)(2,1)S(1)}, u32[]{:S(2)}, u32[]{:S(2)}) collective-permute-start(bf16[384,768]{1,0:T(8,128)(2,1)S(1)} %collective-permute-done.1.refs_1_), channel_id=1, source_target_pairs={{0,8},{8,16},{16,24},{24,32},{32,40},{40,48},{48,56},{56,0},{1,9},... | collective-permute-start | bytes 1769480 | tf_op jit(solution)/shard_map/z1_589kB/ppermute | solution.py:26
  69.7 14.2 %collective-permute-start.4 = (bf16[384,768]{1,0:T(8,128)(2,1)S(1)}, bf16[384,768]{1,0:T(8,128)(2,1)S(1)}, u32[]{:S(2)}, u32[]{:S(2)}) collective-permute-start(bf16[384,768]{1,0:T(8,128)(2,1)S(1)} %collective-permute-done.2.refs_2_), channel_id=1, source_target_pairs={{0,56},{8,0},{16,8},{24,16},{32,24},{40,32},{48,40},{56,48},{1,57}... | collective-permute-start | bytes 1769480 | tf_op jit(solution)/shard_map/z-1_589kB/ppermute | solution.py:26
  83.1 12.5 %collective-permute-start.5 = (bf16[384,768]{1,0:T(8,128)(2,1)S(1)}, bf16[384,768]{1,0:T(8,128)(2,1)S(1)}, u32[]{:S(2)}, u32[]{:S(2)}) collective-permute-start(bf16[384,768]{1,0:T(8,128)(2,1)S(1)} %collective-permute-done.3.refs_3_), channel_id=1, source_target_pairs={{0,8},{8,16},{16,24},{24,32},{32,40},{40,48},{48,56},{56,0},{1,9},... | collective-permute-start | bytes 1769480 | tf_op jit(solution)/shard_map/z1_589kB/ppermute | solution.py:26
  83.1 0.9 copy-start.5
  84.0 12.4 %copy-start.7 = (bf16[384,768]{1,0:T(8,128)(2,1)}, bf16[384,768]{1,0:T(8,128)(2,1)S(1)}, u32[]{:S(2)}) copy-start(bf16[384,768]{1,0:T(8,128)(2,1)S(1)} %collective-permute-done.4.refs_4_) | copy-start | bytes 1769476
  84.0 12.4 %collective-permute-start.6 = (bf16[384,768]{1,0:T(8,128)(2,1)S(1)}, bf16[384,768]{1,0:T(8,128)(2,1)S(1)}, u32[]{:S(2)}, u32[]{:S(2)}) collective-permute-start(bf16[384,768]{1,0:T(8,128)(2,1)S(1)} %collective-permute-done.4.refs_4_), channel_id=1, source_target_pairs={{0,56},{8,0},{16,8},{24,16},{32,24},{40,32},{48,40},{56,48},{1,57}... | collective-permute-start | bytes 1769480 | tf_op jit(solution)/shard_map/z-1_589kB/ppermute | solution.py:26
  96.4 12.8 %collective-permute-start.7 = (bf16[384,384]{1,0:T(8,128)(2,1)}, bf16[384,384]{1,0:T(8,128)(2,1)S(1)}, u32[]{:S(2)}, u32[]{:S(2)}) collective-permute-start(bf16[384,384]{1,0:T(8,128)(2,1)} %slice.17), channel_id=1, source_target_pairs={{0,8},{8,16},{16,24},{24,32},{32,40},{40,48},{48,56},{56,0},{1,9},... | collective-permute-start | bytes 884744 | tf_op jit(solution)/shard_map/z1_294kB/ppermute | solution.py:26
  97.1 12.0 %collective-permute-start.8 = (bf16[384,384]{1,0:T(8,128)(2,1)}, bf16[384,384]{1,0:T(8,128)(2,1)}, u32[]{:S(2)}, u32[]{:S(2)}) collective-permute-start(bf16[384,384]{1,0:T(8,128)(2,1)} %slice.18), channel_id=1, source_target_pairs={{0,56},{8,0},{16,8},{24,16},{32,24},{40,32},{48,40},{56,48},{1,57}... | collective-permute-start | bytes 884744 | tf_op jit(solution)/shard_map/z-1_294kB/ppermute | solution.py:26
  100.4 1.7 copy-start
  102.0 1.1 copy-start.6
  103.1 1.1 copy-start.8
  104.2 5.0 %copy-start.1 = (bf16[384,3072]{1,0:T(8,128)(2,1)S(1)}, bf16[384,3072]{1,0:T(8,128)(2,1)}, u32[]{:S(2)}) copy-start(bf16[384,3072]{1,0:T(8,128)(2,1)} %all-gather.4.cloned.1.call-done.amps_ref) | copy-start | bytes 7077892
  112.6 26.8 %collective-permute-start.10 = (bf16[384,768]{1,0:T(8,128)(2,1)S(1)}, bf16[384,768]{1,0:T(8,128)(2,1)S(1)}, u32[]{:S(2)}, u32[]{:S(2)}) collective-permute-start(bf16[384,768]{1,0:T(8,128)(2,1)S(1)} %get-tuple-element.28), channel_id=1, source_target_pairs={{0,64},{64,128},{128,192},{192,0},{1,65},{65,129},{129,193},{193,1... | collective-permute-start | bytes 1769480 | tf_op jit(solution)/shard_map/y1_589kB/ppermute | solution.py:26
  113.8 25.6 %collective-permute-start.11 = (bf16[384,768]{1,0:T(8,128)(2,1)S(1)}, bf16[384,768]{1,0:T(8,128)(2,1)S(1)}, u32[]{:S(2)}, u32[]{:S(2)}) collective-permute-start(bf16[384,768]{1,0:T(8,128)(2,1)S(1)} %get-tuple-element.29), channel_id=1, source_target_pairs={{0,192},{64,0},{128,64},{192,128},{1,193},{65,1},{129,65},{193,129... | collective-permute-start | bytes 1769480 | tf_op jit(solution)/shard_map/y3_589kB/ppermute | solution.py:26
  115.9 23.5 %collective-permute-start.9 = (bf16[384,768]{1,0:T(8,128)(2,1)S(1)}, bf16[384,768]{1,0:T(8,128)(2,1)S(1)}, u32[]{:S(2)}, u32[]{:S(2)}) collective-permute-start(bf16[384,768]{1,0:T(8,128)(2,1)S(1)} %get-tuple-element.27), channel_id=1, source_target_pairs={{0,128},{64,192},{128,0},{192,64},{1,129},{65,193},{129,1},{193,65... | collective-permute-start | bytes 1769480 | tf_op jit(solution)/shard_map/y2_589kB/ppermute | solution.py:26
  139.4 1.7 copy-start.3
  143.9 17.7 %collective-permute-start.12 = (bf16[96,1536]{1,0:T(8,128)(2,1)S(1)}, bf16[96,1536]{1,0:T(8,128)(2,1)S(1)}, u32[]{:S(2)}, u32[]{:S(2)}) collective-permute-start(bf16[96,1536]{1,0:T(8,128)(2,1)S(1)} %get-tuple-element.31), channel_id=1, source_target_pairs={{0,128},{64,192},{128,0},{192,64},{1,129},{65,193},{129,1},{193,65... | collective-permute-start | bytes 884744 | tf_op jit(solution)/shard_map/y2_294kB/ppermute | solution.py:26
  144.0 20.2 %collective-permute-start.13 = (bf16[96,1536]{1,0:T(8,128)(2,1)S(1)}, bf16[96,1536]{1,0:T(8,128)(2,1)S(1)}, u32[]{:S(2)}, u32[]{:S(2)}) collective-permute-start(bf16[96,1536]{1,0:T(8,128)(2,1)S(1)} %get-tuple-element.32), channel_id=1, source_target_pairs={{0,64},{64,128},{128,192},{192,0},{1,65},{65,129},{129,193},{193,1... | collective-permute-start | bytes 884744 | tf_op jit(solution)/shard_map/y1_294kB/ppermute | solution.py:26
  148.1 16.1 %collective-permute-start.14 = (bf16[96,1536]{1,0:T(8,128)(2,1)S(1)}, bf16[96,1536]{1,0:T(8,128)(2,1)S(1)}, u32[]{:S(2)}, u32[]{:S(2)}) collective-permute-start(bf16[96,1536]{1,0:T(8,128)(2,1)S(1)} %get-tuple-element.33), channel_id=1, source_target_pairs={{0,192},{64,0},{128,64},{192,128},{1,193},{65,1},{129,65},{193,129... | collective-permute-start | bytes 884744 | tf_op jit(solution)/shard_map/y3_294kB/ppermute | solution.py:26
  153.4 1.7 copy-start.4
  157.9 10.7 %collective-permute-start.15 = (bf16[96,1536]{1,0:T(8,128)(2,1)S(1)}, bf16[96,1536]{1,0:T(8,128)(2,1)S(1)}, u32[]{:S(2)}, u32[]{:S(2)}) collective-permute-start(bf16[96,1536]{1,0:T(8,128)(2,1)S(1)} %get-tuple-element.36), channel_id=1, source_target_pairs={{0,128},{64,192},{128,0},{192,64},{1,129},{65,193},{129,1},{193,65... | collective-permute-start | bytes 884744 | tf_op jit(solution)/shard_map/y2_294kB/ppermute | solution.py:26
  161.0 10.7 %collective-permute-start.16 = (bf16[96,1536]{1,0:T(8,128)(2,1)S(1)}, bf16[96,1536]{1,0:T(8,128)(2,1)S(1)}, u32[]{:S(2)}, u32[]{:S(2)}) collective-permute-start(bf16[96,1536]{1,0:T(8,128)(2,1)S(1)} %get-tuple-element.37), channel_id=1, source_target_pairs={{0,64},{64,128},{128,192},{192,0},{1,65},{65,129},{129,193},{193,1... | collective-permute-start | bytes 884744 | tf_op jit(solution)/shard_map/y1_294kB/ppermute | solution.py:26
  161.6 10.1 %collective-permute-start.17 = (bf16[96,1536]{1,0:T(8,128)(2,1)S(1)}, bf16[96,1536]{1,0:T(8,128)(2,1)S(1)}, u32[]{:S(2)}, u32[]{:S(2)}) collective-permute-start(bf16[96,1536]{1,0:T(8,128)(2,1)S(1)} %get-tuple-element.38), channel_id=1, source_target_pairs={{0,192},{64,0},{128,64},{192,128},{1,193},{65,1},{129,65},{193,129... | collective-permute-start | bytes 884744 | tf_op jit(solution)/shard_map/y3_294kB/ppermute | solution.py:26
  164.3 7.5 %copy-start.11 = (f32[1,96,3072]{2,1,0:T(8,128)S(1)}, f32[1,96,3072]{2,1,0:T(8,128)}, u32[]{:S(2)}) copy-start(f32[1,96,3072]{2,1,0:T(8,128)} %param.7) | copy-start | bytes 3538948
Sparse Core Ops, SparseCore 0:
  9.1 44.5 all-gather.5
  55.5 34.3 all-gather.3
  112.7 40.6 all-gather.7

commit v3 on v2

v3 whole, which is shorter than its diff:
```python
import functools

import jax
import jax.numpy as jnp
from jax import lax
from jax.experimental import pallas as pl
from jax.experimental.pallas import tpu as pltpu
from jax.sharding import Mesh
from jax.sharding import PartitionSpec as P

NY, NZ, NX, NC = 4, 8, 4, 2
BF, F32 = jnp.bfloat16, jnp.float32
SIZES = {"y": NY, "z": NZ, "x": NX, "c": NC}
ANY = pl.BlockSpec(memory_space=pl.ANY)
VMEM = pl.BlockSpec(memory_space=pltpu.VMEM)
SMEM = pl.BlockSpec(memory_space=pltpu.SMEM)


def params(mib):
    return pltpu.CompilerParams(vmem_limit_bytes=mib * 2**20)


def shift(block, axis, step):
    n = SIZES[axis]
    with jax.named_scope(f"{axis}{step}_{block.size * 2 // 1000}kB"):
        return lax.ppermute(block, axis, [(i, (i + step) % n) for i in range(n)])


def dot(a, b):
    return jnp.dot(a, b, preferred_element_type=F32)


def dot_t(a, b):
    return lax.dot_general(a, b, (((1,), (1,)), ((), ())), preferred_element_type=F32)


def cost(flops):
    return pl.CostEstimate(flops=flops, bytes_accessed=8 * 2**20, transcendentals=0)


def swap_kernel(place_ref, table_ref, held_ref, amps_ref, sent_ref, out_ref, sems):
    c = place_ref[2]
    copies = [pltpu.make_async_copy(amps_ref, out_ref, sems.at[NX])]
    copies[0].start()
    for k in range(NX):
        want = table_ref[k * NC + 1 - c]
        copies.append(pltpu.make_async_copy(held_ref.at[want >> 1], sent_ref.at[k], sems.at[k]))
        copies[-1].start()
    for copy in copies:
        copy.wait()


def mine_kernel(place_ref, table_ref, held_ref, sent_ref, mine_ref, sems):
    c = place_ref[2]
    for k in range(NX):
        want = table_ref[k * NC + c]
        here = (want & 1) == c

        @pl.when(here)
        def _():
            pltpu.make_async_copy(held_ref.at[want >> 1], mine_ref.at[k], sems.at[k]).start()

        @pl.when(jnp.logical_not(here))
        def _():
            pltpu.make_async_copy(sent_ref.at[k], mine_ref.at[k], sems.at[k]).start()

    for k in range(NX):
        pltpu.make_async_copy(sent_ref.at[k], mine_ref.at[k], sems.at[k]).wait()


def choose(kernel, results, place, table, *arrays):
    return pl.pallas_call(
        kernel,
        out_shape=[jax.ShapeDtypeStruct(a.shape, a.dtype) for a in results],
        in_specs=[SMEM, SMEM] + [ANY] * len(arrays),
        out_specs=[ANY] * len(results),
        scratch_shapes=[pltpu.SemaphoreType.DMA((NX + 1,))],
        compiler_params=params(2),
    )(place, table, *arrays)


def join_kernel(parts_ref, first_ref, chosen_ref, sems):
    copies = [pltpu.make_async_copy(parts_ref.at[k], chosen_ref.at[:, k], sems.at[k]) for k in range(NX)]
    for copy in copies:
        copy.start()
    for copy in copies:
        copy.wait()


def join(parts, first):
    nx, ny, third, aux = parts.shape
    return pl.pallas_call(
        join_kernel,
        out_shape=jax.ShapeDtypeStruct((ny, nx, third, aux), BF),
        in_specs=[ANY] * 2,
        out_specs=ANY,
        scratch_shapes=[pltpu.SemaphoreType.DMA((NX,))],
        compiler_params=params(2),
    )(parts, first)


def last_kernel(fore_ref, back_ref, late_ref, a_ref, b_ref, later_ref, sems):
    h = a_ref.shape[1]
    copies = [
        pltpu.make_async_copy(fore_ref.at[:, pl.ds(0, h)], a_ref, sems.at[0]),
        pltpu.make_async_copy(back_ref.at[:, pl.ds(h, h)], b_ref, sems.at[1]),
        pltpu.make_async_copy(late_ref, later_ref, sems.at[2]),
    ]
    for copy in copies:
        copy.start()
    for copy in copies:
        copy.wait()


def last_step(fore, back, late):
    rows, aux = fore.shape
    half = jax.ShapeDtypeStruct((rows, aux // 2), BF)
    return pl.pallas_call(
        last_kernel,
        out_shape=[half, half, jax.ShapeDtypeStruct(late.shape, BF)],
        in_specs=[ANY] * 3,
        out_specs=[ANY] * 3,
        scratch_shapes=[pltpu.SemaphoreType.DMA((3,))],
        compiler_params=params(2),
    )(fore, back, late)


def left_kernel(dist, more, place_ref, amps_ref, *refs):
    blocks, refs = refs[: len(dist)], refs[len(dist) :]
    before, (left_ref, full_ref, *last_ref, amps, sems) = (refs[:2], refs[2:]) if more else (None, refs)
    z, rows = place_ref[1], blocks[0].shape[0]

    def columns(d):
        return pl.ds(pl.multiple_of((z + NZ + d) % NZ * rows, 128), rows)

    copies = []
    for n, d in enumerate(dist):
        copies.append(pltpu.make_async_copy(blocks[n], full_ref.at[(z + NZ + d) % NZ], sems.at[n, 0]))
        copies.append(pltpu.make_async_copy(amps_ref.at[:, columns(d)], amps.at[n], sems.at[n, 1]))
    if more:
        copies.append(pltpu.make_async_copy(amps_ref.at[:, columns(NZ // 2)], last_ref[0], sems.at[len(dist), 0]))
    for copy in copies:
        copy.start()
    for n, d in enumerate(dist):
        copies[2 * n].wait()
        copies[2 * n + 1].wait()
        block = full_ref[(z + NZ + d) % NZ]
        part = dot(amps[n], block)
        if n:
            left_ref[...] += part
        elif more:
            left_ref[...] = before[0][...] + part
        else:
            left_ref[...] = block.astype(F32) + part
    if more:
        copies[-1].wait()


def add_left(place, amps, dist, blocks, before=()):
    rows, aux = blocks[0].shape
    n, more = len(dist), bool(before)
    shapes = [((rows, aux), F32), ((NZ, rows, aux), BF)] + [((rows, rows), BF)] * more
    return pl.pallas_call(
        functools.partial(left_kernel, dist, more),
        out_shape=[jax.ShapeDtypeStruct(*a) for a in shapes],
        in_specs=[SMEM, VMEM] + [ANY] * n + [VMEM] * len(before),
        out_specs=[VMEM] * len(shapes),
        scratch_shapes=[pltpu.VMEM((n, rows, rows), BF), pltpu.SemaphoreType.DMA((n + 1, 2))],
        input_output_aliases={2 + n: 0, 3 + n: 1} if more else {},
        compiler_params=params(8),
        cost_estimate=cost(2 * rows * aux * rows * n),
    )(place, amps, *blocks, *before)


def first_kernel(pairs, place_ref, amps_ref, acc_ref, full_ref, far_a_ref, far_b_ref, left, part_a_ref, part_b_ref):
    h = far_a_ref.shape[1]
    for at, far in ((0, far_a_ref), (h, far_b_ref)):
        cols = pl.ds(at, h)
        left[:, cols] = (acc_ref[:, cols] + dot(amps_ref[...], far[...])).astype(BF)
    part = columns_for(2, pairs, place_ref, left, full_ref, far_a_ref, far_b_ref).astype(BF)
    part_a_ref[...] = part[:, :h]
    part_b_ref[...] = part[:, h:]


def second_kernel(pairs, place_ref, left, full_ref, far_a_ref, far_b_ref, *refs):
    h = far_a_ref.shape[1]
    for n, d in enumerate((1, 3, 0)):
        part = columns_for(d, pairs, place_ref, left, full_ref, far_a_ref, far_b_ref)
        for ref, half in zip(refs[2 * n : 2 * n + 2], (part[:, :h], part[:, h:])):
            ref[...] = half.astype(ref.dtype)


def columns_for(d, pairs, place_ref, left, full_ref, far_a_ref, far_b_ref):
    last = (place_ref[1] + NZ // 2) % NZ
    at = pl.ds(pl.multiple_of((place_ref[0] + d) % NY * pairs, 32), pairs)
    far = jnp.concatenate([far_a_ref[at], far_b_ref[at]], axis=1)
    block = jnp.concatenate([jnp.where(last == k, far, full_ref[k, at]) for k in range(NZ)], axis=0)
    return dot_t(left[...], block)


def out_kernel(pairs, first, place_ref, total_ref, amps_ref, own_ref, *refs):
    send_refs, (total, rows, amps, sems) = refs[:-4], refs[-4:]
    y = place_ref[0]
    width = total_ref.shape[1]
    step = amps.shape[2]
    copies = [
        pltpu.make_async_copy(amps_ref.at[:, pl.ds(k * step, step)], amps.at[k], sems.at[k])
        for k in range(amps.shape[0])
    ]
    for copy in copies:
        copy.start()
    for d in range(NY):
        block = total_ref[pl.ds(pl.multiple_of((y + d) % NY * pairs, 32), pairs)]
        total[d * pairs : (d + 1) * pairs] = block
        rows[d * pairs : (d + 1) * pairs] = block.astype(BF)
    for k, copy in enumerate(copies):
        n, part = divmod(first + k * step, width)
        cols = pl.ds(k * step, step)
        copy.wait()
        prod = dot(rows[...], amps[k])
        prod += jnp.where(y == n, total[:, part : part + step], 0.0)
        own_ref[:, cols] = prod[:pairs]
        for d in range(1, NY):
            send_refs[d - 1][:, cols] = prod[d * pairs : (d + 1) * pairs].astype(send_refs[d - 1].dtype)


def out_products(place, total, amps_i, first, pairs, kept):
    rows, cols = amps_i.shape
    types = [F32 if d in (0, kept) else BF for d in range(NY)]
    step = total.shape[1] // 2
    return pl.pallas_call(
        functools.partial(out_kernel, pairs, first),
        out_shape=[jax.ShapeDtypeStruct((pairs, cols), t) for t in types],
        in_specs=[SMEM, VMEM, ANY],
        out_specs=[VMEM] * NY,
        scratch_shapes=[
            pltpu.VMEM(total.shape, F32),
            pltpu.VMEM(total.shape, BF),
            pltpu.VMEM((cols // step, rows, step), BF),
            pltpu.SemaphoreType.DMA((cols // step,)),
        ],
        compiler_params=params(10),
        cost_estimate=cost(2 * total.size * cols),
    )(place, total, amps_i)


def collect(own, two, direct, kept, step):
    relay = (kept + shift(two, "y", step).astype(F32)).astype(BF)
    return own + shift(direct, "y", -step).astype(F32) + shift(relay, "y", step).astype(F32)


def shards(pair_table, cholesky, amplitudes, denominators):
    y, z, x, c = (lax.axis_index(a) for a in ("y", "z", "x", "c"))
    place = jnp.stack([y, z, c])
    amps = amplitudes[0]
    pairs, naux = amps.shape[0], cholesky.shape[1]
    aux = -(-naux // (128 * NY)) * 128
    width = NZ * pairs
    rows = NY * pairs
    third = pairs // NX

    early = 4 * NY * width // 8
    amps_i0 = lax.all_gather(amps[:, :early], "z", axis=0, tiled=True)
    by_z = jnp.transpose(amps.reshape(pairs, NY, NZ, pairs), (0, 2, 1, 3)).reshape(pairs, NY * width)

    own = jnp.pad(jnp.transpose(cholesky[0]), ((0, 0), (0, NY * aux - naux)))
    own = jnp.transpose(own.reshape(NX, third, NY, aux), (0, 2, 1, 3)).reshape(NX * NY, third, aux)
    held = lax.all_to_all(own, ("x", "y"), split_axis=0, concat_axis=0, tiled=True).reshape(NX, NY, third, aux)
    sent, by_z = choose(swap_kernel, (held, by_z), place, pair_table, held, by_z)
    (mine,) = choose(mine_kernel, (held,), place, pair_table, held, shift(sent, "c", 1))
    amps_j = lax.all_gather(by_z, "y", axis=0, tiled=True)
    parts = lax.all_to_all(mine, "x", split_axis=0, concat_axis=0, tiled=True)
    chosen = join(parts, amps_i0).reshape(rows, aux)

    dist, blocks = [0], [chosen]
    fore = back = chosen
    for s in range(1, NZ // 2):
        fore, back = shift(fore, "z", 1), shift(back, "z", -1)
        dist += [-s, s]
        blocks += [fore, back]
    far_a, far_b, later = last_step(fore, back, amps[:, early:])
    far_a, far_b = shift(far_a, "z", 1), shift(far_b, "z", -1)
    amps_i1 = lax.all_gather(later, "z", axis=0, tiled=True)

    n = len(blocks) - 2
    acc = add_left(place, amps_j, dist[:n], blocks[:n])
    acc, full, amps_last = add_left(place, amps_j, dist[n:], blocks[n:], acc)
    part, kept = (jax.ShapeDtypeStruct((rows, width // 2), t) for t in (BF, F32))
    left, two_a, two_b = pl.pallas_call(
        functools.partial(first_kernel, pairs),
        out_shape=[jax.ShapeDtypeStruct((rows, aux), BF), part, part],
        in_specs=[SMEM] + [VMEM] * 5,
        out_specs=[VMEM] * 3,
        compiler_params=params(8),
        cost_estimate=cost(2 * rows * aux * (rows + width)),
    )(place, amps_last, acc, full, far_a, far_b)
    one_a, one_b, three_a, three_b, own_a, own_b = pl.pallas_call(
        functools.partial(second_kernel, pairs),
        out_shape=[kept, part, part, kept, kept, kept],
        in_specs=[SMEM] + [VMEM] * 4,
        out_specs=[VMEM] * 6,
        compiler_params=params(8),
        cost_estimate=cost(6 * rows * aux * width),
    )(place, left, full, far_a, far_b)
    total = [collect(own_a, two_a, three_a, one_a, 1), collect(own_b, two_b, one_b, three_b, -1)]
    total = jnp.concatenate(total, axis=1)

    own, one, two, three = out_products(place, total, amps_i0, 0, pairs, 1)
    outs = [collect(own, two, three, one, 1)]
    own, one, two, three = out_products(place, total, amps_i1, early, pairs, 3)
    outs.append(collect(own, two, one, three, -1))
    return (-jnp.concatenate(outs, axis=1) / denominators[0]).astype(BF)[None]


def solution(mesh):
    grid = Mesh(mesh.devices.reshape(NY, NZ, NX, NC), ("y", "z", "x", "c"))
    ka, row = ("x", "c"), ("y", "z")
    in_specs = (P(), P(ka, None, row), P(ka, row, None), P(ka, row, None))
    return jax.shard_map(shards, mesh=grid, in_specs=in_specs, out_specs=P(ka, row, None), check_vma=False)
```

time: 180 us -> 170 us (0.944)
  waiting for transfers between devices: 79.1 us -> 72.1 us
  local copies, waits for them, and re-layouts: 18.3 us -> 14.8 us
  Pallas kernels: 16.9 us -> 19.2 us
    all_gather x1, waiting for transfers between devices: 5.3 us -> 0.01 us  [shards(): amps_i1 = lax.all_gather(later, 'z', axis=0, tiled=True)]
    all_gather x1, waiting for transfers between devices: 5.05 us -> 7.86 us  [shards(): amps_i0 = lax.all_gather(amps[:, :early], 'z', axis=0, tiled=True)]
    ppermute x18 -> x21, waiting for transfers between devices: 58.8 us -> 56.5 us  [shift(): return lax.ppermute(block, axis, [(i, (i + step) % n) for i in range(n)])]
    pallas_call x2 -> x5, Pallas kernels: 8.34 us -> 10.5 us  [the longest x2 5.81 us: add_left(): pl.pallas_call(functools.partial(left_kernel, dist, more), out_shape=[jax...]
    all_to_all x1, waiting for transfers between devices: 9.9 us -> 7.71 us  [shards(): lax.all_to_all(own, ('x', 'y'), split_axis=0, concat_axis=0, tiled=True)]
    another operation x2, local copies, waits for them, and re-layouts: 3.1 us -> 1.07 us  [shards(): amps.reshape(pairs, NY, NZ, pairs)]
    ppermute x18 -> x21, starting transfers between devices: 28.4 us -> 26.8 us  [shift(): return lax.ppermute(block, axis, [(i, (i + step) % n) for i in range(n)])]
    unnamed x26 -> x28, local copies, waits for them, and re-layouts: 9.44 us -> 9.44 us
  transfers between devices with their start and end apart: 22 -> 25, of which waited for: 9 -> 14; matrix products, arithmetic and copies ran while one was open for 4% -> 2% of each run, Pallas kernels for 8% -> 11%
where the time goes in v3:
time: 170 us; the launch traced here: 169 us
  waiting for transfers between devices  72.1 us (42%)
  starting transfers between devices  34.4 us (20%)
  Pallas kernels  19.2 us (11%)
  local copies, waits for them, and re-layouts  14.8 us (9%)
  blocking collectives  13.7 us (8%)
  between operations  13.4 us (8%)
    ppermute x21, waiting for transfers between devices, shift(): return lax.ppermute(block, axis, [(i, (i + step) % n) for i in range(n)])  56.5 us
    ppermute x21, starting transfers between devices, shift(): return lax.ppermute(block, axis, [(i, (i + step) % n) for i in range(n)])  26.8 us
    all_to_all x1, blocking collectives, shards(): parts = lax.all_to_all(mine, 'x', split_axis=0, concat_axis=0, tiled=True)  13.7 us
    unnamed x28, local copies, waits for them, and re-layouts  9.44 us
    all_gather x1, waiting for transfers between devices, shards(): amps_i0 = lax.all_gather(amps[:, :early], 'z', axis=0, tiled=True)  7.86 us
    all_to_all x1, waiting for transfers between devices, shards(): lax.all_to_all(own, ('x', 'y'), split_axis=0, concat_axis=0, tiled=True)  7.71 us
    all_to_all x1, starting transfers between devices, shards(): lax.all_to_all(own, ('x', 'y'), split_axis=0, concat_axis=0, tiled=True)  7.48 us
    pallas_call x2, Pallas kernels, add_left(): pl.pallas_call(functools.partial(left_kernel, dist, more), out_shape=[jax...  5.81 us
  transfers between devices with their start and end apart: 25, of which 14 were waited for; matrix products, arithmetic and copies ran while one was open for 2% of the time, Pallas kernels for 11%

profile of v3, /device:TPU:2, one launch (start us, length us, event | category | flops | bytes accessed | tf_op | source)
XLA Modules:
  0.0 169.2 jit_solution(13106931824712399975)
XLA Ops:
  6.5 1.9 %fusion.2 = (bf16[96,1536]{1,0:T(8,128)(2,1)S(1)}, bf16[96,1536]{1,0:T(8,128)(2,1)}) fusion(bf16[96,3072]{1,0:T(8,128)(2,1)} %bitcast.25), kind=kLoop, calls=%fused_computation.14 | loop fusion | bytes 1179648 | tf_op jit(solution)/shard_map/slice | solution.py:281
  8.9 0.9 copy.7
  9.8 7.5 %all-to-all-start = ((bf16[16,24,768]{2,1,0:T(8,128)(2,1)}), bf16[16,24,768]{2,1,0:T(8,128)(2,1)S(1)}, u32[]{:S(2)}, u32[]{:S(2)}) async-start(bf16[16,24,768]{2,1,0:T(8,128)(2,1)} %bitcast.6), calls=%async_computation | async-start | bytes 1179648 | tf_op jit(solution)/shard_map/all_to_all | solution.py:268
  17.3 0.8 reshape_squeeze.3
  18.5 1.1 reshape.47.amps_ref
  19.6 7.7 %all-to-all-done = bf16[16,24,768]{2,1,0:T(8,128)(2,1)S(1)} async-done(((bf16[16,24,768]{2,1,0:T(8,128)(2,1)}), bf16[16,24,768]{2,1,0:T(8,128)(2,1)S(1)}, u32[]{:S(2)}, u32[]{:S(2)}) %all-to-all-start) | async-done | bytes 589856 | tf_op jit(solution)/shard_map/all_to_all | solution.py:268
  27.3 1.4 shard_map.46
  28.9 2.0 %collective-permute-done.sent_ref = bf16[4,4,24,768]{3,2,1,0:T(8,128)(2,1)S(1)} collective-permute-done((bf16[4,4,24,768]{3,2,1,0:T(8,128)(2,1)S(1)}, bf16[4,4,24,768]{3,2,1,0:T(8,128)(2,1)S(1)}, u32[]{:S(2)}, u32[]{:S(2)}) %collective-permute-start) | collective-permute-done | bytes 589856 | tf_op jit(solution)/shard_map/c1_589kB/ppermute | solution.py:26
  30.9 1.4 shard_map.47
  32.3 13.7 %all_to_all.10.parts_ref = bf16[4,4,24,768]{3,2,1,0:T(8,128)(2,1)S(1)} all-to-all(bf16[4,4,24,768]{3,2,1,0:T(8,128)(2,1)S(1)} %shard_map.47), channel_id=1, replica_groups=mesh['y'=4,'z'=8,'x'=4,'c'=2] {'x'}, dimensions={0} | all-to-all | bytes 1179648 | tf_op jit(solution)/shard_map/all_to_all | solution.py:272
  46.0 7.9 %all-gather.6.cloned.1.call-done.first_ref.amps_ref = bf16[768,1536]{1,0:T(8,128)(2,1)} async-done(((bf16[96,1536]{1,0:T(8,128)(2,1)}), bf16[768,1536]{1,0:T(8,128)(2,1)}) %all-gather.6.cloned.1.call-update) | async-done | bytes 2359312 | tf_op jit(solution)/shard_map/all_gather | solution.py:263
  53.8 1.7 copy-done
  55.7 1.1 collective-permute-start.1
  56.8 2.2 %collective-permute-start.4 = (bf16[384,768]{1,0:T(8,128)(2,1)S(1)}, bf16[384,768]{1,0:T(8,128)(2,1)S(1)}, u32[]{:S(2)}, u32[]{:S(2)}) collective-permute-start(bf16[384,768]{1,0:T(8,128)(2,1)S(1)} %bitcast.21), channel_id=1, source_target_pairs={{0,56},{8,0},{16,8},{24,16},{32,24},{40,32},{48,40},{56,48},{1,57}... | collective-permute-start | bytes 1769480 | tf_op jit(solution)/shard_map/z-1_589kB/ppermute | solution.py:26
  59.0 10.3 %collective-permute-done.1.refs_1_ = bf16[384,768]{1,0:T(8,128)(2,1)S(1)} collective-permute-done((bf16[384,768]{1,0:T(8,128)(2,1)S(1)}, bf16[384,768]{1,0:T(8,128)(2,1)S(1)}, u32[]{:S(2)}, u32[]{:S(2)}) %collective-permute-start.1) | collective-permute-done | bytes 589856 | tf_op jit(solution)/shard_map/z1_589kB/ppermute | solution.py:26
  69.4 3.1 %collective-permute-start.5 = (bf16[384,768]{1,0:T(8,128)(2,1)S(1)}, bf16[384,768]{1,0:T(8,128)(2,1)S(1)}, u32[]{:S(2)}, u32[]{:S(2)}) collective-permute-start(bf16[384,768]{1,0:T(8,128)(2,1)S(1)} %collective-permute-done.4.refs_2_), channel_id=1, source_target_pairs={{0,56},{8,0},{16,8},{24,16},{32,24},{40,32},{48,40},{56,48},{1,57}... | collective-permute-start | bytes 1769480 | tf_op jit(solution)/shard_map/z-1_589kB/ppermute | solution.py:26
  72.5 10.1 %collective-permute-done.2.refs_3_ = bf16[384,768]{1,0:T(8,128)(2,1)S(1)} collective-permute-done((bf16[384,768]{1,0:T(8,128)(2,1)S(1)}, bf16[384,768]{1,0:T(8,128)(2,1)S(1)}, u32[]{:S(2)}, u32[]{:S(2)}) %collective-permute-start.2) | collective-permute-done | bytes 589856 | tf_op jit(solution)/shard_map/z1_589kB/ppermute | solution.py:26
  82.8 3.1 %collective-permute-start.6 = (bf16[384,768]{1,0:T(8,128)(2,1)S(1)}, bf16[384,768]{1,0:T(8,128)(2,1)S(1)}, u32[]{:S(2)}, u32[]{:S(2)}) collective-permute-start(bf16[384,768]{1,0:T(8,128)(2,1)S(1)} %collective-permute-done.5.refs_4_), channel_id=1, source_target_pairs={{0,56},{8,0},{16,8},{24,16},{32,24},{40,32},{48,40},{56,48},{1,57}... | collective-permute-start | bytes 1769480 | tf_op jit(solution)/shard_map/z-1_589kB/ppermute | solution.py:26
  85.9 8.4 %collective-permute-done.3.refs_0_.fore_ref = bf16[384,768]{1,0:T(8,128)(2,1)S(1)} collective-permute-done((bf16[384,768]{1,0:T(8,128)(2,1)S(1)}, bf16[384,768]{1,0:T(8,128)(2,1)S(1)}, u32[]{:S(2)}, u32[]{:S(2)}) %collective-permute-start.3) | collective-permute-done | bytes 589856 | tf_op jit(solution)/shard_map/z1_589kB/ppermute | solution.py:26
  94.3 0.9 shard_map.51
  95.2 0.7 copy-done.10
  96.5 2.8 %collective-permute-start.8 = (bf16[384,384]{1,0:T(8,128)(2,1)}, bf16[384,384]{1,0:T(8,128)(2,1)S(1)}, u32[]{:S(2)}, u32[]{:S(2)}) collective-permute-start(bf16[384,384]{1,0:T(8,128)(2,1)} %copy-done.10), channel_id=1, source_target_pairs={{0,56},{8,0},{16,8},{24,16},{32,24},{40,32},{48,40},{56,48},{1,57}... | collective-permute-start | bytes 884744 | tf_op jit(solution)/shard_map/z-1_294kB/ppermute | solution.py:26
  99.2 1.7 copy-done.2
  100.9 1.1 copy-done.6
  102.0 1.1 copy-done.8
  103.0 3.9 %shard_map.49 = (f32[384,768]{1,0:T(8,128)S(1)}, bf16[8,384,768]{2,1,0:T(8,128)(2,1)S(1)}) custom-call(s32[3]{0:T(128)S(1)} %pad_add_fusion.place_ref, bf16[384,3072]{1,0:T(8,128)(2,1)S(1)} %copy-done.2, bf16[384,768]{1,0:T(8,128)(2,1)S(1)} %bitcast.22, bf16[384,768]{1,0:T(8,128)(2,1)S(1)} %collective-permute-done.1.refs_1_, ...), custom_call_target="tpu_custom_call" | custom-call | flops 1132462080 | bytes 8388608 | tf_op jit(solution)/shard_map/pallas_call | solution.py:163
  106.9 1.9 %shard_map.50 = (f32[384,768]{1,0:T(8,128)S(1)}, bf16[8,384,768]{2,1,0:T(8,128)(2,1)S(1)}, bf16[384,384]{1,0:T(8,128)(2,1)S(1)}) custom-call(s32[3]{0:T(128)S(1)} %pad_add_fusion.place_ref, bf16[384,3072]{1,0:T(8,128)(2,1)S(1)} %copy-done.3, ...), custom_call_target="tpu_custom_call", output_to_operand_aliasing={{0}: (4, {}), {1}: (5, {})} | custom-call | flops 452984832 | bytes 8388608 | tf_op jit(solution)/shard_map/pallas_call | solution.py:163
  108.9 1.7 %shard_map.52 = (bf16[384,768]{1,0:T(8,128)(2,1)S(1)}, bf16[384,384]{1,0:T(8,128)(2,1)S(1)}, bf16[384,384]{1,0:T(8,128)(2,1)S(1)}) custom-call(s32[3]{0:T(128)S(1)} %pad_add_fusion.place_ref, bf16[384,384]{1,0:T(8,128)(2,1)S(1)} %get-tuple-element.36.amps_ref, f32[384,768]{1,0:T(8,128)S(1)} %get-tuple-element.37.acc_ref, ...), custom_call_target="tpu_custom_call" | custom-call | flops 679477248 | bytes 8388608 | tf_op jit(solution)/shard_map/pallas_call | solution.py:289
  110.6 1.6 collective-permute-start.10
  112.2 1.7 %collective-permute-start.13 = (bf16[384,384]{1,0:T(8,128)(2,1)S(1)}, bf16[384,384]{1,0:T(8,128)(2,1)S(1)}, u32[]{:S(2)}, u32[]{:S(2)}) collective-permute-start(bf16[384,384]{1,0:T(8,128)(2,1)S(1)} %get-tuple-element.49), channel_id=1, source_target_pairs={{0,192},{64,0},{128,64},{192,128},{1,193},{65,1},{129,65},{193,129... | collective-permute-start | bytes 884744 | tf_op jit(solution)/shard_map/y-1_294kB/ppermute | solution.py:26
  113.9 2.2 %shard_map.53 = (f32[384,384]{1,0:T(8,128)S(1)}, bf16[384,384]{1,0:T(8,128)(2,1)S(1)}, bf16[384,384]{1,0:T(8,128)(2,1)S(1)}, f32[384,384]{1,0:T(8,128)S(1)}, f32...) custom-call(s32[3]{0:T(128)S(1)} %pad_add_fusion.place_ref, bf16[384,768]{1,0:T(8,128)(2,1)S(1)} %get-tuple-element.41.left, ...), custom_call_target="tpu_custom_call" | custom-call | flops 1358954496 | bytes 8388608 | tf_op jit(solution)/shard_map/pallas_call | solution.py:297
  116.1 1.6 collective-permute-start.9
  117.7 3.9 %collective-permute-done.10 = bf16[384,384]{1,0:T(8,128)(2,1)S(1)} collective-permute-done((bf16[384,384]{1,0:T(8,128)(2,1)S(1)}, bf16[384,384]{1,0:T(8,128)(2,1)S(1)}, u32[]{:S(2)}, u32[]{:S(2)}) %collective-permute-start.10) | collective-permute-done | bytes 294944 | tf_op jit(solution)/shard_map/y1_294kB/ppermute | solution.py:26
  122.2 1.5 collective-permute-start.12
  123.8 1.9 %collective-permute-start.14 = (bf16[384,384]{1,0:T(8,128)(2,1)S(1)}, bf16[384,384]{1,0:T(8,128)(2,1)S(1)}, u32[]{:S(2)}, u32[]{:S(2)}) collective-permute-start(bf16[384,384]{1,0:T(8,128)(2,1)S(1)} %add_convert_fusion.2), channel_id=1, source_target_pairs={{0,192},{64,0},{128,64},{192,128},{1,193},{65,1},{129,65},{193,129... | collective-permute-start | bytes 884744 | tf_op jit(solution)/shard_map/y-1_294kB/ppermute | solution.py:26
  125.6 4.1 %collective-permute-done.11 = bf16[384,384]{1,0:T(8,128)(2,1)S(1)} collective-permute-done((bf16[384,384]{1,0:T(8,128)(2,1)S(1)}, bf16[384,384]{1,0:T(8,128)(2,1)S(1)}, u32[]{:S(2)}, u32[]{:S(2)}) %collective-permute-start.11) | collective-permute-done | bytes 294944 | tf_op jit(solution)/shard_map/y1_294kB/ppermute | solution.py:26
  129.8 3.1 %collective-permute-done.12 = bf16[384,384]{1,0:T(8,128)(2,1)S(1)} collective-permute-done((bf16[384,384]{1,0:T(8,128)(2,1)S(1)}, bf16[384,384]{1,0:T(8,128)(2,1)S(1)}, u32[]{:S(2)}, u32[]{:S(2)}) %collective-permute-start.12) | collective-permute-done | bytes 294944 | tf_op jit(solution)/shard_map/y1_294kB/ppermute | solution.py:26
  133.0 1.6 copy-done.1
  134.6 2.8 %shard_map.54 = (f32[96,1536]{1,0:T(8,128)S(1)}, f32[96,1536]{1,0:T(8,128)S(1)}, bf16[96,1536]{1,0:T(8,128)(2,1)S(1)}, bf16[96,1536]{1,0:T(8,128)(2,1)S(1)}) custom-call(s32[3]{0:T(128)S(1)} %pad_add_fusion.place_ref, f32[384,768]{1,0:T(8,128)S(1)} %pad_maximum_fusion.total_ref, bf16[768,1536]{1,0:T(8,128)(2,1)S(1)} %copy-done.1), custom_call_target="tpu_custom_call" | custom-call | flops 905969664 | bytes 8388608 | tf_op jit(solution)/shard_map/pallas_call | solution.py:231
  137.7 3.2 %collective-permute-start.15 = (bf16[96,1536]{1,0:T(8,128)(2,1)S(1)}, bf16[96,1536]{1,0:T(8,128)(2,1)S(1)}, u32[]{:S(2)}, u32[]{:S(2)}) collective-permute-start(bf16[96,1536]{1,0:T(8,128)(2,1)S(1)} %get-tuple-element.51), channel_id=1, source_target_pairs={{0,192},{64,0},{128,64},{192,128},{1,193},{65,1},{129,65},{193,129... | collective-permute-start | bytes 884744 | tf_op jit(solution)/shard_map/y-1_294kB/ppermute | solution.py:26
  141.0 1.7 copy-done.4
  142.6 2.8 %shard_map.55 = (f32[96,1536]{1,0:T(8,128)S(1)}, bf16[96,1536]{1,0:T(8,128)(2,1)S(1)}, bf16[96,1536]{1,0:T(8,128)(2,1)S(1)}, f32[96,1536]{1,0:T(8,128)S(1)}) custom-call(s32[3]{0:T(128)S(1)} %pad_add_fusion.place_ref, f32[384,768]{1,0:T(8,128)S(1)} %pad_maximum_fusion.total_ref, bf16[768,1536]{1,0:T(8,128)(2,1)S(1)} %copy-done.4), custom_call_target="tpu_custom_call" | custom-call | flops 905969664 | bytes 8388608 | tf_op jit(solution)/shard_map/pallas_call | solution.py:231
  145.5 1.1 collective-permute-done.16
  146.6 1.0 collective-permute-start.17
  147.8 7.0 %collective-permute-done.19 = bf16[96,1536]{1,0:T(8,128)(2,1)S(1)} collective-permute-done((bf16[96,1536]{1,0:T(8,128)(2,1)S(1)}, bf16[96,1536]{1,0:T(8,128)(2,1)S(1)}, u32[]{:S(2)}, u32[]{:S(2)}) %collective-permute-start.19) | collective-permute-done | bytes 294944 | tf_op jit(solution)/shard_map/y-1_294kB/ppermute | solution.py:26
  155.2 3.1 %collective-permute-done.18 = bf16[96,1536]{1,0:T(8,128)(2,1)S(1)} collective-permute-done((bf16[96,1536]{1,0:T(8,128)(2,1)S(1)}, bf16[96,1536]{1,0:T(8,128)(2,1)S(1)}, u32[]{:S(2)}, u32[]{:S(2)}) %collective-permute-start.18) | collective-permute-done | bytes 294944 | tf_op jit(solution)/shard_map/y1_294kB/ppermute | solution.py:26
  158.3 3.3 %collective-permute-done.20 = bf16[96,1536]{1,0:T(8,128)(2,1)S(1)} collective-permute-done((bf16[96,1536]{1,0:T(8,128)(2,1)S(1)}, bf16[96,1536]{1,0:T(8,128)(2,1)S(1)}, u32[]{:S(2)}, u32[]{:S(2)}) %collective-permute-start.20) | collective-permute-done | bytes 294944 | tf_op jit(solution)/shard_map/y-1_294kB/ppermute | solution.py:26
  161.7 1.0 fusion.1
  (62 shorter events, 4.1 us)
Async XLA Ops:
  6.5 1.9 %copy-start.13 = (bf16[1,3000,96]{1,2,0:T(8,128)(2,1)S(1)}, bf16[1,3000,96]{1,2,0:T(8,128)(2,1)}, u32[]{:S(2)}) copy-start(bf16[1,3000,96]{1,2,0:T(8,128)(2,1)} %param.5) | copy-start | bytes 1728004
  6.5 47.3 %all-gather.6.cloned.1.call-start = ((), (), s32[]{:S(2)}) async-start(), calls=%async_computation.3 | async-start | bytes 2654208 | tf_op jit(solution)/shard_map/all_gather | solution.py:263
  8.9 8.4 %copy-start.11 = (bf16[1,96,3072]{2,1,0:T(8,128)(2,1)S(1)}, bf16[1,96,3072]{2,1,0:T(8,128)(2,1)}, u32[]{:S(2)}) copy-start(bf16[1,96,3072]{2,1,0:T(8,128)(2,1)} %param.6) | copy-start | bytes 1769476
  9.8 17.5 %all-to-all-start = ((bf16[16,24,768]{2,1,0:T(8,128)(2,1)}), bf16[16,24,768]{2,1,0:T(8,128)(2,1)S(1)}, u32[]{:S(2)}, u32[]{:S(2)}) async-start(bf16[16,24,768]{2,1,0:T(8,128)(2,1)} %bitcast.6), calls=%async_computation | async-start | bytes 1179648 | tf_op jit(solution)/shard_map/all_to_all | solution.py:268
  17.3 81.9 %all-gather.4.cloned.1.call-start = ((), (), s32[]{:S(2)}) async-start(), calls=%async_computation.2 | async-start | bytes 2949120 | tf_op jit(solution)/shard_map/all_gather | solution.py:271
  18.1 9.2 %copy-start.9 = (s32[8]{0:T(128)S(1)}, s32[8]{0:T(128)}, u32[]{:S(2)}) copy-start(s32[8]{0:T(128)} %table_ref.3) | copy-start | bytes 100
  28.8 112.2 %all-gather.8.cloned.1.call-start = ((), (), s32[]{:S(2)}) async-start(), calls=%async_computation.4 | async-start | bytes 2654208 | tf_op jit(solution)/shard_map/all_gather | solution.py:283
  28.8 2.1 %collective-permute-start = (bf16[4,4,24,768]{3,2,1,0:T(8,128)(2,1)S(1)}, bf16[4,4,24,768]{3,2,1,0:T(8,128)(2,1)S(1)}, u32[]{:S(2)}, u32[]{:S(2)}) collective-permute-start(bf16[4,4,24,768]{3,2,1,0:T(8,128)(2,1)S(1)} %get-tuple-element.33), channel_id=1, source_target_pairs={{0,1},{1,0},{2,3},{3,2},{4,5},{5,4},{6,7},{7,6},{8,9},{9,8},{10,11... | collective-permute-start | bytes 1769480 | tf_op jit(solution)/shard_map/c1_589kB/ppermute | solution.py:26
  53.8 1.7 copy-start
  55.7 13.6 %collective-permute-start.1 = (bf16[384,768]{1,0:T(8,128)(2,1)S(1)}, bf16[384,768]{1,0:T(8,128)(2,1)S(1)}, u32[]{:S(2)}, u32[]{:S(2)}) collective-permute-start(bf16[384,768]{1,0:T(8,128)(2,1)S(1)} %bitcast.20), channel_id=1, source_target_pairs={{0,8},{8,16},{16,24},{24,32},{32,40},{40,48},{48,56},{56,0},{1,9},... | collective-permute-start | bytes 1769480 | tf_op jit(solution)/shard_map/z1_589kB/ppermute | solution.py:26
  56.8 12.6 %collective-permute-start.4 = (bf16[384,768]{1,0:T(8,128)(2,1)S(1)}, bf16[384,768]{1,0:T(8,128)(2,1)S(1)}, u32[]{:S(2)}, u32[]{:S(2)}) collective-permute-start(bf16[384,768]{1,0:T(8,128)(2,1)S(1)} %bitcast.21), channel_id=1, source_target_pairs={{0,56},{8,0},{16,8},{24,16},{32,24},{40,32},{48,40},{56,48},{1,57}... | collective-permute-start | bytes 1769480 | tf_op jit(solution)/shard_map/z-1_589kB/ppermute | solution.py:26
  69.3 13.4 %collective-permute-start.2 = (bf16[384,768]{1,0:T(8,128)(2,1)S(1)}, bf16[384,768]{1,0:T(8,128)(2,1)S(1)}, u32[]{:S(2)}, u32[]{:S(2)}) collective-permute-start(bf16[384,768]{1,0:T(8,128)(2,1)S(1)} %collective-permute-done.1.refs_1_), channel_id=1, source_target_pairs={{0,8},{8,16},{16,24},{24,32},{32,40},{40,48},{48,56},{56,0},{1,9},... | collective-permute-start | bytes 1769480 | tf_op jit(solution)/shard_map/z1_589kB/ppermute | solution.py:26
  69.4 13.4 %collective-permute-start.5 = (bf16[384,768]{1,0:T(8,128)(2,1)S(1)}, bf16[384,768]{1,0:T(8,128)(2,1)S(1)}, u32[]{:S(2)}, u32[]{:S(2)}) collective-permute-start(bf16[384,768]{1,0:T(8,128)(2,1)S(1)} %collective-permute-done.4.refs_2_), channel_id=1, source_target_pairs={{0,56},{8,0},{16,8},{24,16},{32,24},{40,32},{48,40},{56,48},{1,57}... | collective-permute-start | bytes 1769480 | tf_op jit(solution)/shard_map/z-1_589kB/ppermute | solution.py:26
  82.7 12.5 %copy-start.5 = (bf16[384,768]{1,0:T(8,128)(2,1)}, bf16[384,768]{1,0:T(8,128)(2,1)S(1)}, u32[]{:S(2)}) copy-start(bf16[384,768]{1,0:T(8,128)(2,1)S(1)} %collective-permute-done.2.refs_3_) | copy-start | bytes 1769476
  82.7 11.6 %collective-permute-start.3 = (bf16[384,768]{1,0:T(8,128)(2,1)S(1)}, bf16[384,768]{1,0:T(8,128)(2,1)S(1)}, u32[]{:S(2)}, u32[]{:S(2)}) collective-permute-start(bf16[384,768]{1,0:T(8,128)(2,1)S(1)} %collective-permute-done.2.refs_3_), channel_id=1, source_target_pairs={{0,8},{8,16},{16,24},{24,32},{32,40},{40,48},{48,56},{56,0},{1,9},... | collective-permute-start | bytes 1769480 | tf_op jit(solution)/shard_map/z1_589kB/ppermute | solution.py:26
  82.8 12.4 %copy-start.7 = (bf16[384,768]{1,0:T(8,128)(2,1)}, bf16[384,768]{1,0:T(8,128)(2,1)S(1)}, u32[]{:S(2)}) copy-start(bf16[384,768]{1,0:T(8,128)(2,1)S(1)} %collective-permute-done.5.refs_4_) | copy-start | bytes 1769476
  82.8 11.5 %collective-permute-start.6 = (bf16[384,768]{1,0:T(8,128)(2,1)S(1)}, bf16[384,768]{1,0:T(8,128)(2,1)S(1)}, u32[]{:S(2)}, u32[]{:S(2)}) collective-permute-start(bf16[384,768]{1,0:T(8,128)(2,1)S(1)} %collective-permute-done.5.refs_4_), channel_id=1, source_target_pairs={{0,56},{8,0},{16,8},{24,16},{32,24},{40,32},{48,40},{56,48},{1,57}... | collective-permute-start | bytes 1769480 | tf_op jit(solution)/shard_map/z-1_589kB/ppermute | solution.py:26
  95.2 0.7 copy-start.10
  95.9 12.9 %collective-permute-start.7 = (bf16[384,384]{1,0:T(8,128)(2,1)}, bf16[384,384]{1,0:T(8,128)(2,1)S(1)}, u32[]{:S(2)}, u32[]{:S(2)}) collective-permute-start(bf16[384,384]{1,0:T(8,128)(2,1)} %get-tuple-element.39), channel_id=1, source_target_pairs={{0,8},{8,16},{16,24},{24,32},{32,40},{40,48},{48,56},{56,0},{1,9},... | collective-permute-start | bytes 884744 | tf_op jit(solution)/shard_map/z1_294kB/ppermute | solution.py:26
  96.5 12.4 %collective-permute-start.8 = (bf16[384,384]{1,0:T(8,128)(2,1)}, bf16[384,384]{1,0:T(8,128)(2,1)S(1)}, u32[]{:S(2)}, u32[]{:S(2)}) collective-permute-start(bf16[384,384]{1,0:T(8,128)(2,1)} %copy-done.10), channel_id=1, source_target_pairs={{0,56},{8,0},{16,8},{24,16},{32,24},{40,32},{48,40},{56,48},{1,57}... | collective-permute-start | bytes 884744 | tf_op jit(solution)/shard_map/z-1_294kB/ppermute | solution.py:26
  99.2 1.7 copy-start.2
  100.9 1.1 copy-start.6
  102.0 1.1 copy-start.8
  103.0 3.9 %copy-start.3 = (bf16[384,3072]{1,0:T(8,128)(2,1)S(1)}, bf16[384,3072]{1,0:T(8,128)(2,1)}, u32[]{:S(2)}) copy-start(bf16[384,3072]{1,0:T(8,128)(2,1)} %all-gather.4.cloned.1.call-done.amps_ref) | copy-start | bytes 7077892
  110.6 11.0 %collective-permute-start.10 = (bf16[384,384]{1,0:T(8,128)(2,1)S(1)}, bf16[384,384]{1,0:T(8,128)(2,1)S(1)}, u32[]{:S(2)}, u32[]{:S(2)}) collective-permute-start(bf16[384,384]{1,0:T(8,128)(2,1)S(1)} %get-tuple-element.45), channel_id=1, source_target_pairs={{0,64},{64,128},{128,192},{192,0},{1,65},{65,129},{129,193},{193,1... | collective-permute-start | bytes 884744 | tf_op jit(solution)/shard_map/y1_294kB/ppermute | solution.py:26
  112.2 11.5 %collective-permute-start.13 = (bf16[384,384]{1,0:T(8,128)(2,1)S(1)}, bf16[384,384]{1,0:T(8,128)(2,1)S(1)}, u32[]{:S(2)}, u32[]{:S(2)}) collective-permute-start(bf16[384,384]{1,0:T(8,128)(2,1)S(1)} %get-tuple-element.49), channel_id=1, source_target_pairs={{0,192},{64,0},{128,64},{192,128},{1,193},{65,1},{129,65},{193,129... | collective-permute-start | bytes 884744 | tf_op jit(solution)/shard_map/y-1_294kB/ppermute | solution.py:26
  116.1 9.5 %collective-permute-start.9 = (bf16[384,384]{1,0:T(8,128)(2,1)S(1)}, bf16[384,384]{1,0:T(8,128)(2,1)S(1)}, u32[]{:S(2)}, u32[]{:S(2)}) collective-permute-start(bf16[384,384]{1,0:T(8,128)(2,1)S(1)} %get-tuple-element.43), channel_id=1, source_target_pairs={{0,192},{64,0},{128,64},{192,128},{1,193},{65,1},{129,65},{193,129... | collective-permute-start | bytes 884744 | tf_op jit(solution)/shard_map/y-1_294kB/ppermute | solution.py:26
  121.7 8.0 %collective-permute-start.11 = (bf16[384,384]{1,0:T(8,128)(2,1)S(1)}, bf16[384,384]{1,0:T(8,128)(2,1)S(1)}, u32[]{:S(2)}, u32[]{:S(2)}) collective-permute-start(bf16[384,384]{1,0:T(8,128)(2,1)S(1)} %add_convert_fusion.3), channel_id=1, source_target_pairs={{0,64},{64,128},{128,192},{192,0},{1,65},{65,129},{129,193},{193,1... | collective-permute-start | bytes 884744 | tf_op jit(solution)/shard_map/y1_294kB/ppermute | solution.py:26
  122.2 10.6 %collective-permute-start.12 = (bf16[384,384]{1,0:T(8,128)(2,1)S(1)}, bf16[384,384]{1,0:T(8,128)(2,1)S(1)}, u32[]{:S(2)}, u32[]{:S(2)}) collective-permute-start(bf16[384,384]{1,0:T(8,128)(2,1)S(1)} %get-tuple-element.47), channel_id=1, source_target_pairs={{0,64},{64,128},{128,192},{192,0},{1,65},{65,129},{129,193},{193,1... | collective-permute-start | bytes 884744 | tf_op jit(solution)/shard_map/y1_294kB/ppermute | solution.py:26
  123.8 9.1 %collective-permute-start.14 = (bf16[384,384]{1,0:T(8,128)(2,1)S(1)}, bf16[384,384]{1,0:T(8,128)(2,1)S(1)}, u32[]{:S(2)}, u32[]{:S(2)}) collective-permute-start(bf16[384,384]{1,0:T(8,128)(2,1)S(1)} %add_convert_fusion.2), channel_id=1, source_target_pairs={{0,192},{64,0},{128,64},{192,128},{1,193},{65,1},{129,65},{193,129... | collective-permute-start | bytes 884744 | tf_op jit(solution)/shard_map/y-1_294kB/ppermute | solution.py:26
  132.9 1.7 copy-start.1
  137.4 9.1 %collective-permute-start.16 = (bf16[96,1536]{1,0:T(8,128)(2,1)S(1)}, bf16[96,1536]{1,0:T(8,128)(2,1)S(1)}, u32[]{:S(2)}, u32[]{:S(2)}) collective-permute-start(bf16[96,1536]{1,0:T(8,128)(2,1)S(1)} %get-tuple-element.53), channel_id=1, source_target_pairs={{0,64},{64,128},{128,192},{192,0},{1,65},{65,129},{129,193},{193,1... | collective-permute-start | bytes 884744 | tf_op jit(solution)/shard_map/y1_294kB/ppermute | solution.py:26
  137.7 17.1 %collective-permute-start.15 = (bf16[96,1536]{1,0:T(8,128)(2,1)S(1)}, bf16[96,1536]{1,0:T(8,128)(2,1)S(1)}, u32[]{:S(2)}, u32[]{:S(2)}) collective-permute-start(bf16[96,1536]{1,0:T(8,128)(2,1)S(1)} %get-tuple-element.51), channel_id=1, source_target_pairs={{0,192},{64,0},{128,64},{192,128},{1,193},{65,1},{129,65},{193,129... | collective-permute-start | bytes 884744 | tf_op jit(solution)/shard_map/y-1_294kB/ppermute | solution.py:26
  141.0 1.7 copy-start.4
  145.4 9.3 %collective-permute-start.19 = (bf16[96,1536]{1,0:T(8,128)(2,1)S(1)}, bf16[96,1536]{1,0:T(8,128)(2,1)S(1)}, u32[]{:S(2)}, u32[]{:S(2)}) collective-permute-start(bf16[96,1536]{1,0:T(8,128)(2,1)S(1)} %get-tuple-element.58), channel_id=1, source_target_pairs={{0,192},{64,0},{128,64},{192,128},{1,193},{65,1},{129,65},{193,129... | collective-permute-start | bytes 884744 | tf_op jit(solution)/shard_map/y-1_294kB/ppermute | solution.py:26
  146.6 8.5 %collective-permute-start.17 = (bf16[96,1536]{1,0:T(8,128)(2,1)S(1)}, bf16[96,1536]{1,0:T(8,128)(2,1)S(1)}, u32[]{:S(2)}, u32[]{:S(2)}) collective-permute-start(bf16[96,1536]{1,0:T(8,128)(2,1)S(1)} %add_convert_fusion.1), channel_id=1, source_target_pairs={{0,64},{64,128},{128,192},{192,0},{1,65},{65,129},{129,193},{193,1... | collective-permute-start | bytes 884744 | tf_op jit(solution)/shard_map/y1_294kB/ppermute | solution.py:26
  147.7 10.6 %collective-permute-start.18 = (bf16[96,1536]{1,0:T(8,128)(2,1)S(1)}, bf16[96,1536]{1,0:T(8,128)(2,1)S(1)}, u32[]{:S(2)}, u32[]{:S(2)}) collective-permute-start(bf16[96,1536]{1,0:T(8,128)(2,1)S(1)} %get-tuple-element.56), channel_id=1, source_target_pairs={{0,64},{64,128},{128,192},{192,0},{1,65},{65,129},{129,193},{193,1... | collective-permute-start | bytes 884744 | tf_op jit(solution)/shard_map/y1_294kB/ppermute | solution.py:26
  154.8 6.8 %collective-permute-start.20 = (bf16[96,1536]{1,0:T(8,128)(2,1)S(1)}, bf16[96,1536]{1,0:T(8,128)(2,1)S(1)}, u32[]{:S(2)}, u32[]{:S(2)}) collective-permute-start(bf16[96,1536]{1,0:T(8,128)(2,1)S(1)} %add_convert_fusion), channel_id=1, source_target_pairs={{0,192},{64,0},{128,64},{192,128},{1,193},{65,1},{129,65},{193,129... | collective-permute-start | bytes 884744 | tf_op jit(solution)/shard_map/y-1_294kB/ppermute | solution.py:26
  155.2 6.4 %copy-start.12 = (f32[1,96,3072]{2,1,0:T(8,128)S(1)}, f32[1,96,3072]{2,1,0:T(8,128)}, u32[]{:S(2)}) copy-start(f32[1,96,3072]{2,1,0:T(8,128)} %param.7) | copy-start | bytes 3538948
Sparse Core Ops, SparseCore 0:
  9.1 44.6 all-gather.5
  55.6 34.1 all-gather.3
  96.0 40.8 all-gather.7

commit v4 on v3

--- a/solution.py
+++ b/solution.py
@@ -79,7 +79,7 @@
     )(place, table, *arrays)
 
 
-def join_kernel(parts_ref, first_ref, chosen_ref, sems):
+def join_kernel(parts_ref, chosen_ref, sems):
     copies = [pltpu.make_async_copy(parts_ref.at[k], chosen_ref.at[:, k], sems.at[k]) for k in range(NX)]
     for copy in copies:
         copy.start()
@@ -87,16 +87,31 @@
         copy.wait()
 
 
-def join(parts, first):
+def join(parts):
     nx, ny, third, aux = parts.shape
     return pl.pallas_call(
         join_kernel,
         out_shape=jax.ShapeDtypeStruct((ny, nx, third, aux), BF),
-        in_specs=[ANY] * 2,
+        in_specs=[ANY],
         out_specs=ANY,
         scratch_shapes=[pltpu.SemaphoreType.DMA((NX,))],
         compiler_params=params(2),
-    )(parts, first)
+    )(parts)
+
+
+def same_kernel(block_ref, other_ref, same_ref):
+    pass
+
+
+def after(block, other):
+    return pl.pallas_call(
+        same_kernel,
+        out_shape=jax.ShapeDtypeStruct(block.shape, BF),
+        in_specs=[ANY] * 2,
+        out_specs=ANY,
+        input_output_aliases={0: 0},
+        compiler_params=params(62),
+    )(block, other)
 
 
 def last_kernel(fore_ref, back_ref, late_ref, a_ref, b_ref, later_ref, sems):
@@ -125,51 +140,36 @@
     )(fore, back, late)
 
 
-def left_kernel(dist, more, place_ref, amps_ref, *refs):
-    blocks, refs = refs[: len(dist)], refs[len(dist) :]
-    before, (left_ref, full_ref, *last_ref, amps, sems) = (refs[:2], refs[2:]) if more else (None, refs)
+def left_kernel(dist, place_ref, amps_ref, *refs):
+    blocks, (left_ref, full_ref, last_ref) = refs[:-3], refs[-3:]
     z, rows = place_ref[1], blocks[0].shape[0]
 
-    def columns(d):
-        return pl.ds(pl.multiple_of((z + NZ + d) % NZ * rows, 128), rows)
-
-    copies = []
+    def amps(d):
+        return amps_ref[:, pl.ds(pl.multiple_of((z + NZ + d) % NZ * rows, 128), rows)]
+
     for n, d in enumerate(dist):
-        copies.append(pltpu.make_async_copy(blocks[n], full_ref.at[(z + NZ + d) % NZ], sems.at[n, 0]))
-        copies.append(pltpu.make_async_copy(amps_ref.at[:, columns(d)], amps.at[n], sems.at[n, 1]))
-    if more:
-        copies.append(pltpu.make_async_copy(amps_ref.at[:, columns(NZ // 2)], last_ref[0], sems.at[len(dist), 0]))
-    for copy in copies:
-        copy.start()
-    for n, d in enumerate(dist):
-        copies[2 * n].wait()
-        copies[2 * n + 1].wait()
-        block = full_ref[(z + NZ + d) % NZ]
-        part = dot(amps[n], block)
+        block = blocks[n][...]
+        full_ref[(z + NZ + d) % NZ] = block
+        part = dot(amps(d), block)
         if n:
             left_ref[...] += part
-        elif more:
-            left_ref[...] = before[0][...] + part
         else:
             left_ref[...] = block.astype(F32) + part
-    if more:
-        copies[-1].wait()
-
-
-def add_left(place, amps, dist, blocks, before=()):
+    last_ref[...] = amps(NZ // 2)
+
+
+def add_left(place, amps, dist, blocks):
     rows, aux = blocks[0].shape
-    n, more = len(dist), bool(before)
-    shapes = [((rows, aux), F32), ((NZ, rows, aux), BF)] + [((rows, rows), BF)] * more
-    return pl.pallas_call(
-        functools.partial(left_kernel, dist, more),
+    n = len(dist)
+    shapes = [((rows, aux), F32), ((NZ, rows, aux), BF), ((rows, rows), BF)]
+    return pl.pallas_call(
+        functools.partial(left_kernel, dist),
         out_shape=[jax.ShapeDtypeStruct(*a) for a in shapes],
-        in_specs=[SMEM, VMEM] + [ANY] * n + [VMEM] * len(before),
+        in_specs=[SMEM, VMEM] + [VMEM] * n,
         out_specs=[VMEM] * len(shapes),
-        scratch_shapes=[pltpu.VMEM((n, rows, rows), BF), pltpu.SemaphoreType.DMA((n + 1, 2))],
-        input_output_aliases={2 + n: 0, 3 + n: 1} if more else {},
         compiler_params=params(8),
         cost_estimate=cost(2 * rows * aux * rows * n),
-    )(place, amps, *blocks, *before)
+    )(place, amps, *blocks)
 
 
 def first_kernel(pairs, place_ref, amps_ref, acc_ref, full_ref, far_a_ref, far_b_ref, left, part_a_ref, part_b_ref):
@@ -182,12 +182,16 @@
     part_b_ref[...] = part[:, h:]
 
 
-def second_kernel(pairs, place_ref, left, full_ref, far_a_ref, far_b_ref, *refs):
+def second_kernel(pairs, place_ref, left, full_ref, far_a_ref, far_b_ref, amps_ref, *refs):
+    copy_ref, sem = refs[-2:]
+    copy = pltpu.make_async_copy(amps_ref, copy_ref, sem)
+    copy.start()
     h = far_a_ref.shape[1]
     for n, d in enumerate((1, 3, 0)):
         part = columns_for(d, pairs, place_ref, left, full_ref, far_a_ref, far_b_ref)
         for ref, half in zip(refs[2 * n : 2 * n + 2], (part[:, :h], part[:, h:])):
             ref[...] = half.astype(ref.dtype)
+    copy.wait()
 
 
 def columns_for(d, pairs, place_ref, left, full_ref, far_a_ref, far_b_ref):
@@ -199,25 +203,18 @@
 
 
 def out_kernel(pairs, first, place_ref, total_ref, amps_ref, own_ref, *refs):
-    send_refs, (total, rows, amps, sems) = refs[:-4], refs[-4:]
+    send_refs, (total, rows) = refs[:-2], refs[-2:]
     y = place_ref[0]
     width = total_ref.shape[1]
-    step = amps.shape[2]
-    copies = [
-        pltpu.make_async_copy(amps_ref.at[:, pl.ds(k * step, step)], amps.at[k], sems.at[k])
-        for k in range(amps.shape[0])
-    ]
-    for copy in copies:
-        copy.start()
+    step = width // 2
     for d in range(NY):
         block = total_ref[pl.ds(pl.multiple_of((y + d) % NY * pairs, 32), pairs)]
         total[d * pairs : (d + 1) * pairs] = block
         rows[d * pairs : (d + 1) * pairs] = block.astype(BF)
-    for k, copy in enumerate(copies):
+    for k in range(amps_ref.shape[1] // step):
         n, part = divmod(first + k * step, width)
         cols = pl.ds(k * step, step)
-        copy.wait()
-        prod = dot(rows[...], amps[k])
+        prod = dot(rows[...], amps_ref[:, cols])
         prod += jnp.where(y == n, total[:, part : part + step], 0.0)
         own_ref[:, cols] = prod[:pairs]
         for d in range(1, NY):
@@ -227,17 +224,14 @@
 def out_products(place, total, amps_i, first, pairs, kept):
     rows, cols = amps_i.shape
     types = [F32 if d in (0, kept) else BF for d in range(NY)]
-    step = total.shape[1] // 2
     return pl.pallas_call(
         functools.partial(out_kernel, pairs, first),
         out_shape=[jax.ShapeDtypeStruct((pairs, cols), t) for t in types],
-        in_specs=[SMEM, VMEM, ANY],
+        in_specs=[SMEM, VMEM, VMEM],
         out_specs=[VMEM] * NY,
         scratch_shapes=[
             pltpu.VMEM(total.shape, F32),
             pltpu.VMEM(total.shape, BF),
-            pltpu.VMEM((cols // step, rows, step), BF),
-            pltpu.SemaphoreType.DMA((cols // step,)),
         ],
         compiler_params=params(10),
         cost_estimate=cost(2 * total.size * cols),
@@ -270,7 +264,7 @@
     (mine,) = choose(mine_kernel, (held,), place, pair_table, held, shift(sent, "c", 1))
     amps_j = lax.all_gather(by_z, "y", axis=0, tiled=True)
     parts = lax.all_to_all(mine, "x", split_axis=0, concat_axis=0, tiled=True)
-    chosen = join(parts, amps_i0).reshape(rows, aux)
+    chosen = after(join(parts).reshape(rows, aux), amps_i0)
 
     dist, blocks = [0], [chosen]
     fore = back = chosen
@@ -282,9 +276,7 @@
     far_a, far_b = shift(far_a, "z", 1), shift(far_b, "z", -1)
     amps_i1 = lax.all_gather(later, "z", axis=0, tiled=True)
 
-    n = len(blocks) - 2
-    acc = add_left(place, amps_j, dist[:n], blocks[:n])
-    acc, full, amps_last = add_left(place, amps_j, dist[n:], blocks[n:], acc)
+    acc, full, amps_last = add_left(place, amps_j, dist, blocks)
     part, kept = (jax.ShapeDtypeStruct((rows, width // 2), t) for t in (BF, F32))
     left, two_a, two_b = pl.pallas_call(
         functools.partial(first_kernel, pairs),
@@ -294,14 +286,15 @@
         compiler_params=params(8),
         cost_estimate=cost(2 * rows * aux * (rows + width)),
     )(place, amps_last, acc, full, far_a, far_b)
-    one_a, one_b, three_a, three_b, own_a, own_b = pl.pallas_call(
+    one_a, one_b, three_a, three_b, own_a, own_b, amps_i0 = pl.pallas_call(
         functools.partial(second_kernel, pairs),
-        out_shape=[kept, part, part, kept, kept, kept],
-        in_specs=[SMEM] + [VMEM] * 4,
-        out_specs=[VMEM] * 6,
+        out_shape=[kept, part, part, kept, kept, kept, jax.ShapeDtypeStruct(amps_i0.shape, BF)],
+        in_specs=[SMEM] + [VMEM] * 4 + [ANY],
+        out_specs=[VMEM] * 7,
+        scratch_shapes=[pltpu.SemaphoreType.DMA],
         compiler_params=params(8),
         cost_estimate=cost(6 * rows * aux * width),
-    )(place, left, full, far_a, far_b)
+    )(place, left, full, far_a, far_b, amps_i0)
     total = [collect(own_a, two_a, three_a, one_a, 1), collect(own_b, two_b, one_b, three_b, -1)]
     total = jnp.concatenate(total, axis=1)
 

time: 170 us -> 164 us (0.965)
  waiting for transfers between devices: 72.1 us -> 63.4 us
  starting transfers between devices: 34.4 us -> 40.1 us
  Pallas kernels: 19.2 us -> 14.7 us
  other arithmetic: 1.68 us -> 3.66 us
    ppermute x21, starting transfers between devices: 26.8 us -> 32.5 us  [shift(): return lax.ppermute(block, axis, [(i, (i + step) % n) for i in range(n)])]
    ppermute x21, waiting for transfers between devices: 56.5 us -> 51.3 us  [shift(): return lax.ppermute(block, axis, [(i, (i + step) % n) for i in range(n)])]
    pallas_call x2, Pallas kernels: 5.81 us -> 2.98 us  [the longest x1 2.97 us: add_left(): pl.pallas_call(functools.partial(left_kernel, dist), out_shape=[jax.Shape...]
    unnamed x28, local copies, waits for them, and re-layouts: 9.44 us -> 7.02 us
    all_to_all x1, waiting for transfers between devices: 7.71 us -> 5.37 us  [shards(): lax.all_to_all(own, ('x', 'y'), split_axis=0, concat_axis=0, tiled=True)]
    pallas_call x2, Pallas kernels: 5.6 us -> 3.89 us  [out_products(): pl.pallas_call(functools.partial(out_kernel, pairs, first), out_shape=[ja...]
  transfers between devices with their start and end apart: 25 -> 25, of which waited for: 14 -> 12; matrix products, arithmetic and copies ran while one was open for 2% -> 5% of each run, Pallas kernels for 11% -> 9%
where the time goes in v4:
time: 164 us
  waiting for transfers between devices  63.4 us (39%)
  starting transfers between devices  40.1 us (24%)
  local copies, waits for them, and re-layouts  14.7 us (9%)
  Pallas kernels  14.7 us (9%)
  blocking collectives  13.7 us (8%)
  between operations  13.4 us (8%)
  other arithmetic  3.66 us (2%)
    ppermute x21, waiting for transfers between devices, shift(): return lax.ppermute(block, axis, [(i, (i + step) % n) for i in range(n)])  51.3 us
    ppermute x21, starting transfers between devices, shift(): return lax.ppermute(block, axis, [(i, (i + step) % n) for i in range(n)])  32.5 us
    all_to_all x1, blocking collectives, shards(): parts = lax.all_to_all(mine, 'x', split_axis=0, concat_axis=0, tiled=True)  13.7 us
    all_to_all x1, starting transfers between devices, shards(): lax.all_to_all(own, ('x', 'y'), split_axis=0, concat_axis=0, tiled=True)  7.48 us
    unnamed x28, local copies, waits for them, and re-layouts  7.02 us
    all_gather x1, waiting for transfers between devices, shards(): amps_i0 = lax.all_gather(amps[:, :early], 'z', axis=0, tiled=True)  6.68 us
    all_to_all x1, waiting for transfers between devices, shards(): lax.all_to_all(own, ('x', 'y'), split_axis=0, concat_axis=0, tiled=True)  5.37 us
    pallas_call x2, Pallas kernels, out_products(): pl.pallas_call(functools.partial(out_kernel, pairs, first), out_shape=[ja...  3.89 us
  transfers between devices with their start and end apart: 25, of which 12 were waited for; matrix products, arithmetic and copies ran while one was open for 5% of the time, Pallas kernels for 9%

profile of v4, /device:TPU:2, one launch (start us, length us, event | category | flops | bytes accessed | tf_op | source)
XLA Modules:
  0.0 163.6 jit_solution(6366256959963152120)
XLA Ops:
  6.5 1.9 %fusion.2 = (bf16[96,1536]{1,0:T(8,128)(2,1)S(1)}, bf16[96,1536]{1,0:T(8,128)(2,1)}) fusion(bf16[96,3072]{1,0:T(8,128)(2,1)} %bitcast.23), kind=kLoop, calls=%fused_computation.14 | loop fusion | bytes 1179648 | tf_op jit(solution)/shard_map/slice | solution.py:275
  8.9 0.9 copy.6
  9.8 7.5 %all-to-all-start = ((bf16[16,24,768]{2,1,0:T(8,128)(2,1)}), bf16[16,24,768]{2,1,0:T(8,128)(2,1)S(1)}, u32[]{:S(2)}, u32[]{:S(2)}) async-start(bf16[16,24,768]{2,1,0:T(8,128)(2,1)} %bitcast.6), calls=%async_computation | async-start | bytes 1179648 | tf_op jit(solution)/shard_map/all_to_all | solution.py:262
  18.1 1.2 copy.9
  19.3 2.5 %reshape.47.amps_ref = bf16[96,3072]{1,0:T(8,128)(2,1)S(1)} reshape(bf16[96,8,4,96]{3,2,1,0:T(4,128)(2,1)} %bitcast.21) | data formatting | bytes 1179648 | tf_op jit(solution)/shard_map/reshape | solution.py:258
  21.9 5.4 %all-to-all-done = bf16[16,24,768]{2,1,0:T(8,128)(2,1)S(1)} async-done(((bf16[16,24,768]{2,1,0:T(8,128)(2,1)}), bf16[16,24,768]{2,1,0:T(8,128)(2,1)S(1)}, u32[]{:S(2)}, u32[]{:S(2)}) %all-to-all-start) | async-done | bytes 589856 | tf_op jit(solution)/shard_map/all_to_all | solution.py:262
  27.3 1.4 shard_map.46
  28.9 2.0 %collective-permute-done.sent_ref = bf16[4,4,24,768]{3,2,1,0:T(8,128)(2,1)S(1)} collective-permute-done((bf16[4,4,24,768]{3,2,1,0:T(8,128)(2,1)S(1)}, bf16[4,4,24,768]{3,2,1,0:T(8,128)(2,1)S(1)}, u32[]{:S(2)}, u32[]{:S(2)}) %collective-permute-start) | collective-permute-done | bytes 589856 | tf_op jit(solution)/shard_map/c1_589kB/ppermute | solution.py:26
  30.9 1.4 shard_map.47
  32.3 13.7 %all_to_all.10.parts_ref = bf16[4,4,24,768]{3,2,1,0:T(8,128)(2,1)S(1)} all-to-all(bf16[4,4,24,768]{3,2,1,0:T(8,128)(2,1)S(1)} %shard_map.47), channel_id=1, replica_groups=mesh['y'=4,'z'=8,'x'=4,'c'=2] {'x'}, dimensions={0} | all-to-all | bytes 1179648 | tf_op jit(solution)/shard_map/all_to_all | solution.py:266
  47.0 6.7 %all-gather.6.cloned.1.call-done.other_ref.amps_ref = bf16[768,1536]{1,0:T(8,128)(2,1)} async-done(((bf16[96,1536]{1,0:T(8,128)(2,1)}), bf16[768,1536]{1,0:T(8,128)(2,1)}) %all-gather.6.cloned.1.call-update) | async-done | bytes 2359312 | tf_op jit(solution)/shard_map/all_gather | solution.py:257
  53.7 1.6 collective-permute-start.1
  55.3 1.7 %collective-permute-start.2 = (bf16[384,768]{1,0:T(8,128)(2,1)}, bf16[384,768]{1,0:T(8,128)(2,1)S(1)}, u32[]{:S(2)}, u32[]{:S(2)}) collective-permute-start(bf16[384,768]{1,0:T(8,128)(2,1)} %shard_map.49.refs_0_), channel_id=1, source_target_pairs={{0,56},{8,0},{16,8},{24,16},{32,24},{40,32},{48,40},{56,48},{1,57}... | collective-permute-start | bytes 1769480 | tf_op jit(solution)/shard_map/z-1_589kB/ppermute | solution.py:26
  56.9 10.5 %collective-permute-done.1.refs_1_ = bf16[384,768]{1,0:T(8,128)(2,1)S(1)} collective-permute-done((bf16[384,768]{1,0:T(8,128)(2,1)}, bf16[384,768]{1,0:T(8,128)(2,1)S(1)}, u32[]{:S(2)}, u32[]{:S(2)}) %collective-permute-start.1) | collective-permute-done | bytes 589856 | tf_op jit(solution)/shard_map/z1_589kB/ppermute | solution.py:26
  67.5 3.1 %collective-permute-start.4 = (bf16[384,768]{1,0:T(8,128)(2,1)S(1)}, bf16[384,768]{1,0:T(8,128)(2,1)S(1)}, u32[]{:S(2)}, u32[]{:S(2)}) collective-permute-start(bf16[384,768]{1,0:T(8,128)(2,1)S(1)} %collective-permute-done.2.refs_2_), channel_id=1, source_target_pairs={{0,56},{8,0},{16,8},{24,16},{32,24},{40,32},{48,40},{56,48},{1,57}... | collective-permute-start | bytes 1769480 | tf_op jit(solution)/shard_map/z-1_589kB/ppermute | solution.py:26
  70.6 10.1 %collective-permute-done.3.refs_3_ = bf16[384,768]{1,0:T(8,128)(2,1)S(1)} collective-permute-done((bf16[384,768]{1,0:T(8,128)(2,1)S(1)}, bf16[384,768]{1,0:T(8,128)(2,1)S(1)}, u32[]{:S(2)}, u32[]{:S(2)}) %collective-permute-start.3) | collective-permute-done | bytes 589856 | tf_op jit(solution)/shard_map/z1_589kB/ppermute | solution.py:26
  80.9 3.1 %collective-permute-start.6 = (bf16[384,768]{1,0:T(8,128)(2,1)S(1)}, bf16[384,768]{1,0:T(8,128)(2,1)S(1)}, u32[]{:S(2)}, u32[]{:S(2)}) collective-permute-start(bf16[384,768]{1,0:T(8,128)(2,1)S(1)} %collective-permute-done.4.refs_4_), channel_id=1, source_target_pairs={{0,56},{8,0},{16,8},{24,16},{32,24},{40,32},{48,40},{56,48},{1,57}... | collective-permute-start | bytes 1769480 | tf_op jit(solution)/shard_map/z-1_589kB/ppermute | solution.py:26
  84.0 8.6 %collective-permute-done.5.refs_5_.fore_ref = bf16[384,768]{1,0:T(8,128)(2,1)S(1)} collective-permute-done((bf16[384,768]{1,0:T(8,128)(2,1)S(1)}, bf16[384,768]{1,0:T(8,128)(2,1)S(1)}, u32[]{:S(2)}, u32[]{:S(2)}) %collective-permute-start.5) | collective-permute-done | bytes 589856 | tf_op jit(solution)/shard_map/z1_589kB/ppermute | solution.py:26
  92.7 0.8 shard_map.51
  94.7 2.9 %collective-permute-start.8 = (bf16[384,384]{1,0:T(8,128)(2,1)}, bf16[384,384]{1,0:T(8,128)(2,1)S(1)}, u32[]{:S(2)}, u32[]{:S(2)}) collective-permute-start(bf16[384,384]{1,0:T(8,128)(2,1)} %copy-done.10), channel_id=1, source_target_pairs={{0,56},{8,0},{16,8},{24,16},{32,24},{40,32},{48,40},{56,48},{1,57}... | collective-permute-start | bytes 884744 | tf_op jit(solution)/shard_map/z-1_294kB/ppermute | solution.py:26
  97.6 1.7 %copy-done.3 = bf16[384,3072]{1,0:T(8,128)(2,1)S(1)} copy-done((bf16[384,3072]{1,0:T(8,128)(2,1)S(1)}, bf16[384,3072]{1,0:T(8,128)(2,1)}, u32[]{:S(2)}) %copy-start.3) | copy-done | bytes 2359320
  99.2 1.1 copy-done.6
  100.3 1.1 copy-done.8
  101.4 3.0 %shard_map.50 = (f32[384,768]{1,0:T(8,128)S(1)}, bf16[8,384,768]{2,1,0:T(8,128)(2,1)S(1)}, bf16[384,384]{1,0:T(8,128)(2,1)S(1)}) custom-call(s32[3]{0:T(128)S(1)} %pad_add_fusion.place_ref, bf16[384,3072]{1,0:T(8,128)(2,1)S(1)} %copy-done.3, bf16[384,768]{1,0:T(8,128)(2,1)S(1)} %copy-done.2, bf16[384,768]{1,0:T(8,128)(2,1)S(1)} %collective-permute-done.1.refs_1_, ...), custom_call_target="tpu_custom_call" | custom-call | flops 1585446912 | bytes 8388608 | tf_op jit(solution)/shard_map/pallas_call | solution.py:165
  104.4 1.7 %shard_map.52 = (bf16[384,768]{1,0:T(8,128)(2,1)S(1)}, bf16[384,384]{1,0:T(8,128)(2,1)S(1)}, bf16[384,384]{1,0:T(8,128)(2,1)S(1)}) custom-call(s32[3]{0:T(128)S(1)} %pad_add_fusion.place_ref, bf16[384,384]{1,0:T(8,128)(2,1)S(1)} %get-tuple-element.33.amps_ref, f32[384,768]{1,0:T(8,128)S(1)} %get-tuple-element.34.acc_ref, ...), custom_call_target="tpu_custom_call" | custom-call | flops 679477248 | bytes 8388608 | tf_op jit(solution)/shard_map/pallas_call | solution.py:281
  106.1 2.0 %collective-permute-start.10 = (bf16[384,384]{1,0:T(8,128)(2,1)S(1)}, bf16[384,384]{1,0:T(8,128)(2,1)S(1)}, u32[]{:S(2)}, u32[]{:S(2)}) collective-permute-start(bf16[384,384]{1,0:T(8,128)(2,1)S(1)} %get-tuple-element.42), channel_id=1, source_target_pairs={{0,64},{64,128},{128,192},{192,0},{1,65},{65,129},{129,193},{193,1... | collective-permute-start | bytes 884744 | tf_op jit(solution)/shard_map/y1_294kB/ppermute | solution.py:26
  108.1 1.3 collective-permute-start.13
  109.4 2.3 %shard_map.53 = (f32[384,384]{1,0:T(8,128)S(1)}, bf16[384,384]{1,0:T(8,128)(2,1)S(1)}, bf16[384,384]{1,0:T(8,128)(2,1)S(1)}, f32[384,384]{1,0:T(8,128)S(1)}, f32...) custom-call(s32[3]{0:T(128)S(1)} %pad_add_fusion.place_ref, ...), custom_call_target="tpu_custom_call" | custom-call | flops 1358954496 | bytes 8388608 | tf_op jit(solution)/shard_map/pallas_call | solution.py:289
  111.7 1.7 %collective-permute-start.9 = (bf16[384,384]{1,0:T(8,128)(2,1)S(1)}, bf16[384,384]{1,0:T(8,128)(2,1)S(1)}, u32[]{:S(2)}, u32[]{:S(2)}) collective-permute-start(bf16[384,384]{1,0:T(8,128)(2,1)S(1)} %get-tuple-element.40), channel_id=1, source_target_pairs={{0,192},{64,0},{128,64},{192,128},{1,193},{65,1},{129,65},{193,129... | collective-permute-start | bytes 884744 | tf_op jit(solution)/shard_map/y-1_294kB/ppermute | solution.py:26
  113.4 3.8 %collective-permute-done.10 = bf16[384,384]{1,0:T(8,128)(2,1)S(1)} collective-permute-done((bf16[384,384]{1,0:T(8,128)(2,1)S(1)}, bf16[384,384]{1,0:T(8,128)(2,1)S(1)}, u32[]{:S(2)}, u32[]{:S(2)}) %collective-permute-start.10) | collective-permute-done | bytes 294944 | tf_op jit(solution)/shard_map/y1_294kB/ppermute | solution.py:26
  117.3 0.9 collective-permute-start.11
  118.2 0.9 collective-permute-start.12
  119.2 2.4 %collective-permute-start.14 = (bf16[384,384]{1,0:T(8,128)(2,1)S(1)}, bf16[384,384]{1,0:T(8,128)(2,1)S(1)}, u32[]{:S(2)}, u32[]{:S(2)}) collective-permute-start(bf16[384,384]{1,0:T(8,128)(2,1)S(1)} %add_convert_fusion.2), channel_id=1, source_target_pairs={{0,192},{64,0},{128,64},{192,128},{1,193},{65,1},{129,65},{193,129... | collective-permute-start | bytes 884744 | tf_op jit(solution)/shard_map/y-1_294kB/ppermute | solution.py:26
  121.6 3.7 %collective-permute-done.11 = bf16[384,384]{1,0:T(8,128)(2,1)S(1)} collective-permute-done((bf16[384,384]{1,0:T(8,128)(2,1)S(1)}, bf16[384,384]{1,0:T(8,128)(2,1)S(1)}, u32[]{:S(2)}, u32[]{:S(2)}) %collective-permute-start.11) | collective-permute-done | bytes 294944 | tf_op jit(solution)/shard_map/y1_294kB/ppermute | solution.py:26
  125.4 5.2 %collective-permute-done.12 = bf16[384,384]{1,0:T(8,128)(2,1)S(1)} collective-permute-done((bf16[384,384]{1,0:T(8,128)(2,1)S(1)}, bf16[384,384]{1,0:T(8,128)(2,1)S(1)}, u32[]{:S(2)}, u32[]{:S(2)}) %collective-permute-start.12) | collective-permute-done | bytes 294944 | tf_op jit(solution)/shard_map/y1_294kB/ppermute | solution.py:26
  130.8 2.0 %shard_map.54 = (f32[96,1536]{1,0:T(8,128)S(1)}, f32[96,1536]{1,0:T(8,128)S(1)}, bf16[96,1536]{1,0:T(8,128)(2,1)S(1)}, bf16[96,1536]{1,0:T(8,128)(2,1)S(1)}) custom-call(s32[3]{0:T(128)S(1)} %pad_add_fusion.place_ref, f32[384,768]{1,0:T(8,128)S(1)} %pad_maximum_fusion.total_ref, bf16[768,1536]{1,0:T(8,128)(2,1)S(1)} %get-tuple-element.47.amps_ref), custom_call_target="tpu_custom_call" | custom-call | flops 905969664 | bytes 8388608 | tf_op jit(solution)/shard_map/pallas_call | solution.py:227
  133.0 3.1 %collective-permute-start.15 = (bf16[96,1536]{1,0:T(8,128)(2,1)S(1)}, bf16[96,1536]{1,0:T(8,128)(2,1)}, u32[]{:S(2)}, u32[]{:S(2)}) collective-permute-start(bf16[96,1536]{1,0:T(8,128)(2,1)S(1)} %get-tuple-element.49), channel_id=1, source_target_pairs={{0,192},{64,0},{128,64},{192,128},{1,193},{65,1},{129,65},{193,129... | collective-permute-start | bytes 884744 | tf_op jit(solution)/shard_map/y-1_294kB/ppermute | solution.py:26
  136.1 1.7 %copy-done.4 = bf16[768,1536]{1,0:T(8,128)(2,1)S(1)} copy-done((bf16[768,1536]{1,0:T(8,128)(2,1)S(1)}, bf16[768,1536]{1,0:T(8,128)(2,1)}, u32[]{:S(2)}) %copy-start.4) | copy-done | bytes 2359320
  137.8 1.9 %shard_map.55 = (f32[96,1536]{1,0:T(8,128)S(1)}, bf16[96,1536]{1,0:T(8,128)(2,1)S(1)}, bf16[96,1536]{1,0:T(8,128)(2,1)S(1)}, f32[96,1536]{1,0:T(8,128)S(1)}) custom-call(s32[3]{0:T(128)S(1)} %pad_add_fusion.place_ref, f32[384,768]{1,0:T(8,128)S(1)} %pad_maximum_fusion.total_ref, bf16[768,1536]{1,0:T(8,128)(2,1)S(1)} %copy-done.4), custom_call_target="tpu_custom_call" | custom-call | flops 905969664 | bytes 8388608 | tf_op jit(solution)/shard_map/pallas_call | solution.py:227
  139.7 2.1 %collective-permute-start.19 = (bf16[96,1536]{1,0:T(8,128)(2,1)S(1)}, bf16[96,1536]{1,0:T(8,128)(2,1)S(1)}, u32[]{:S(2)}, u32[]{:S(2)}) collective-permute-start(bf16[96,1536]{1,0:T(8,128)(2,1)S(1)} %get-tuple-element.56), channel_id=1, source_target_pairs={{0,192},{64,0},{128,64},{192,128},{1,193},{65,1},{129,65},{193,129... | collective-permute-start | bytes 884744 | tf_op jit(solution)/shard_map/y-1_294kB/ppermute | solution.py:26
  141.8 1.0 add_convert_fusion.1
  143.0 0.9 collective-permute-start.18
  143.8 2.8 %collective-permute-done.19 = bf16[96,1536]{1,0:T(8,128)(2,1)S(1)} collective-permute-done((bf16[96,1536]{1,0:T(8,128)(2,1)S(1)}, bf16[96,1536]{1,0:T(8,128)(2,1)S(1)}, u32[]{:S(2)}, u32[]{:S(2)}) %collective-permute-start.19) | collective-permute-done | bytes 294944 | tf_op jit(solution)/shard_map/y-1_294kB/ppermute | solution.py:26
  146.8 3.8 %collective-permute-start.20 = (bf16[96,1536]{1,0:T(8,128)(2,1)S(1)}, bf16[96,1536]{1,0:T(8,128)(2,1)S(1)}, u32[]{:S(2)}, u32[]{:S(2)}) collective-permute-start(bf16[96,1536]{1,0:T(8,128)(2,1)S(1)} %add_convert_fusion), channel_id=1, source_target_pairs={{0,192},{64,0},{128,64},{192,128},{1,193},{65,1},{129,65},{193,129... | collective-permute-start | bytes 884744 | tf_op jit(solution)/shard_map/y-1_294kB/ppermute | solution.py:26
  150.5 2.3 %collective-permute-done.17 = bf16[96,1536]{1,0:T(8,128)(2,1)S(1)} collective-permute-done((bf16[96,1536]{1,0:T(8,128)(2,1)S(1)}, bf16[96,1536]{1,0:T(8,128)(2,1)S(1)}, u32[]{:S(2)}, u32[]{:S(2)}) %collective-permute-start.17) | collective-permute-done | bytes 294944 | tf_op jit(solution)/shard_map/y1_294kB/ppermute | solution.py:26
  152.8 1.0 add_bitcast_fusion.1
  153.9 2.1 %collective-permute-done.18 = bf16[96,1536]{1,0:T(8,128)(2,1)S(1)} collective-permute-done((bf16[96,1536]{1,0:T(8,128)(2,1)S(1)}, bf16[96,1536]{1,0:T(8,128)(2,1)S(1)}, u32[]{:S(2)}, u32[]{:S(2)}) %collective-permute-start.18) | collective-permute-done | bytes 294944 | tf_op jit(solution)/shard_map/y1_294kB/ppermute | solution.py:26
  156.1 1.0 fusion.1
  (62 shorter events, 4.8 us)
Async XLA Ops:
  6.5 1.9 %copy-start.13 = (bf16[1,3000,96]{1,2,0:T(8,128)(2,1)S(1)}, bf16[1,3000,96]{1,2,0:T(8,128)(2,1)}, u32[]{:S(2)}) copy-start(bf16[1,3000,96]{1,2,0:T(8,128)(2,1)} %param.5) | copy-start | bytes 1728004
  6.5 47.2 %all-gather.6.cloned.1.call-start = ((), (), s32[]{:S(2)}) async-start(), calls=%async_computation.3 | async-start | bytes 2654208 | tf_op jit(solution)/shard_map/all_gather | solution.py:257
  8.9 8.4 %copy-start.11 = (bf16[1,96,3072]{2,1,0:T(8,128)(2,1)S(1)}, bf16[1,96,3072]{2,1,0:T(8,128)(2,1)}, u32[]{:S(2)}) copy-start(bf16[1,96,3072]{2,1,0:T(8,128)(2,1)} %param.6) | copy-start | bytes 1769476
  9.8 17.5 %all-to-all-start = ((bf16[16,24,768]{2,1,0:T(8,128)(2,1)}), bf16[16,24,768]{2,1,0:T(8,128)(2,1)S(1)}, u32[]{:S(2)}, u32[]{:S(2)}) async-start(bf16[16,24,768]{2,1,0:T(8,128)(2,1)} %bitcast.6), calls=%async_computation | async-start | bytes 1179648 | tf_op jit(solution)/shard_map/all_to_all | solution.py:262
  17.3 80.3 %all-gather.4.cloned.1.call-start = ((), (), s32[]{:S(2)}) async-start(), calls=%async_computation.2 | async-start | bytes 2949120 | tf_op jit(solution)/shard_map/all_gather | solution.py:265
  18.1 9.2 %copy-start.9 = (s32[8]{0:T(128)S(1)}, s32[8]{0:T(128)}, u32[]{:S(2)}) copy-start(s32[8]{0:T(128)} %table_ref.3) | copy-start | bytes 100
  28.7 107.4 %all-gather.8.cloned.1.call-start = ((), (), s32[]{:S(2)}) async-start(), calls=%async_computation.4 | async-start | bytes 2654208 | tf_op jit(solution)/shard_map/all_gather | solution.py:277
  28.8 2.1 %collective-permute-start = (bf16[4,4,24,768]{3,2,1,0:T(8,128)(2,1)S(1)}, bf16[4,4,24,768]{3,2,1,0:T(8,128)(2,1)S(1)}, u32[]{:S(2)}, u32[]{:S(2)}) collective-permute-start(bf16[4,4,24,768]{3,2,1,0:T(8,128)(2,1)S(1)} %get-tuple-element.32), channel_id=1, source_target_pairs={{0,1},{1,0},{2,3},{3,2},{4,5},{5,4},{6,7},{7,6},{8,9},{9,8},{10,11... | collective-permute-start | bytes 1769480 | tf_op jit(solution)/shard_map/c1_589kB/ppermute | solution.py:26
  46.2 0.8 copy-start.1
  53.7 43.9 %copy-start.2 = (bf16[384,768]{1,0:T(8,128)(2,1)S(1)}, bf16[384,768]{1,0:T(8,128)(2,1)}, u32[]{:S(2)}) copy-start(bf16[384,768]{1,0:T(8,128)(2,1)} %shard_map.49.refs_0_) | copy-start | bytes 1769476
  53.7 13.7 %collective-permute-start.1 = (bf16[384,768]{1,0:T(8,128)(2,1)}, bf16[384,768]{1,0:T(8,128)(2,1)S(1)}, u32[]{:S(2)}, u32[]{:S(2)}) collective-permute-start(bf16[384,768]{1,0:T(8,128)(2,1)} %shard_map.49.refs_0_), channel_id=1, source_target_pairs={{0,8},{8,16},{16,24},{24,32},{32,40},{40,48},{48,56},{56,0},{1,9},... | collective-permute-start | bytes 1769480 | tf_op jit(solution)/shard_map/z1_589kB/ppermute | solution.py:26
  55.3 12.2 %collective-permute-start.2 = (bf16[384,768]{1,0:T(8,128)(2,1)}, bf16[384,768]{1,0:T(8,128)(2,1)S(1)}, u32[]{:S(2)}, u32[]{:S(2)}) collective-permute-start(bf16[384,768]{1,0:T(8,128)(2,1)} %shard_map.49.refs_0_), channel_id=1, source_target_pairs={{0,56},{8,0},{16,8},{24,16},{32,24},{40,32},{48,40},{56,48},{1,57}... | collective-permute-start | bytes 1769480 | tf_op jit(solution)/shard_map/z-1_589kB/ppermute | solution.py:26
  67.4 13.4 %collective-permute-start.3 = (bf16[384,768]{1,0:T(8,128)(2,1)S(1)}, bf16[384,768]{1,0:T(8,128)(2,1)S(1)}, u32[]{:S(2)}, u32[]{:S(2)}) collective-permute-start(bf16[384,768]{1,0:T(8,128)(2,1)S(1)} %collective-permute-done.1.refs_1_), channel_id=1, source_target_pairs={{0,8},{8,16},{16,24},{24,32},{32,40},{40,48},{48,56},{56,0},{1,9},... | collective-permute-start | bytes 1769480 | tf_op jit(solution)/shard_map/z1_589kB/ppermute | solution.py:26
  67.5 13.4 %collective-permute-start.4 = (bf16[384,768]{1,0:T(8,128)(2,1)S(1)}, bf16[384,768]{1,0:T(8,128)(2,1)S(1)}, u32[]{:S(2)}, u32[]{:S(2)}) collective-permute-start(bf16[384,768]{1,0:T(8,128)(2,1)S(1)} %collective-permute-done.2.refs_2_), channel_id=1, source_target_pairs={{0,56},{8,0},{16,8},{24,16},{32,24},{40,32},{48,40},{56,48},{1,57}... | collective-permute-start | bytes 1769480 | tf_op jit(solution)/shard_map/z-1_589kB/ppermute | solution.py:26
  80.8 12.7 %copy-start.5 = (bf16[384,768]{1,0:T(8,128)(2,1)}, bf16[384,768]{1,0:T(8,128)(2,1)S(1)}, u32[]{:S(2)}) copy-start(bf16[384,768]{1,0:T(8,128)(2,1)S(1)} %collective-permute-done.3.refs_3_) | copy-start | bytes 1769476
  80.8 11.9 %collective-permute-start.5 = (bf16[384,768]{1,0:T(8,128)(2,1)S(1)}, bf16[384,768]{1,0:T(8,128)(2,1)S(1)}, u32[]{:S(2)}, u32[]{:S(2)}) collective-permute-start(bf16[384,768]{1,0:T(8,128)(2,1)S(1)} %collective-permute-done.3.refs_3_), channel_id=1, source_target_pairs={{0,8},{8,16},{16,24},{24,32},{32,40},{40,48},{48,56},{56,0},{1,9},... | collective-permute-start | bytes 1769480 | tf_op jit(solution)/shard_map/z1_589kB/ppermute | solution.py:26
  80.9 12.6 %copy-start.7 = (bf16[384,768]{1,0:T(8,128)(2,1)}, bf16[384,768]{1,0:T(8,128)(2,1)S(1)}, u32[]{:S(2)}) copy-start(bf16[384,768]{1,0:T(8,128)(2,1)S(1)} %collective-permute-done.4.refs_4_) | copy-start | bytes 1769476
  80.9 11.8 %collective-permute-start.6 = (bf16[384,768]{1,0:T(8,128)(2,1)S(1)}, bf16[384,768]{1,0:T(8,128)(2,1)S(1)}, u32[]{:S(2)}, u32[]{:S(2)}) collective-permute-start(bf16[384,768]{1,0:T(8,128)(2,1)S(1)} %collective-permute-done.4.refs_4_), channel_id=1, source_target_pairs={{0,56},{8,0},{16,8},{24,16},{32,24},{40,32},{48,40},{56,48},{1,57}... | collective-permute-start | bytes 1769480 | tf_op jit(solution)/shard_map/z-1_589kB/ppermute | solution.py:26
  93.5 0.7 copy-start.10
  94.3 10.1 %collective-permute-start.7 = (bf16[384,384]{1,0:T(8,128)(2,1)}, bf16[384,384]{1,0:T(8,128)(2,1)S(1)}, u32[]{:S(2)}, u32[]{:S(2)}) collective-permute-start(bf16[384,384]{1,0:T(8,128)(2,1)} %get-tuple-element.36), channel_id=1, source_target_pairs={{0,8},{8,16},{16,24},{24,32},{32,40},{40,48},{48,56},{56,0},{1,9},... | collective-permute-start | bytes 884744 | tf_op jit(solution)/shard_map/z1_294kB/ppermute | solution.py:26
  94.7 9.7 %collective-permute-start.8 = (bf16[384,384]{1,0:T(8,128)(2,1)}, bf16[384,384]{1,0:T(8,128)(2,1)S(1)}, u32[]{:S(2)}, u32[]{:S(2)}) collective-permute-start(bf16[384,384]{1,0:T(8,128)(2,1)} %copy-done.10), channel_id=1, source_target_pairs={{0,56},{8,0},{16,8},{24,16},{32,24},{40,32},{48,40},{56,48},{1,57}... | collective-permute-start | bytes 884744 | tf_op jit(solution)/shard_map/z-1_294kB/ppermute | solution.py:26
  97.6 1.7 %copy-start.3 = (bf16[384,3072]{1,0:T(8,128)(2,1)S(1)}, bf16[384,3072]{1,0:T(8,128)(2,1)}, u32[]{:S(2)}) copy-start(bf16[384,3072]{1,0:T(8,128)(2,1)} %all-gather.4.cloned.1.call-done.amps_ref) | copy-start | bytes 7077892
  99.2 1.1 copy-start.6
  100.3 1.1 copy-start.8
  104.4 5.0 %copy-start = (bf16[768,1536]{1,0:T(8,128)(2,1)S(1)}, bf16[768,1536]{1,0:T(8,128)(2,1)}, u32[]{:S(2)}) copy-start(bf16[768,1536]{1,0:T(8,128)(2,1)} %all-gather.6.cloned.1.call-done.other_ref.amps_ref) | copy-start | bytes 7077892
  106.1 11.2 %collective-permute-start.10 = (bf16[384,384]{1,0:T(8,128)(2,1)S(1)}, bf16[384,384]{1,0:T(8,128)(2,1)S(1)}, u32[]{:S(2)}, u32[]{:S(2)}) collective-permute-start(bf16[384,384]{1,0:T(8,128)(2,1)S(1)} %get-tuple-element.42), channel_id=1, source_target_pairs={{0,64},{64,128},{128,192},{192,0},{1,65},{65,129},{129,193},{193,1... | collective-permute-start | bytes 884744 | tf_op jit(solution)/shard_map/y1_294kB/ppermute | solution.py:26
  108.1 11.0 %collective-permute-start.13 = (bf16[384,384]{1,0:T(8,128)(2,1)S(1)}, bf16[384,384]{1,0:T(8,128)(2,1)S(1)}, u32[]{:S(2)}, u32[]{:S(2)}) collective-permute-start(bf16[384,384]{1,0:T(8,128)(2,1)S(1)} %get-tuple-element.46), channel_id=1, source_target_pairs={{0,192},{64,0},{128,64},{192,128},{1,193},{65,1},{129,65},{193,129... | collective-permute-start | bytes 884744 | tf_op jit(solution)/shard_map/y-1_294kB/ppermute | solution.py:26
  111.7 9.9 %collective-permute-start.9 = (bf16[384,384]{1,0:T(8,128)(2,1)S(1)}, bf16[384,384]{1,0:T(8,128)(2,1)S(1)}, u32[]{:S(2)}, u32[]{:S(2)}) collective-permute-start(bf16[384,384]{1,0:T(8,128)(2,1)S(1)} %get-tuple-element.40), channel_id=1, source_target_pairs={{0,192},{64,0},{128,64},{192,128},{1,193},{65,1},{129,65},{193,129... | collective-permute-start | bytes 884744 | tf_op jit(solution)/shard_map/y-1_294kB/ppermute | solution.py:26
  117.3 8.0 %collective-permute-start.11 = (bf16[384,384]{1,0:T(8,128)(2,1)S(1)}, bf16[384,384]{1,0:T(8,128)(2,1)S(1)}, u32[]{:S(2)}, u32[]{:S(2)}) collective-permute-start(bf16[384,384]{1,0:T(8,128)(2,1)S(1)} %add_convert_fusion.3), channel_id=1, source_target_pairs={{0,64},{64,128},{128,192},{192,0},{1,65},{65,129},{129,193},{193,1... | collective-permute-start | bytes 884744 | tf_op jit(solution)/shard_map/y1_294kB/ppermute | solution.py:26
  118.2 12.4 %collective-permute-start.12 = (bf16[384,384]{1,0:T(8,128)(2,1)S(1)}, bf16[384,384]{1,0:T(8,128)(2,1)S(1)}, u32[]{:S(2)}, u32[]{:S(2)}) collective-permute-start(bf16[384,384]{1,0:T(8,128)(2,1)S(1)} %get-tuple-element.44), channel_id=1, source_target_pairs={{0,64},{64,128},{128,192},{192,0},{1,65},{65,129},{129,193},{193,1... | collective-permute-start | bytes 884744 | tf_op jit(solution)/shard_map/y1_294kB/ppermute | solution.py:26
  119.2 11.5 %collective-permute-start.14 = (bf16[384,384]{1,0:T(8,128)(2,1)S(1)}, bf16[384,384]{1,0:T(8,128)(2,1)S(1)}, u32[]{:S(2)}, u32[]{:S(2)}) collective-permute-start(bf16[384,384]{1,0:T(8,128)(2,1)S(1)} %add_convert_fusion.2), channel_id=1, source_target_pairs={{0,192},{64,0},{128,64},{192,128},{1,193},{65,1},{129,65},{193,129... | collective-permute-start | bytes 884744 | tf_op jit(solution)/shard_map/y-1_294kB/ppermute | solution.py:26
  132.8 9.0 %collective-permute-start.16 = (bf16[96,1536]{1,0:T(8,128)(2,1)S(1)}, bf16[96,1536]{1,0:T(8,128)(2,1)}, u32[]{:S(2)}, u32[]{:S(2)}) collective-permute-start(bf16[96,1536]{1,0:T(8,128)(2,1)S(1)} %get-tuple-element.51), channel_id=1, source_target_pairs={{0,64},{64,128},{128,192},{192,0},{1,65},{65,129},{129,193},{193,1... | collective-permute-start | bytes 884744 | tf_op jit(solution)/shard_map/y1_294kB/ppermute | solution.py:26
  133.0 17.5 %collective-permute-start.15 = (bf16[96,1536]{1,0:T(8,128)(2,1)S(1)}, bf16[96,1536]{1,0:T(8,128)(2,1)}, u32[]{:S(2)}, u32[]{:S(2)}) collective-permute-start(bf16[96,1536]{1,0:T(8,128)(2,1)S(1)} %get-tuple-element.49), channel_id=1, source_target_pairs={{0,192},{64,0},{128,64},{192,128},{1,193},{65,1},{129,65},{193,129... | collective-permute-start | bytes 884744 | tf_op jit(solution)/shard_map/y-1_294kB/ppermute | solution.py:26
  136.1 1.7 %copy-start.4 = (bf16[768,1536]{1,0:T(8,128)(2,1)S(1)}, bf16[768,1536]{1,0:T(8,128)(2,1)}, u32[]{:S(2)}) copy-start(bf16[768,1536]{1,0:T(8,128)(2,1)} %all-gather.8.cloned.1.call-done.amps_ref) | copy-start | bytes 7077892
  139.7 7.0 %collective-permute-start.19 = (bf16[96,1536]{1,0:T(8,128)(2,1)S(1)}, bf16[96,1536]{1,0:T(8,128)(2,1)S(1)}, u32[]{:S(2)}, u32[]{:S(2)}) collective-permute-start(bf16[96,1536]{1,0:T(8,128)(2,1)S(1)} %get-tuple-element.56), channel_id=1, source_target_pairs={{0,192},{64,0},{128,64},{192,128},{1,193},{65,1},{129,65},{193,129... | collective-permute-start | bytes 884744 | tf_op jit(solution)/shard_map/y-1_294kB/ppermute | solution.py:26
  142.9 10.0 %collective-permute-start.17 = (bf16[96,1536]{1,0:T(8,128)(2,1)S(1)}, bf16[96,1536]{1,0:T(8,128)(2,1)S(1)}, u32[]{:S(2)}, u32[]{:S(2)}) collective-permute-start(bf16[96,1536]{1,0:T(8,128)(2,1)S(1)} %add_convert_fusion.1), channel_id=1, source_target_pairs={{0,64},{64,128},{128,192},{192,0},{1,65},{65,129},{129,193},{193,1... | collective-permute-start | bytes 884744 | tf_op jit(solution)/shard_map/y1_294kB/ppermute | solution.py:26
  143.0 13.0 %collective-permute-start.18 = (bf16[96,1536]{1,0:T(8,128)(2,1)S(1)}, bf16[96,1536]{1,0:T(8,128)(2,1)S(1)}, u32[]{:S(2)}, u32[]{:S(2)}) collective-permute-start(bf16[96,1536]{1,0:T(8,128)(2,1)S(1)} %get-tuple-element.54), channel_id=1, source_target_pairs={{0,64},{64,128},{128,192},{192,0},{1,65},{65,129},{129,193},{193,1... | collective-permute-start | bytes 884744 | tf_op jit(solution)/shard_map/y1_294kB/ppermute | solution.py:26
  146.8 9.2 %collective-permute-start.20 = (bf16[96,1536]{1,0:T(8,128)(2,1)S(1)}, bf16[96,1536]{1,0:T(8,128)(2,1)S(1)}, u32[]{:S(2)}, u32[]{:S(2)}) collective-permute-start(bf16[96,1536]{1,0:T(8,128)(2,1)S(1)} %add_convert_fusion), channel_id=1, source_target_pairs={{0,192},{64,0},{128,64},{192,128},{1,193},{65,1},{129,65},{193,129... | collective-permute-start | bytes 884744 | tf_op jit(solution)/shard_map/y-1_294kB/ppermute | solution.py:26
  153.9 2.2 %copy-start.12 = (f32[1,96,3072]{2,1,0:T(8,128)S(1)}, f32[1,96,3072]{2,1,0:T(8,128)}, u32[]{:S(2)}) copy-start(f32[1,96,3072]{2,1,0:T(8,128)} %param.7) | copy-start | bytes 3538948
Sparse Core Ops, SparseCore 0:
  9.1 44.5 all-gather.5
  55.5 34.3 all-gather.3
  94.4 40.9 all-gather.7

commit v5 on v4

--- a/solution.py
+++ b/solution.py
@@ -50,8 +50,10 @@
         copy.wait()
 
 
-def mine_kernel(place_ref, table_ref, held_ref, sent_ref, mine_ref, sems):
+def mine_kernel(place_ref, table_ref, held_ref, sent_ref, amps_ref, mine_ref, out_ref, sems):
     c = place_ref[2]
+    amps = pltpu.make_async_copy(amps_ref, out_ref, sems.at[NX])
+    amps.start()
     for k in range(NX):
         want = table_ref[k * NC + c]
         here = (want & 1) == c
@@ -66,6 +68,7 @@
 
     for k in range(NX):
         pltpu.make_async_copy(sent_ref.at[k], mine_ref.at[k], sems.at[k]).wait()
+    amps.wait()
 
 
 def choose(kernel, results, place, table, *arrays):
@@ -114,12 +117,11 @@
     )(block, other)
 
 
-def last_kernel(fore_ref, back_ref, late_ref, a_ref, b_ref, later_ref, sems):
+def last_kernel(fore_ref, back_ref, a_ref, b_ref, sems):
     h = a_ref.shape[1]
     copies = [
         pltpu.make_async_copy(fore_ref.at[:, pl.ds(0, h)], a_ref, sems.at[0]),
         pltpu.make_async_copy(back_ref.at[:, pl.ds(h, h)], b_ref, sems.at[1]),
-        pltpu.make_async_copy(late_ref, later_ref, sems.at[2]),
     ]
     for copy in copies:
         copy.start()
@@ -127,17 +129,17 @@
         copy.wait()
 
 
-def last_step(fore, back, late):
+def last_step(fore, back):
     rows, aux = fore.shape
     half = jax.ShapeDtypeStruct((rows, aux // 2), BF)
     return pl.pallas_call(
         last_kernel,
-        out_shape=[half, half, jax.ShapeDtypeStruct(late.shape, BF)],
-        in_specs=[ANY] * 3,
-        out_specs=[ANY] * 3,
-        scratch_shapes=[pltpu.SemaphoreType.DMA((3,))],
+        out_shape=[half, half],
+        in_specs=[ANY] * 2,
+        out_specs=[ANY] * 2,
+        scratch_shapes=[pltpu.SemaphoreType.DMA((2,))],
         compiler_params=params(2),
-    )(fore, back, late)
+    )(fore, back)
 
 
 def left_kernel(dist, place_ref, amps_ref, *refs):
@@ -261,7 +263,8 @@
     own = jnp.transpose(own.reshape(NX, third, NY, aux), (0, 2, 1, 3)).reshape(NX * NY, third, aux)
     held = lax.all_to_all(own, ("x", "y"), split_axis=0, concat_axis=0, tiled=True).reshape(NX, NY, third, aux)
     sent, by_z = choose(swap_kernel, (held, by_z), place, pair_table, held, by_z)
-    (mine,) = choose(mine_kernel, (held,), place, pair_table, held, shift(sent, "c", 1))
+    late = amps[:, early:]
+    mine, later = choose(mine_kernel, (held, late), place, pair_table, held, shift(sent, "c", 1), late)
     amps_j = lax.all_gather(by_z, "y", axis=0, tiled=True)
     parts = lax.all_to_all(mine, "x", split_axis=0, concat_axis=0, tiled=True)
     chosen = after(join(parts).reshape(rows, aux), amps_i0)
@@ -272,7 +275,7 @@
         fore, back = shift(fore, "z", 1), shift(back, "z", -1)
         dist += [-s, s]
         blocks += [fore, back]
-    far_a, far_b, later = last_step(fore, back, amps[:, early:])
+    far_a, far_b = last_step(fore, back)
     far_a, far_b = shift(far_a, "z", 1), shift(far_b, "z", -1)
     amps_i1 = lax.all_gather(later, "z", axis=0, tiled=True)
 
@@ -295,8 +298,13 @@
         compiler_params=params(8),
         cost_estimate=cost(6 * rows * aux * width),
     )(place, left, full, far_a, far_b, amps_i0)
-    total = [collect(own_a, two_a, three_a, one_a, 1), collect(own_b, two_b, one_b, three_b, -1)]
-    total = jnp.concatenate(total, axis=1)
+    relay_a, relay_b = shift(two_a, "y", 1), shift(two_b, "y", -1)
+    direct_a, direct_b = shift(three_a, "y", -1), shift(one_b, "y", 1)
+    direct = jnp.concatenate([direct_a, direct_b], axis=1).astype(F32)
+    relay_a = shift((one_a + relay_a.astype(F32)).astype(BF), "y", 1)
+    relay_b = shift((three_b + relay_b.astype(F32)).astype(BF), "y", -1)
+    own = jnp.concatenate([own_a, own_b], axis=1)
+    total = own + direct + jnp.concatenate([relay_a, relay_b], axis=1).astype(F32)
 
     own, one, two, three = out_products(place, total, amps_i0, 0, pairs, 1)
     outs = [collect(own, two, three, one, 1)]

time: 164 us -> 163 us (level)
  local copies, waits for them, and re-layouts: 14.7 us -> 12.8 us
    ppermute x21, waiting for transfers between devices: 51.3 us -> 47.2 us  [shift(): return lax.ppermute(block, axis, [(i, (i + step) % n) for i in range(n)])]
    all_to_all x1, waiting for transfers between devices: 5.37 us -> 7.71 us  [shards(): lax.all_to_all(own, ('x', 'y'), split_axis=0, concat_axis=0, tiled=True)]
    unnamed x28 -> x26, local copies, waits for them, and re-layouts: 7.02 us -> 7.47 us
  transfers between devices with their start and end apart: 25 -> 25, of which waited for: 12 -> 13; matrix products, arithmetic and copies ran while one was open for 5% -> 4% of each run, Pallas kernels for 9% -> 9%
where the time goes in v5:
time: 163 us
  waiting for transfers between devices  63 us (39%)
  starting transfers between devices  41.4 us (25%)
  Pallas kernels  14.7 us (9%)
  blocking collectives  13.7 us (8%)
  between operations  13.4 us (8%)
  local copies, waits for them, and re-layouts  12.8 us (8%)
  other arithmetic  3.6 us (2%)
    ppermute x21, waiting for transfers between devices, shift(): return lax.ppermute(block, axis, [(i, (i + step) % n) for i in range(n)])  47.2 us
    ppermute x21, starting transfers between devices, shift(): return lax.ppermute(block, axis, [(i, (i + step) % n) for i in range(n)])  33.9 us
    all_to_all x1, blocking collectives, shards(): parts = lax.all_to_all(mine, 'x', split_axis=0, concat_axis=0, tiled=True)  13.7 us
    all_to_all x1, waiting for transfers between devices, shards(): lax.all_to_all(own, ('x', 'y'), split_axis=0, concat_axis=0, tiled=True)  7.71 us
    all_to_all x1, starting transfers between devices, shards(): lax.all_to_all(own, ('x', 'y'), split_axis=0, concat_axis=0, tiled=True)  7.48 us
    unnamed x26, local copies, waits for them, and re-layouts  7.47 us
    all_gather x1, waiting for transfers between devices, shards(): amps_i0 = lax.all_gather(amps[:, :early], 'z', axis=0, tiled=True)  6.66 us
    pallas_call x2, Pallas kernels, out_products(): pl.pallas_call(functools.partial(out_kernel, pairs, first), out_shape=[ja...  3.9 us
  transfers between devices with their start and end apart: 25, of which 13 were waited for; matrix products, arithmetic and copies ran while one was open for 4% of the time, Pallas kernels for 9%

profile of v5, /device:TPU:2, one launch (start us, length us, event | category | flops | bytes accessed | tf_op | source)
XLA Modules:
  0.0 162.7 jit_solution(403189082624681532)
XLA Ops:
  6.5 1.9 %fusion.3 = (bf16[96,1536]{1,0:T(8,128)(2,1)}, bf16[96,1536]{1,0:T(8,128)(2,1)S(1)}) fusion(bf16[96,3072]{1,0:T(8,128)(2,1)} %bitcast.23), kind=kLoop, calls=%fused_computation.13 | loop fusion | bytes 1179648 | tf_op jit(solution)/shard_map/slice | solution.py:259
  8.9 0.9 copy.6
  9.8 7.5 %all-to-all-start = ((bf16[16,24,768]{2,1,0:T(8,128)(2,1)}), bf16[16,24,768]{2,1,0:T(8,128)(2,1)S(1)}, u32[]{:S(2)}, u32[]{:S(2)}) async-start(bf16[16,24,768]{2,1,0:T(8,128)(2,1)} %bitcast.6), calls=%async_computation | async-start | bytes 1179648 | tf_op jit(solution)/shard_map/all_to_all | solution.py:264
  17.3 0.8 reshape_squeeze.3
  18.5 1.1 reshape.47.amps_ref
  19.6 7.7 %all-to-all-done = bf16[16,24,768]{2,1,0:T(8,128)(2,1)S(1)} async-done(((bf16[16,24,768]{2,1,0:T(8,128)(2,1)}), bf16[16,24,768]{2,1,0:T(8,128)(2,1)S(1)}, u32[]{:S(2)}, u32[]{:S(2)}) %all-to-all-start) | async-done | bytes 589856 | tf_op jit(solution)/shard_map/all_to_all | solution.py:264
  27.3 1.4 shard_map.46
  28.9 2.0 %collective-permute-done.sent_ref = bf16[4,4,24,768]{3,2,1,0:T(8,128)(2,1)S(1)} collective-permute-done((bf16[4,4,24,768]{3,2,1,0:T(8,128)(2,1)S(1)}, bf16[4,4,24,768]{3,2,1,0:T(8,128)(2,1)S(1)}, u32[]{:S(2)}, u32[]{:S(2)}) %collective-permute-start) | collective-permute-done | bytes 589856 | tf_op jit(solution)/shard_map/c1_589kB/ppermute | solution.py:26
  30.9 1.4 shard_map.47
  32.3 13.7 %all_to_all.10.parts_ref = bf16[4,4,24,768]{3,2,1,0:T(8,128)(2,1)S(1)} all-to-all(bf16[4,4,24,768]{3,2,1,0:T(8,128)(2,1)S(1)} %get-tuple-element.34), channel_id=1, replica_groups=mesh['y'=4,'z'=8,'x'=4,'c'=2] {'x'}, dimensions={0} | all-to-all | bytes 1179648 | tf_op jit(solution)/shard_map/all_to_all | solution.py:269
  46.2 0.8 copy-done.1
  47.0 6.7 %all-gather.6.cloned.1.call-done.other_ref.amps_ref = bf16[768,1536]{1,0:T(8,128)(2,1)} async-done(((bf16[96,1536]{1,0:T(8,128)(2,1)}), bf16[768,1536]{1,0:T(8,128)(2,1)}) %all-gather.6.cloned.1.call-update) | async-done | bytes 2359312 | tf_op jit(solution)/shard_map/all_gather | solution.py:259
  53.7 1.1 collective-permute-start.1
  54.8 2.1 %collective-permute-start.2 = (bf16[384,768]{1,0:T(8,128)(2,1)}, bf16[384,768]{1,0:T(8,128)(2,1)S(1)}, u32[]{:S(2)}, u32[]{:S(2)}) collective-permute-start(bf16[384,768]{1,0:T(8,128)(2,1)} %shard_map.49.refs_0_), channel_id=1, source_target_pairs={{0,56},{8,0},{16,8},{24,16},{32,24},{40,32},{48,40},{56,48},{1,57}... | collective-permute-start | bytes 1769480 | tf_op jit(solution)/shard_map/z-1_589kB/ppermute | solution.py:26
  56.9 10.5 %collective-permute-done.1.refs_1_ = bf16[384,768]{1,0:T(8,128)(2,1)S(1)} collective-permute-done((bf16[384,768]{1,0:T(8,128)(2,1)}, bf16[384,768]{1,0:T(8,128)(2,1)S(1)}, u32[]{:S(2)}, u32[]{:S(2)}) %collective-permute-start.1) | collective-permute-done | bytes 589856 | tf_op jit(solution)/shard_map/z1_589kB/ppermute | solution.py:26
  67.5 3.1 %collective-permute-start.4 = (bf16[384,768]{1,0:T(8,128)(2,1)S(1)}, bf16[384,768]{1,0:T(8,128)(2,1)S(1)}, u32[]{:S(2)}, u32[]{:S(2)}) collective-permute-start(bf16[384,768]{1,0:T(8,128)(2,1)S(1)} %collective-permute-done.2.refs_2_), channel_id=1, source_target_pairs={{0,56},{8,0},{16,8},{24,16},{32,24},{40,32},{48,40},{56,48},{1,57}... | collective-permute-start | bytes 1769480 | tf_op jit(solution)/shard_map/z-1_589kB/ppermute | solution.py:26
  70.7 10.1 %collective-permute-done.3.refs_3_ = bf16[384,768]{1,0:T(8,128)(2,1)S(1)} collective-permute-done((bf16[384,768]{1,0:T(8,128)(2,1)S(1)}, bf16[384,768]{1,0:T(8,128)(2,1)S(1)}, u32[]{:S(2)}, u32[]{:S(2)}) %collective-permute-start.3) | collective-permute-done | bytes 589856 | tf_op jit(solution)/shard_map/z1_589kB/ppermute | solution.py:26
  80.9 3.1 %collective-permute-start.6 = (bf16[384,768]{1,0:T(8,128)(2,1)S(1)}, bf16[384,768]{1,0:T(8,128)(2,1)S(1)}, u32[]{:S(2)}, u32[]{:S(2)}) collective-permute-start(bf16[384,768]{1,0:T(8,128)(2,1)S(1)} %collective-permute-done.4.refs_4_), channel_id=1, source_target_pairs={{0,56},{8,0},{16,8},{24,16},{32,24},{40,32},{48,40},{56,48},{1,57}... | collective-permute-start | bytes 1769480 | tf_op jit(solution)/shard_map/z-1_589kB/ppermute | solution.py:26
  84.0 9.0 %collective-permute-done.5.refs_5_.fore_ref = bf16[384,768]{1,0:T(8,128)(2,1)S(1)} collective-permute-done((bf16[384,768]{1,0:T(8,128)(2,1)S(1)}, bf16[384,768]{1,0:T(8,128)(2,1)S(1)}, u32[]{:S(2)}, u32[]{:S(2)}) %collective-permute-start.5) | collective-permute-done | bytes 589856 | tf_op jit(solution)/shard_map/z1_589kB/ppermute | solution.py:26
  93.1 0.8 shard_map.51
  94.5 2.7 %collective-permute-start.8 = (bf16[384,384]{1,0:T(8,128)(2,1)}, bf16[384,384]{1,0:T(8,128)(2,1)S(1)}, u32[]{:S(2)}, u32[]{:S(2)}) collective-permute-start(bf16[384,384]{1,0:T(8,128)(2,1)} %get-tuple-element.39), channel_id=1, source_target_pairs={{0,56},{8,0},{16,8},{24,16},{32,24},{40,32},{48,40},{56,48},{1,57}... | collective-permute-start | bytes 884744 | tf_op jit(solution)/shard_map/z-1_294kB/ppermute | solution.py:26
  97.2 1.7 %copy-done.3 = bf16[384,3072]{1,0:T(8,128)(2,1)S(1)} copy-done((bf16[384,3072]{1,0:T(8,128)(2,1)S(1)}, bf16[384,3072]{1,0:T(8,128)(2,1)}, u32[]{:S(2)}) %copy-start.3) | copy-done | bytes 2359320
  98.9 1.1 copy-done.6
  100.0 1.1 copy-done.8
  101.0 3.0 %shard_map.50 = (f32[384,768]{1,0:T(8,128)S(1)}, bf16[8,384,768]{2,1,0:T(8,128)(2,1)S(1)}, bf16[384,384]{1,0:T(8,128)(2,1)S(1)}) custom-call(s32[3]{0:T(128)S(1)} %pad_add_fusion.place_ref, bf16[384,3072]{1,0:T(8,128)(2,1)S(1)} %copy-done.3, bf16[384,768]{1,0:T(8,128)(2,1)S(1)} %copy-done.2, bf16[384,768]{1,0:T(8,128)(2,1)S(1)} %collective-permute-done.1.refs_1_, ...), custom_call_target="tpu_custom_call" | custom-call | flops 1585446912 | bytes 8388608 | tf_op jit(solution)/shard_map/pallas_call | solution.py:167
  104.0 1.7 %shard_map.52 = (bf16[384,768]{1,0:T(8,128)(2,1)S(1)}, bf16[384,384]{1,0:T(8,128)(2,1)S(1)}, bf16[384,384]{1,0:T(8,128)(2,1)S(1)}) custom-call(s32[3]{0:T(128)S(1)} %pad_add_fusion.place_ref, bf16[384,384]{1,0:T(8,128)(2,1)S(1)} %get-tuple-element.35.amps_ref, f32[384,768]{1,0:T(8,128)S(1)} %get-tuple-element.36.acc_ref, ...), custom_call_target="tpu_custom_call" | custom-call | flops 679477248 | bytes 8388608 | tf_op jit(solution)/shard_map/pallas_call | solution.py:284
  105.7 1.9 %collective-permute-start.11 = (bf16[384,384]{1,0:T(8,128)(2,1)S(1)}, bf16[384,384]{1,0:T(8,128)(2,1)S(1)}, u32[]{:S(2)}, u32[]{:S(2)}) collective-permute-start(bf16[384,384]{1,0:T(8,128)(2,1)S(1)} %get-tuple-element.46), channel_id=1, source_target_pairs={{0,64},{64,128},{128,192},{192,0},{1,65},{65,129},{129,193},{193,1... | collective-permute-start | bytes 884744 | tf_op jit(solution)/shard_map/y1_294kB/ppermute | solution.py:26
  107.6 1.4 collective-permute-start.13
  109.1 2.3 %shard_map.53 = (f32[384,384]{1,0:T(8,128)S(1)}, bf16[384,384]{1,0:T(8,128)(2,1)S(1)}, bf16[384,384]{1,0:T(8,128)(2,1)S(1)}, f32[384,384]{1,0:T(8,128)S(1)}, f32...) custom-call(s32[3]{0:T(128)S(1)} %pad_add_fusion.place_ref, ...), custom_call_target="tpu_custom_call" | custom-call | flops 1358954496 | bytes 8388608 | tf_op jit(solution)/shard_map/pallas_call | solution.py:292
  111.4 0.7 collective-permute-start.10
  112.0 2.7 %collective-permute-start.9 = (bf16[384,384]{1,0:T(8,128)(2,1)S(1)}, bf16[384,384]{1,0:T(8,128)(2,1)S(1)}, u32[]{:S(2)}, u32[]{:S(2)}) collective-permute-start(bf16[384,384]{1,0:T(8,128)(2,1)S(1)} %get-tuple-element.43), channel_id=1, source_target_pairs={{0,192},{64,0},{128,64},{192,128},{1,193},{65,1},{129,65},{193,129... | collective-permute-start | bytes 884744 | tf_op jit(solution)/shard_map/y-1_294kB/ppermute | solution.py:26
  114.7 2.3 %collective-permute-done.11 = bf16[384,384]{1,0:T(8,128)(2,1)S(1)} collective-permute-done((bf16[384,384]{1,0:T(8,128)(2,1)S(1)}, bf16[384,384]{1,0:T(8,128)(2,1)S(1)}, u32[]{:S(2)}, u32[]{:S(2)}) %collective-permute-start.11) | collective-permute-done | bytes 294944 | tf_op jit(solution)/shard_map/y1_294kB/ppermute | solution.py:26
  117.2 3.3 %collective-permute-start.14 = (bf16[384,384]{1,0:T(8,128)(2,1)S(1)}, bf16[384,384]{1,0:T(8,128)(2,1)S(1)}, u32[]{:S(2)}, u32[]{:S(2)}) collective-permute-start(bf16[384,384]{1,0:T(8,128)(2,1)S(1)} %add_convert_fusion.2), channel_id=1, source_target_pairs={{0,192},{64,0},{128,64},{192,128},{1,193},{65,1},{129,65},{193,129... | collective-permute-start | bytes 884744 | tf_op jit(solution)/shard_map/y-1_294kB/ppermute | solution.py:26
  120.7 5.0 %collective-permute-done.12 = bf16[384,384]{1,0:T(8,128)(2,1)S(1)} collective-permute-done((bf16[384,384]{1,0:T(8,128)(2,1)S(1)}, bf16[384,384]{1,0:T(8,128)(2,1)S(1)}, u32[]{:S(2)}, u32[]{:S(2)}) %collective-permute-start.12) | collective-permute-done | bytes 294944 | tf_op jit(solution)/shard_map/y1_294kB/ppermute | solution.py:26
  126.0 2.0 %shard_map.54 = (f32[96,1536]{1,0:T(8,128)S(1)}, f32[96,1536]{1,0:T(8,128)S(1)}, bf16[96,1536]{1,0:T(8,128)(2,1)S(1)}, bf16[96,1536]{1,0:T(8,128)(2,1)S(1)}) custom-call(s32[3]{0:T(128)S(1)} %pad_add_fusion.place_ref, f32[384,768]{1,0:T(8,128)S(1)} %fusion.total_ref, bf16[768,1536]{1,0:T(8,128)(2,1)S(1)} %get-tuple-element.49.amps_ref), custom_call_target="tpu_custom_call" | custom-call | flops 905969664 | bytes 8388608 | tf_op jit(solution)/shard_map/pallas_call | solution.py:229
  128.0 4.0 %collective-permute-start.15 = (bf16[96,1536]{1,0:T(8,128)(2,1)S(1)}, bf16[96,1536]{1,0:T(8,128)(2,1)}, u32[]{:S(2)}, u32[]{:S(2)}) collective-permute-start(bf16[96,1536]{1,0:T(8,128)(2,1)S(1)} %get-tuple-element.51), channel_id=1, source_target_pairs={{0,192},{64,0},{128,64},{192,128},{1,193},{65,1},{129,65},{193,129... | collective-permute-start | bytes 884744 | tf_op jit(solution)/shard_map/y-1_294kB/ppermute | solution.py:26
  132.0 1.4 all-gather.8.cloned.1.call-done.amps_ref
  133.5 1.7 %copy-done.4 = bf16[768,1536]{1,0:T(8,128)(2,1)S(1)} copy-done((bf16[768,1536]{1,0:T(8,128)(2,1)S(1)}, bf16[768,1536]{1,0:T(8,128)(2,1)}, u32[]{:S(2)}) %copy-start.4) | copy-done | bytes 2359320
  135.1 1.9 %shard_map.55 = (f32[96,1536]{1,0:T(8,128)S(1)}, bf16[96,1536]{1,0:T(8,128)(2,1)S(1)}, bf16[96,1536]{1,0:T(8,128)(2,1)S(1)}, f32[96,1536]{1,0:T(8,128)S(1)}) custom-call(s32[3]{0:T(128)S(1)} %pad_add_fusion.place_ref, f32[384,768]{1,0:T(8,128)S(1)} %fusion.total_ref, bf16[768,1536]{1,0:T(8,128)(2,1)S(1)} %copy-done.4), custom_call_target="tpu_custom_call" | custom-call | flops 905969664 | bytes 8388608 | tf_op jit(solution)/shard_map/pallas_call | solution.py:229
  137.1 2.7 %collective-permute-start.19 = (bf16[96,1536]{1,0:T(8,128)(2,1)S(1)}, bf16[96,1536]{1,0:T(8,128)(2,1)S(1)}, u32[]{:S(2)}, u32[]{:S(2)}) collective-permute-start(bf16[96,1536]{1,0:T(8,128)(2,1)S(1)} %get-tuple-element.58), channel_id=1, source_target_pairs={{0,192},{64,0},{128,64},{192,128},{1,193},{65,1},{129,65},{193,129... | collective-permute-start | bytes 884744 | tf_op jit(solution)/shard_map/y-1_294kB/ppermute | solution.py:26
  139.8 1.0 add_convert_fusion.1
  140.8 0.8 collective-permute-start.17
  141.6 3.3 %collective-permute-done.19 = bf16[96,1536]{1,0:T(8,128)(2,1)S(1)} collective-permute-done((bf16[96,1536]{1,0:T(8,128)(2,1)S(1)}, bf16[96,1536]{1,0:T(8,128)(2,1)S(1)}, u32[]{:S(2)}, u32[]{:S(2)}) %collective-permute-start.19) | collective-permute-done | bytes 294944 | tf_op jit(solution)/shard_map/y-1_294kB/ppermute | solution.py:26
  145.0 3.2 %collective-permute-start.20 = (bf16[96,1536]{1,0:T(8,128)(2,1)S(1)}, bf16[96,1536]{1,0:T(8,128)(2,1)S(1)}, u32[]{:S(2)}, u32[]{:S(2)}) collective-permute-start(bf16[96,1536]{1,0:T(8,128)(2,1)S(1)} %add_convert_fusion), channel_id=1, source_target_pairs={{0,192},{64,0},{128,64},{192,128},{1,193},{65,1},{129,65},{193,129... | collective-permute-start | bytes 884744 | tf_op jit(solution)/shard_map/y-1_294kB/ppermute | solution.py:26
  148.1 4.7 %collective-permute-done.17 = bf16[96,1536]{1,0:T(8,128)(2,1)S(1)} collective-permute-done((bf16[96,1536]{1,0:T(8,128)(2,1)S(1)}, bf16[96,1536]{1,0:T(8,128)(2,1)S(1)}, u32[]{:S(2)}, u32[]{:S(2)}) %collective-permute-start.17) | collective-permute-done | bytes 294944 | tf_op jit(solution)/shard_map/y1_294kB/ppermute | solution.py:26
  152.8 1.0 add_bitcast_fusion.1
  154.0 1.1 copy-done.11
  155.1 1.0 fusion.2
  (58 shorter events, 3.1 us)
Async XLA Ops:
  6.5 1.9 %copy-start.12 = (bf16[1,3000,96]{1,2,0:T(8,128)(2,1)S(1)}, bf16[1,3000,96]{1,2,0:T(8,128)(2,1)}, u32[]{:S(2)}) copy-start(bf16[1,3000,96]{1,2,0:T(8,128)(2,1)} %param.5) | copy-start | bytes 1728004
  6.5 47.2 %all-gather.6.cloned.1.call-start = ((), (), s32[]{:S(2)}) async-start(), calls=%async_computation.3 | async-start | bytes 2654208 | tf_op jit(solution)/shard_map/all_gather | solution.py:259
  8.9 8.4 %copy-start.10 = (bf16[1,96,3072]{2,1,0:T(8,128)(2,1)S(1)}, bf16[1,96,3072]{2,1,0:T(8,128)(2,1)}, u32[]{:S(2)}) copy-start(bf16[1,96,3072]{2,1,0:T(8,128)(2,1)} %param.6) | copy-start | bytes 1769476
  9.8 17.5 %all-to-all-start = ((bf16[16,24,768]{2,1,0:T(8,128)(2,1)}), bf16[16,24,768]{2,1,0:T(8,128)(2,1)S(1)}, u32[]{:S(2)}, u32[]{:S(2)}) async-start(bf16[16,24,768]{2,1,0:T(8,128)(2,1)} %bitcast.6), calls=%async_computation | async-start | bytes 1179648 | tf_op jit(solution)/shard_map/all_to_all | solution.py:264
  17.3 79.9 %all-gather.4.cloned.1.call-start = ((), (), s32[]{:S(2)}) async-start(), calls=%async_computation.2 | async-start | bytes 2949120 | tf_op jit(solution)/shard_map/all_gather | solution.py:268
  18.1 9.2 %copy-start.9 = (s32[8]{0:T(128)S(1)}, s32[8]{0:T(128)}, u32[]{:S(2)}) copy-start(s32[8]{0:T(128)} %table_ref.3) | copy-start | bytes 100
  28.8 104.7 %all-gather.8.cloned.1.call-start = ((), (), s32[]{:S(2)}) async-start(), calls=%async_computation.4 | async-start | bytes 2654208 | tf_op jit(solution)/shard_map/all_gather | solution.py:280
  28.8 2.1 %collective-permute-start = (bf16[4,4,24,768]{3,2,1,0:T(8,128)(2,1)S(1)}, bf16[4,4,24,768]{3,2,1,0:T(8,128)(2,1)S(1)}, u32[]{:S(2)}, u32[]{:S(2)}) collective-permute-start(bf16[4,4,24,768]{3,2,1,0:T(8,128)(2,1)S(1)} %get-tuple-element.33), channel_id=1, source_target_pairs={{0,1},{1,0},{2,3},{3,2},{4,5},{5,4},{6,7},{7,6},{8,9},{9,8},{10,11... | collective-permute-start | bytes 1769480 | tf_op jit(solution)/shard_map/c1_589kB/ppermute | solution.py:26
  46.2 0.8 copy-start.1
  53.7 43.5 %copy-start.2 = (bf16[384,768]{1,0:T(8,128)(2,1)S(1)}, bf16[384,768]{1,0:T(8,128)(2,1)}, u32[]{:S(2)}) copy-start(bf16[384,768]{1,0:T(8,128)(2,1)} %shard_map.49.refs_0_) | copy-start | bytes 1769476
  53.7 13.7 %collective-permute-start.1 = (bf16[384,768]{1,0:T(8,128)(2,1)}, bf16[384,768]{1,0:T(8,128)(2,1)S(1)}, u32[]{:S(2)}, u32[]{:S(2)}) collective-permute-start(bf16[384,768]{1,0:T(8,128)(2,1)} %shard_map.49.refs_0_), channel_id=1, source_target_pairs={{0,8},{8,16},{16,24},{24,32},{32,40},{40,48},{48,56},{56,0},{1,9},... | collective-permute-start | bytes 1769480 | tf_op jit(solution)/shard_map/z1_589kB/ppermute | solution.py:26
  54.8 12.7 %collective-permute-start.2 = (bf16[384,768]{1,0:T(8,128)(2,1)}, bf16[384,768]{1,0:T(8,128)(2,1)S(1)}, u32[]{:S(2)}, u32[]{:S(2)}) collective-permute-start(bf16[384,768]{1,0:T(8,128)(2,1)} %shard_map.49.refs_0_), channel_id=1, source_target_pairs={{0,56},{8,0},{16,8},{24,16},{32,24},{40,32},{48,40},{56,48},{1,57}... | collective-permute-start | bytes 1769480 | tf_op jit(solution)/shard_map/z-1_589kB/ppermute | solution.py:26
  67.4 13.4 %collective-permute-start.3 = (bf16[384,768]{1,0:T(8,128)(2,1)S(1)}, bf16[384,768]{1,0:T(8,128)(2,1)S(1)}, u32[]{:S(2)}, u32[]{:S(2)}) collective-permute-start(bf16[384,768]{1,0:T(8,128)(2,1)S(1)} %collective-permute-done.1.refs_1_), channel_id=1, source_target_pairs={{0,8},{8,16},{16,24},{24,32},{32,40},{40,48},{48,56},{56,0},{1,9},... | collective-permute-start | bytes 1769480 | tf_op jit(solution)/shard_map/z1_589kB/ppermute | solution.py:26
  67.5 13.4 %collective-permute-start.4 = (bf16[384,768]{1,0:T(8,128)(2,1)S(1)}, bf16[384,768]{1,0:T(8,128)(2,1)S(1)}, u32[]{:S(2)}, u32[]{:S(2)}) collective-permute-start(bf16[384,768]{1,0:T(8,128)(2,1)S(1)} %collective-permute-done.2.refs_2_), channel_id=1, source_target_pairs={{0,56},{8,0},{16,8},{24,16},{32,24},{40,32},{48,40},{56,48},{1,57}... | collective-permute-start | bytes 1769480 | tf_op jit(solution)/shard_map/z-1_589kB/ppermute | solution.py:26
  80.8 13.1 %copy-start.5 = (bf16[384,768]{1,0:T(8,128)(2,1)}, bf16[384,768]{1,0:T(8,128)(2,1)S(1)}, u32[]{:S(2)}) copy-start(bf16[384,768]{1,0:T(8,128)(2,1)S(1)} %collective-permute-done.3.refs_3_) | copy-start | bytes 1769476
  80.8 12.3 %collective-permute-start.5 = (bf16[384,768]{1,0:T(8,128)(2,1)S(1)}, bf16[384,768]{1,0:T(8,128)(2,1)S(1)}, u32[]{:S(2)}, u32[]{:S(2)}) collective-permute-start(bf16[384,768]{1,0:T(8,128)(2,1)S(1)} %collective-permute-done.3.refs_3_), channel_id=1, source_target_pairs={{0,8},{8,16},{16,24},{24,32},{32,40},{40,48},{48,56},{56,0},{1,9},... | collective-permute-start | bytes 1769480 | tf_op jit(solution)/shard_map/z1_589kB/ppermute | solution.py:26
  80.9 13.6 %copy-start.7 = (bf16[384,768]{1,0:T(8,128)(2,1)}, bf16[384,768]{1,0:T(8,128)(2,1)S(1)}, u32[]{:S(2)}) copy-start(bf16[384,768]{1,0:T(8,128)(2,1)S(1)} %collective-permute-done.4.refs_4_) | copy-start | bytes 1769476
  80.9 12.1 %collective-permute-start.6 = (bf16[384,768]{1,0:T(8,128)(2,1)S(1)}, bf16[384,768]{1,0:T(8,128)(2,1)S(1)}, u32[]{:S(2)}, u32[]{:S(2)}) collective-permute-start(bf16[384,768]{1,0:T(8,128)(2,1)S(1)} %collective-permute-done.4.refs_4_), channel_id=1, source_target_pairs={{0,56},{8,0},{16,8},{24,16},{32,24},{40,32},{48,40},{56,48},{1,57}... | collective-permute-start | bytes 1769480 | tf_op jit(solution)/shard_map/z-1_589kB/ppermute | solution.py:26
  93.9 10.1 %collective-permute-start.7 = (bf16[384,384]{1,0:T(8,128)(2,1)}, bf16[384,384]{1,0:T(8,128)(2,1)S(1)}, u32[]{:S(2)}, u32[]{:S(2)}) collective-permute-start(bf16[384,384]{1,0:T(8,128)(2,1)} %get-tuple-element.38), channel_id=1, source_target_pairs={{0,8},{8,16},{16,24},{24,32},{32,40},{40,48},{48,56},{56,0},{1,9},... | collective-permute-start | bytes 884744 | tf_op jit(solution)/shard_map/z1_294kB/ppermute | solution.py:26
  94.5 9.5 %collective-permute-start.8 = (bf16[384,384]{1,0:T(8,128)(2,1)}, bf16[384,384]{1,0:T(8,128)(2,1)S(1)}, u32[]{:S(2)}, u32[]{:S(2)}) collective-permute-start(bf16[384,384]{1,0:T(8,128)(2,1)} %get-tuple-element.39), channel_id=1, source_target_pairs={{0,56},{8,0},{16,8},{24,16},{32,24},{40,32},{48,40},{56,48},{1,57}... | collective-permute-start | bytes 884744 | tf_op jit(solution)/shard_map/z-1_294kB/ppermute | solution.py:26
  97.2 1.7 %copy-start.3 = (bf16[384,3072]{1,0:T(8,128)(2,1)S(1)}, bf16[384,3072]{1,0:T(8,128)(2,1)}, u32[]{:S(2)}) copy-start(bf16[384,3072]{1,0:T(8,128)(2,1)} %all-gather.4.cloned.1.call-done.amps_ref) | copy-start | bytes 7077892
  98.9 1.1 copy-start.6
  100.0 1.1 copy-start.8
  104.0 5.0 %copy-start = (bf16[768,1536]{1,0:T(8,128)(2,1)S(1)}, bf16[768,1536]{1,0:T(8,128)(2,1)}, u32[]{:S(2)}) copy-start(bf16[768,1536]{1,0:T(8,128)(2,1)} %all-gather.6.cloned.1.call-done.other_ref.amps_ref) | copy-start | bytes 7077892
  105.7 11.2 %collective-permute-start.11 = (bf16[384,384]{1,0:T(8,128)(2,1)S(1)}, bf16[384,384]{1,0:T(8,128)(2,1)S(1)}, u32[]{:S(2)}, u32[]{:S(2)}) collective-permute-start(bf16[384,384]{1,0:T(8,128)(2,1)S(1)} %get-tuple-element.46), channel_id=1, source_target_pairs={{0,64},{64,128},{128,192},{192,0},{1,65},{65,129},{129,193},{193,1... | collective-permute-start | bytes 884744 | tf_op jit(solution)/shard_map/y1_294kB/ppermute | solution.py:26
  107.6 9.5 %collective-permute-start.13 = (bf16[384,384]{1,0:T(8,128)(2,1)S(1)}, bf16[384,384]{1,0:T(8,128)(2,1)S(1)}, u32[]{:S(2)}, u32[]{:S(2)}) collective-permute-start(bf16[384,384]{1,0:T(8,128)(2,1)S(1)} %get-tuple-element.48), channel_id=1, source_target_pairs={{0,192},{64,0},{128,64},{192,128},{1,193},{65,1},{129,65},{193,129... | collective-permute-start | bytes 884744 | tf_op jit(solution)/shard_map/y-1_294kB/ppermute | solution.py:26
  111.4 9.3 %collective-permute-start.10 = (bf16[384,384]{1,0:T(8,128)(2,1)S(1)}, bf16[384,384]{1,0:T(8,128)(2,1)S(1)}, u32[]{:S(2)}, u32[]{:S(2)}) collective-permute-start(bf16[384,384]{1,0:T(8,128)(2,1)S(1)} %get-tuple-element.44), channel_id=1, source_target_pairs={{0,64},{64,128},{128,192},{192,0},{1,65},{65,129},{129,193},{193,1... | collective-permute-start | bytes 884744 | tf_op jit(solution)/shard_map/y1_294kB/ppermute | solution.py:26
  112.0 8.7 %collective-permute-start.9 = (bf16[384,384]{1,0:T(8,128)(2,1)S(1)}, bf16[384,384]{1,0:T(8,128)(2,1)S(1)}, u32[]{:S(2)}, u32[]{:S(2)}) collective-permute-start(bf16[384,384]{1,0:T(8,128)(2,1)S(1)} %get-tuple-element.43), channel_id=1, source_target_pairs={{0,192},{64,0},{128,64},{192,128},{1,193},{65,1},{129,65},{193,129... | collective-permute-start | bytes 884744 | tf_op jit(solution)/shard_map/y-1_294kB/ppermute | solution.py:26
  117.0 8.7 %collective-permute-start.12 = (bf16[384,384]{1,0:T(8,128)(2,1)S(1)}, bf16[384,384]{1,0:T(8,128)(2,1)S(1)}, u32[]{:S(2)}, u32[]{:S(2)}) collective-permute-start(bf16[384,384]{1,0:T(8,128)(2,1)S(1)} %add_convert_fusion.3), channel_id=1, source_target_pairs={{0,64},{64,128},{128,192},{192,0},{1,65},{65,129},{129,193},{193,1... | collective-permute-start | bytes 884744 | tf_op jit(solution)/shard_map/y1_294kB/ppermute | solution.py:26
  117.2 8.6 %collective-permute-start.14 = (bf16[384,384]{1,0:T(8,128)(2,1)S(1)}, bf16[384,384]{1,0:T(8,128)(2,1)S(1)}, u32[]{:S(2)}, u32[]{:S(2)}) collective-permute-start(bf16[384,384]{1,0:T(8,128)(2,1)S(1)} %add_convert_fusion.2), channel_id=1, source_target_pairs={{0,192},{64,0},{128,64},{192,128},{1,193},{65,1},{129,65},{193,129... | collective-permute-start | bytes 884744 | tf_op jit(solution)/shard_map/y-1_294kB/ppermute | solution.py:26
  128.0 11.8 %collective-permute-start.16 = (bf16[96,1536]{1,0:T(8,128)(2,1)S(1)}, bf16[96,1536]{1,0:T(8,128)(2,1)}, u32[]{:S(2)}, u32[]{:S(2)}) collective-permute-start(bf16[96,1536]{1,0:T(8,128)(2,1)S(1)} %get-tuple-element.53), channel_id=1, source_target_pairs={{0,64},{64,128},{128,192},{192,0},{1,65},{65,129},{129,193},{193,1... | collective-permute-start | bytes 884744 | tf_op jit(solution)/shard_map/y1_294kB/ppermute | solution.py:26
  128.0 20.1 %collective-permute-start.15 = (bf16[96,1536]{1,0:T(8,128)(2,1)S(1)}, bf16[96,1536]{1,0:T(8,128)(2,1)}, u32[]{:S(2)}, u32[]{:S(2)}) collective-permute-start(bf16[96,1536]{1,0:T(8,128)(2,1)S(1)} %get-tuple-element.51), channel_id=1, source_target_pairs={{0,192},{64,0},{128,64},{192,128},{1,193},{65,1},{129,65},{193,129... | collective-permute-start | bytes 884744 | tf_op jit(solution)/shard_map/y-1_294kB/ppermute | solution.py:26
  133.5 1.7 %copy-start.4 = (bf16[768,1536]{1,0:T(8,128)(2,1)S(1)}, bf16[768,1536]{1,0:T(8,128)(2,1)}, u32[]{:S(2)}) copy-start(bf16[768,1536]{1,0:T(8,128)(2,1)} %all-gather.8.cloned.1.call-done.amps_ref) | copy-start | bytes 7077892
  137.1 7.8 %collective-permute-start.19 = (bf16[96,1536]{1,0:T(8,128)(2,1)S(1)}, bf16[96,1536]{1,0:T(8,128)(2,1)S(1)}, u32[]{:S(2)}, u32[]{:S(2)}) collective-permute-start(bf16[96,1536]{1,0:T(8,128)(2,1)S(1)} %get-tuple-element.58), channel_id=1, source_target_pairs={{0,192},{64,0},{128,64},{192,128},{1,193},{65,1},{129,65},{193,129... | collective-permute-start | bytes 884744 | tf_op jit(solution)/shard_map/y-1_294kB/ppermute | solution.py:26
  139.8 14.1 %collective-permute-start.18 = (bf16[96,1536]{1,0:T(8,128)(2,1)S(1)}, bf16[96,1536]{1,0:T(8,128)(2,1)S(1)}, u32[]{:S(2)}, u32[]{:S(2)}) collective-permute-start(bf16[96,1536]{1,0:T(8,128)(2,1)S(1)} %get-tuple-element.56), channel_id=1, source_target_pairs={{0,64},{64,128},{128,192},{192,0},{1,65},{65,129},{129,193},{193,1... | collective-permute-start | bytes 884744 | tf_op jit(solution)/shard_map/y1_294kB/ppermute | solution.py:26
  140.8 12.0 %collective-permute-start.17 = (bf16[96,1536]{1,0:T(8,128)(2,1)S(1)}, bf16[96,1536]{1,0:T(8,128)(2,1)S(1)}, u32[]{:S(2)}, u32[]{:S(2)}) collective-permute-start(bf16[96,1536]{1,0:T(8,128)(2,1)S(1)} %add_convert_fusion.1), channel_id=1, source_target_pairs={{0,64},{64,128},{128,192},{192,0},{1,65},{65,129},{129,193},{193,1... | collective-permute-start | bytes 884744 | tf_op jit(solution)/shard_map/y1_294kB/ppermute | solution.py:26
  145.0 8.9 %collective-permute-start.20 = (bf16[96,1536]{1,0:T(8,128)(2,1)S(1)}, bf16[96,1536]{1,0:T(8,128)(2,1)S(1)}, u32[]{:S(2)}, u32[]{:S(2)}) collective-permute-start(bf16[96,1536]{1,0:T(8,128)(2,1)S(1)} %add_convert_fusion), channel_id=1, source_target_pairs={{0,192},{64,0},{128,64},{192,128},{1,193},{65,1},{129,65},{193,129... | collective-permute-start | bytes 884744 | tf_op jit(solution)/shard_map/y-1_294kB/ppermute | solution.py:26
  153.9 1.3 copy-start.11
Sparse Core Ops, SparseCore 0:
  9.1 44.5 all-gather.5
  55.5 34.3 all-gather.3
  91.7 41.7 all-gather.7

commit v6 on v5

--- a/solution.py
+++ b/solution.py
@@ -238,11 +238,6 @@
         compiler_params=params(10),
         cost_estimate=cost(2 * total.size * cols),
     )(place, total, amps_i)
-
-
-def collect(own, two, direct, kept, step):
-    relay = (kept + shift(two, "y", step).astype(F32)).astype(BF)
-    return own + shift(direct, "y", -step).astype(F32) + shift(relay, "y", step).astype(F32)
 
 
 def shards(pair_table, cholesky, amplitudes, denominators):
@@ -306,11 +301,16 @@
     own = jnp.concatenate([own_a, own_b], axis=1)
     total = own + direct + jnp.concatenate([relay_a, relay_b], axis=1).astype(F32)
 
-    own, one, two, three = out_products(place, total, amps_i0, 0, pairs, 1)
-    outs = [collect(own, two, three, one, 1)]
-    own, one, two, three = out_products(place, total, amps_i1, early, pairs, 3)
-    outs.append(collect(own, two, one, three, -1))
-    return (-jnp.concatenate(outs, axis=1) / denominators[0]).astype(BF)[None]
+    own_a, one_a, two_a, three_a = out_products(place, total, amps_i0, 0, pairs, 1)
+    relay_a, direct_a = shift(two_a, "y", 1), shift(three_a, "y", -1)
+    own_b, one_b, two_b, three_b = out_products(place, total, amps_i1, early, pairs, 3)
+    relay_b, direct_b = shift(two_b, "y", -1), shift(one_b, "y", 1)
+    own = jnp.concatenate([own_a, own_b], axis=1)
+    direct = jnp.concatenate([direct_a, direct_b], axis=1).astype(F32)
+    relay_a = shift((one_a + relay_a.astype(F32)).astype(BF), "y", 1)
+    relay_b = shift((three_b + relay_b.astype(F32)).astype(BF), "y", -1)
+    out = own + direct + jnp.concatenate([relay_a, relay_b], axis=1).astype(F32)
+    return (-out / denominators[0]).astype(BF)[None]
 
 
 def solution(mesh):

time: 163 us -> 165 us (1.012)
  waiting for transfers between devices: 63 us -> 69 us
  other arithmetic: 3.6 us -> 1.59 us
  starting transfers between devices: 41.4 us -> 39.6 us
    all_gather x1, waiting for transfers between devices: 1.44 us -> 5.47 us  [shards(): amps_i1 = lax.all_gather(later, 'z', axis=0, tiled=True)]
    ppermute x21, waiting for transfers between devices: 47.2 us -> 49.1 us  [shift(): return lax.ppermute(block, axis, [(i, (i + step) % n) for i in range(n)])]
    ppermute x21, starting transfers between devices: 33.9 us -> 32 us  [shift(): return lax.ppermute(block, axis, [(i, (i + step) % n) for i in range(n)])]
  transfers between devices with their start and end apart: 25 -> 25, of which waited for: 13 -> 14; matrix products, arithmetic and copies ran while one was open for 4% -> 2% of each run, Pallas kernels for 9% -> 9%
where the time goes in v6:
time: 165 us; the launch traced here: 164 us
  waiting for transfers between devices  69 us (42%)
  starting transfers between devices  39.6 us (24%)
  Pallas kernels  14.7 us (9%)
  blocking collectives  13.7 us (8%)
  between operations  13.4 us (8%)
  local copies, waits for them, and re-layouts  11.7 us (7%)
    ppermute x21, waiting for transfers between devices, shift(): return lax.ppermute(block, axis, [(i, (i + step) % n) for i in range(n)])  49.1 us
    ppermute x21, starting transfers between devices, shift(): return lax.ppermute(block, axis, [(i, (i + step) % n) for i in range(n)])  32 us
    all_to_all x1, blocking collectives, shards(): parts = lax.all_to_all(mine, 'x', split_axis=0, concat_axis=0, tiled=True)  13.7 us
    all_to_all x1, waiting for transfers between devices, shards(): lax.all_to_all(own, ('x', 'y'), split_axis=0, concat_axis=0, tiled=True)  7.71 us
    all_to_all x1, starting transfers between devices, shards(): lax.all_to_all(own, ('x', 'y'), split_axis=0, concat_axis=0, tiled=True)  7.48 us
    all_gather x1, waiting for transfers between devices, shards(): amps_i0 = lax.all_gather(amps[:, :early], 'z', axis=0, tiled=True)  6.67 us
    unnamed x26, local copies, waits for them, and re-layouts  6.32 us
    all_gather x1, waiting for transfers between devices, shards(): amps_i1 = lax.all_gather(later, 'z', axis=0, tiled=True)  5.47 us
  transfers between devices with their start and end apart: 25, of which 14 were waited for; matrix products, arithmetic and copies ran while one was open for 2% of the time, Pallas kernels for 9%

profile of v6, /device:TPU:2, one launch (start us, length us, event | category | flops | bytes accessed | tf_op | source)
XLA Modules:
  0.0 163.6 jit_solution(8086394897826920441)
XLA Ops:
  6.5 1.9 %fusion.5 = (bf16[96,1536]{1,0:T(8,128)(2,1)}, bf16[96,1536]{1,0:T(8,128)(2,1)S(1)}) fusion(bf16[96,3072]{1,0:T(8,128)(2,1)} %bitcast.27), kind=kLoop, calls=%fused_computation.13 | loop fusion | bytes 1179648 | tf_op jit(solution)/shard_map/slice | solution.py:254
  8.9 0.9 copy.6
  9.8 7.5 %all-to-all-start = ((bf16[16,24,768]{2,1,0:T(8,128)(2,1)}), bf16[16,24,768]{2,1,0:T(8,128)(2,1)S(1)}, u32[]{:S(2)}, u32[]{:S(2)}) async-start(bf16[16,24,768]{2,1,0:T(8,128)(2,1)} %bitcast.6), calls=%async_computation | async-start | bytes 1179648 | tf_op jit(solution)/shard_map/all_to_all | solution.py:259
  17.3 0.8 reshape_squeeze.3
  18.5 1.1 reshape.111.amps_ref
  19.6 7.7 %all-to-all-done = bf16[16,24,768]{2,1,0:T(8,128)(2,1)S(1)} async-done(((bf16[16,24,768]{2,1,0:T(8,128)(2,1)}), bf16[16,24,768]{2,1,0:T(8,128)(2,1)S(1)}, u32[]{:S(2)}, u32[]{:S(2)}) %all-to-all-start) | async-done | bytes 589856 | tf_op jit(solution)/shard_map/all_to_all | solution.py:259
  27.3 1.4 shard_map.46
  28.9 2.0 %collective-permute-done.sent_ref = bf16[4,4,24,768]{3,2,1,0:T(8,128)(2,1)S(1)} collective-permute-done((bf16[4,4,24,768]{3,2,1,0:T(8,128)(2,1)S(1)}, bf16[4,4,24,768]{3,2,1,0:T(8,128)(2,1)S(1)}, u32[]{:S(2)}, u32[]{:S(2)}) %collective-permute-start) | collective-permute-done | bytes 589856 | tf_op jit(solution)/shard_map/c1_589kB/ppermute | solution.py:26
  30.9 1.4 shard_map.47
  32.3 13.7 %all_to_all.10.parts_ref = bf16[4,4,24,768]{3,2,1,0:T(8,128)(2,1)S(1)} all-to-all(bf16[4,4,24,768]{3,2,1,0:T(8,128)(2,1)S(1)} %get-tuple-element.34), channel_id=1, replica_groups=mesh['y'=4,'z'=8,'x'=4,'c'=2] {'x'}, dimensions={0} | all-to-all | bytes 1179648 | tf_op jit(solution)/shard_map/all_to_all | solution.py:264
  46.2 0.8 copy-done.1
  47.0 6.7 %all-gather.6.cloned.1.call-done.other_ref.amps_ref = bf16[768,1536]{1,0:T(8,128)(2,1)} async-done(((bf16[96,1536]{1,0:T(8,128)(2,1)}), bf16[768,1536]{1,0:T(8,128)(2,1)}) %all-gather.6.cloned.1.call-update) | async-done | bytes 2359312 | tf_op jit(solution)/shard_map/all_gather | solution.py:254
  53.7 1.1 collective-permute-start.1
  54.8 2.1 %collective-permute-start.2 = (bf16[384,768]{1,0:T(8,128)(2,1)}, bf16[384,768]{1,0:T(8,128)(2,1)S(1)}, u32[]{:S(2)}, u32[]{:S(2)}) collective-permute-start(bf16[384,768]{1,0:T(8,128)(2,1)} %shard_map.49.refs_0_), channel_id=1, source_target_pairs={{0,56},{8,0},{16,8},{24,16},{32,24},{40,32},{48,40},{56,48},{1,57}... | collective-permute-start | bytes 1769480 | tf_op jit(solution)/shard_map/z-1_589kB/ppermute | solution.py:26
  57.0 10.5 %collective-permute-done.1.refs_1_ = bf16[384,768]{1,0:T(8,128)(2,1)S(1)} collective-permute-done((bf16[384,768]{1,0:T(8,128)(2,1)}, bf16[384,768]{1,0:T(8,128)(2,1)S(1)}, u32[]{:S(2)}, u32[]{:S(2)}) %collective-permute-start.1) | collective-permute-done | bytes 589856 | tf_op jit(solution)/shard_map/z1_589kB/ppermute | solution.py:26
  67.5 3.1 %collective-permute-start.4 = (bf16[384,768]{1,0:T(8,128)(2,1)S(1)}, bf16[384,768]{1,0:T(8,128)(2,1)S(1)}, u32[]{:S(2)}, u32[]{:S(2)}) collective-permute-start(bf16[384,768]{1,0:T(8,128)(2,1)S(1)} %collective-permute-done.2.refs_2_), channel_id=1, source_target_pairs={{0,56},{8,0},{16,8},{24,16},{32,24},{40,32},{48,40},{56,48},{1,57}... | collective-permute-start | bytes 1769480 | tf_op jit(solution)/shard_map/z-1_589kB/ppermute | solution.py:26
  70.7 10.1 %collective-permute-done.3.refs_3_ = bf16[384,768]{1,0:T(8,128)(2,1)S(1)} collective-permute-done((bf16[384,768]{1,0:T(8,128)(2,1)S(1)}, bf16[384,768]{1,0:T(8,128)(2,1)S(1)}, u32[]{:S(2)}, u32[]{:S(2)}) %collective-permute-start.3) | collective-permute-done | bytes 589856 | tf_op jit(solution)/shard_map/z1_589kB/ppermute | solution.py:26
  80.9 3.1 %collective-permute-start.6 = (bf16[384,768]{1,0:T(8,128)(2,1)S(1)}, bf16[384,768]{1,0:T(8,128)(2,1)S(1)}, u32[]{:S(2)}, u32[]{:S(2)}) collective-permute-start(bf16[384,768]{1,0:T(8,128)(2,1)S(1)} %collective-permute-done.4.refs_4_), channel_id=1, source_target_pairs={{0,56},{8,0},{16,8},{24,16},{32,24},{40,32},{48,40},{56,48},{1,57}... | collective-permute-start | bytes 1769480 | tf_op jit(solution)/shard_map/z-1_589kB/ppermute | solution.py:26
  84.1 9.0 %collective-permute-done.5.refs_5_.fore_ref = bf16[384,768]{1,0:T(8,128)(2,1)S(1)} collective-permute-done((bf16[384,768]{1,0:T(8,128)(2,1)S(1)}, bf16[384,768]{1,0:T(8,128)(2,1)S(1)}, u32[]{:S(2)}, u32[]{:S(2)}) %collective-permute-start.5) | collective-permute-done | bytes 589856 | tf_op jit(solution)/shard_map/z1_589kB/ppermute | solution.py:26
  93.1 0.8 shard_map.51
  93.9 0.6 collective-permute-start.7
  94.5 2.7 %collective-permute-start.8 = (bf16[384,384]{1,0:T(8,128)(2,1)}, bf16[384,384]{1,0:T(8,128)(2,1)S(1)}, u32[]{:S(2)}, u32[]{:S(2)}) collective-permute-start(bf16[384,384]{1,0:T(8,128)(2,1)} %get-tuple-element.39), channel_id=1, source_target_pairs={{0,56},{8,0},{16,8},{24,16},{32,24},{40,32},{48,40},{56,48},{1,57}... | collective-permute-start | bytes 884744 | tf_op jit(solution)/shard_map/z-1_294kB/ppermute | solution.py:26
  97.2 1.7 %copy-done.3 = bf16[384,3072]{1,0:T(8,128)(2,1)S(1)} copy-done((bf16[384,3072]{1,0:T(8,128)(2,1)S(1)}, bf16[384,3072]{1,0:T(8,128)(2,1)}, u32[]{:S(2)}) %copy-start.3) | copy-done | bytes 2359320
  98.9 1.1 copy-done.6
  100.0 1.1 copy-done.8
  101.0 3.0 %shard_map.50 = (f32[384,768]{1,0:T(8,128)S(1)}, bf16[8,384,768]{2,1,0:T(8,128)(2,1)S(1)}, bf16[384,384]{1,0:T(8,128)(2,1)S(1)}) custom-call(s32[3]{0:T(128)S(1)} %pad_add_fusion.place_ref, bf16[384,3072]{1,0:T(8,128)(2,1)S(1)} %copy-done.3, bf16[384,768]{1,0:T(8,128)(2,1)S(1)} %copy-done.2, bf16[384,768]{1,0:T(8,128)(2,1)S(1)} %collective-permute-done.1.refs_1_, ...), custom_call_target="tpu_custom_call" | custom-call | flops 1585446912 | bytes 8388608 | tf_op jit(solution)/shard_map/pallas_call | solution.py:167
  104.0 1.7 %shard_map.52 = (bf16[384,768]{1,0:T(8,128)(2,1)S(1)}, bf16[384,384]{1,0:T(8,128)(2,1)S(1)}, bf16[384,384]{1,0:T(8,128)(2,1)S(1)}) custom-call(s32[3]{0:T(128)S(1)} %pad_add_fusion.place_ref, bf16[384,384]{1,0:T(8,128)(2,1)S(1)} %get-tuple-element.35.amps_ref, f32[384,768]{1,0:T(8,128)S(1)} %get-tuple-element.36.acc_ref, ...), custom_call_target="tpu_custom_call" | custom-call | flops 679477248 | bytes 8388608 | tf_op jit(solution)/shard_map/pallas_call | solution.py:279
  105.7 1.9 %collective-permute-start.11 = (bf16[384,384]{1,0:T(8,128)(2,1)S(1)}, bf16[384,384]{1,0:T(8,128)(2,1)S(1)}, u32[]{:S(2)}, u32[]{:S(2)}) collective-permute-start(bf16[384,384]{1,0:T(8,128)(2,1)S(1)} %get-tuple-element.46), channel_id=1, source_target_pairs={{0,64},{64,128},{128,192},{192,0},{1,65},{65,129},{129,193},{193,1... | collective-permute-start | bytes 884744 | tf_op jit(solution)/shard_map/y1_294kB/ppermute | solution.py:26
  107.6 1.5 collective-permute-start.13
  109.1 2.3 %shard_map.53 = (f32[384,384]{1,0:T(8,128)S(1)}, bf16[384,384]{1,0:T(8,128)(2,1)S(1)}, bf16[384,384]{1,0:T(8,128)(2,1)S(1)}, f32[384,384]{1,0:T(8,128)S(1)}, f32...) custom-call(s32[3]{0:T(128)S(1)} %pad_add_fusion.place_ref, ...), custom_call_target="tpu_custom_call" | custom-call | flops 1358954496 | bytes 8388608 | tf_op jit(solution)/shard_map/pallas_call | solution.py:287
  111.4 0.6 collective-permute-start.10
  112.0 2.7 %collective-permute-start.9 = (bf16[384,384]{1,0:T(8,128)(2,1)S(1)}, bf16[384,384]{1,0:T(8,128)(2,1)S(1)}, u32[]{:S(2)}, u32[]{:S(2)}) collective-permute-start(bf16[384,384]{1,0:T(8,128)(2,1)S(1)} %get-tuple-element.43), channel_id=1, source_target_pairs={{0,192},{64,0},{128,64},{192,128},{1,193},{65,1},{129,65},{193,129... | collective-permute-start | bytes 884744 | tf_op jit(solution)/shard_map/y-1_294kB/ppermute | solution.py:26
  114.7 2.3 %collective-permute-done.11 = bf16[384,384]{1,0:T(8,128)(2,1)S(1)} collective-permute-done((bf16[384,384]{1,0:T(8,128)(2,1)S(1)}, bf16[384,384]{1,0:T(8,128)(2,1)S(1)}, u32[]{:S(2)}, u32[]{:S(2)}) %collective-permute-start.11) | collective-permute-done | bytes 294944 | tf_op jit(solution)/shard_map/y1_294kB/ppermute | solution.py:26
  117.2 3.3 %collective-permute-start.14 = (bf16[384,384]{1,0:T(8,128)(2,1)S(1)}, bf16[384,384]{1,0:T(8,128)(2,1)S(1)}, u32[]{:S(2)}, u32[]{:S(2)}) collective-permute-start(bf16[384,384]{1,0:T(8,128)(2,1)S(1)} %add_convert_fusion.2), channel_id=1, source_target_pairs={{0,192},{64,0},{128,64},{192,128},{1,193},{65,1},{129,65},{193,129... | collective-permute-start | bytes 884744 | tf_op jit(solution)/shard_map/y-1_294kB/ppermute | solution.py:26
  120.7 5.0 %collective-permute-done.12 = bf16[384,384]{1,0:T(8,128)(2,1)S(1)} collective-permute-done((bf16[384,384]{1,0:T(8,128)(2,1)S(1)}, bf16[384,384]{1,0:T(8,128)(2,1)S(1)}, u32[]{:S(2)}, u32[]{:S(2)}) %collective-permute-start.12) | collective-permute-done | bytes 294944 | tf_op jit(solution)/shard_map/y1_294kB/ppermute | solution.py:26
  125.9 2.0 %shard_map.54 = (f32[96,1536]{1,0:T(8,128)S(1)}, f32[96,1536]{1,0:T(8,128)S(1)}, bf16[96,1536]{1,0:T(8,128)(2,1)S(1)}, bf16[96,1536]{1,0:T(8,128)(2,1)S(1)}) custom-call(s32[3]{0:T(128)S(1)} %pad_add_fusion.place_ref, f32[384,768]{1,0:T(8,128)S(1)} %fusion.total_ref, bf16[768,1536]{1,0:T(8,128)(2,1)S(1)} %get-tuple-element.49.amps_ref), custom_call_target="tpu_custom_call" | custom-call | flops 905969664 | bytes 8388608 | tf_op jit(solution)/shard_map/pallas_call | solution.py:229
  128.0 5.5 %all-gather.8.cloned.1.call-done.amps_ref = bf16[768,1536]{1,0:T(8,128)(2,1)} async-done(((bf16[96,1536]{1,0:T(8,128)(2,1)}), bf16[768,1536]{1,0:T(8,128)(2,1)}) %all-gather.8.cloned.1.call-update) | async-done | bytes 2359312 | tf_op jit(solution)/shard_map/all_gather | solution.py:275
  133.5 1.7 %copy-done.4 = bf16[768,1536]{1,0:T(8,128)(2,1)S(1)} copy-done((bf16[768,1536]{1,0:T(8,128)(2,1)S(1)}, bf16[768,1536]{1,0:T(8,128)(2,1)}, u32[]{:S(2)}) %copy-start.4) | copy-done | bytes 2359320
  135.1 1.9 %shard_map.55 = (f32[96,1536]{1,0:T(8,128)S(1)}, bf16[96,1536]{1,0:T(8,128)(2,1)S(1)}, bf16[96,1536]{1,0:T(8,128)(2,1)S(1)}, f32[96,1536]{1,0:T(8,128)S(1)}) custom-call(s32[3]{0:T(128)S(1)} %pad_add_fusion.place_ref, f32[384,768]{1,0:T(8,128)S(1)} %fusion.total_ref, bf16[768,1536]{1,0:T(8,128)(2,1)S(1)} %copy-done.4), custom_call_target="tpu_custom_call" | custom-call | flops 905969664 | bytes 8388608 | tf_op jit(solution)/shard_map/pallas_call | solution.py:229
  137.1 2.9 %collective-permute-start.19 = (bf16[96,1536]{1,0:T(8,128)(2,1)S(1)}, bf16[96,1536]{1,0:T(8,128)(2,1)S(1)}, u32[]{:S(2)}, u32[]{:S(2)}) collective-permute-start(bf16[96,1536]{1,0:T(8,128)(2,1)S(1)} %get-tuple-element.58), channel_id=1, source_target_pairs={{0,192},{64,0},{128,64},{192,128},{1,193},{65,1},{129,65},{193,129... | collective-permute-start | bytes 884744 | tf_op jit(solution)/shard_map/y-1_294kB/ppermute | solution.py:26
  140.0 0.8 collective-permute-start.15
  140.8 1.2 collective-permute-start.16
  142.2 5.3 %collective-permute-done.19 = bf16[96,1536]{1,0:T(8,128)(2,1)S(1)} collective-permute-done((bf16[96,1536]{1,0:T(8,128)(2,1)S(1)}, bf16[96,1536]{1,0:T(8,128)(2,1)S(1)}, u32[]{:S(2)}, u32[]{:S(2)}) %collective-permute-start.19) | collective-permute-done | bytes 294944 | tf_op jit(solution)/shard_map/y-1_294kB/ppermute | solution.py:26
  147.5 3.8 %collective-permute-start.20 = (bf16[96,1536]{1,0:T(8,128)(2,1)S(1)}, bf16[96,1536]{1,0:T(8,128)(2,1)S(1)}, u32[]{:S(2)}, u32[]{:S(2)}) collective-permute-start(bf16[96,1536]{1,0:T(8,128)(2,1)S(1)} %add_convert_fusion), channel_id=1, source_target_pairs={{0,192},{64,0},{128,64},{192,128},{1,193},{65,1},{129,65},{193,129... | collective-permute-start | bytes 884744 | tf_op jit(solution)/shard_map/y-1_294kB/ppermute | solution.py:26
  151.3 1.5 collective-permute-done.15
  152.8 0.8 collective-permute-done.18
  153.6 2.4 %collective-permute-done.20 = bf16[96,1536]{1,0:T(8,128)(2,1)S(1)} collective-permute-done((bf16[96,1536]{1,0:T(8,128)(2,1)S(1)}, bf16[96,1536]{1,0:T(8,128)(2,1)S(1)}, u32[]{:S(2)}, u32[]{:S(2)}) %collective-permute-start.20) | collective-permute-done | bytes 294944 | tf_op jit(solution)/shard_map/y-1_294kB/ppermute | solution.py:26
  156.0 1.1 fusion.4
  (56 shorter events, 2.5 us)
Async XLA Ops:
  6.5 1.9 %copy-start.12 = (bf16[1,3000,96]{1,2,0:T(8,128)(2,1)S(1)}, bf16[1,3000,96]{1,2,0:T(8,128)(2,1)}, u32[]{:S(2)}) copy-start(bf16[1,3000,96]{1,2,0:T(8,128)(2,1)} %param.5) | copy-start | bytes 1728004
  6.5 47.2 %all-gather.6.cloned.1.call-start = ((), (), s32[]{:S(2)}) async-start(), calls=%async_computation.3 | async-start | bytes 2654208 | tf_op jit(solution)/shard_map/all_gather | solution.py:254
  8.9 8.4 %copy-start.10 = (bf16[1,96,3072]{2,1,0:T(8,128)(2,1)S(1)}, bf16[1,96,3072]{2,1,0:T(8,128)(2,1)}, u32[]{:S(2)}) copy-start(bf16[1,96,3072]{2,1,0:T(8,128)(2,1)} %param.6) | copy-start | bytes 1769476
  9.8 17.5 %all-to-all-start = ((bf16[16,24,768]{2,1,0:T(8,128)(2,1)}), bf16[16,24,768]{2,1,0:T(8,128)(2,1)S(1)}, u32[]{:S(2)}, u32[]{:S(2)}) async-start(bf16[16,24,768]{2,1,0:T(8,128)(2,1)} %bitcast.6), calls=%async_computation | async-start | bytes 1179648 | tf_op jit(solution)/shard_map/all_to_all | solution.py:259
  17.3 79.9 %all-gather.4.cloned.1.call-start = ((), (), s32[]{:S(2)}) async-start(), calls=%async_computation.2 | async-start | bytes 2949120 | tf_op jit(solution)/shard_map/all_gather | solution.py:263
  18.1 9.2 %copy-start.9 = (s32[8]{0:T(128)S(1)}, s32[8]{0:T(128)}, u32[]{:S(2)}) copy-start(s32[8]{0:T(128)} %table_ref.3) | copy-start | bytes 100
  28.8 104.7 %all-gather.8.cloned.1.call-start = ((), (), s32[]{:S(2)}) async-start(), calls=%async_computation.4 | async-start | bytes 2654208 | tf_op jit(solution)/shard_map/all_gather | solution.py:275
  28.8 2.1 %collective-permute-start = (bf16[4,4,24,768]{3,2,1,0:T(8,128)(2,1)S(1)}, bf16[4,4,24,768]{3,2,1,0:T(8,128)(2,1)S(1)}, u32[]{:S(2)}, u32[]{:S(2)}) collective-permute-start(bf16[4,4,24,768]{3,2,1,0:T(8,128)(2,1)S(1)} %get-tuple-element.33), channel_id=1, source_target_pairs={{0,1},{1,0},{2,3},{3,2},{4,5},{5,4},{6,7},{7,6},{8,9},{9,8},{10,11... | collective-permute-start | bytes 1769480 | tf_op jit(solution)/shard_map/c1_589kB/ppermute | solution.py:26
  46.2 0.8 copy-start.1
  53.7 43.5 %copy-start.2 = (bf16[384,768]{1,0:T(8,128)(2,1)S(1)}, bf16[384,768]{1,0:T(8,128)(2,1)}, u32[]{:S(2)}) copy-start(bf16[384,768]{1,0:T(8,128)(2,1)} %shard_map.49.refs_0_) | copy-start | bytes 1769476
  53.7 13.7 %collective-permute-start.1 = (bf16[384,768]{1,0:T(8,128)(2,1)}, bf16[384,768]{1,0:T(8,128)(2,1)S(1)}, u32[]{:S(2)}, u32[]{:S(2)}) collective-permute-start(bf16[384,768]{1,0:T(8,128)(2,1)} %shard_map.49.refs_0_), channel_id=1, source_target_pairs={{0,8},{8,16},{16,24},{24,32},{32,40},{40,48},{48,56},{56,0},{1,9},... | collective-permute-start | bytes 1769480 | tf_op jit(solution)/shard_map/z1_589kB/ppermute | solution.py:26
  54.8 12.7 %collective-permute-start.2 = (bf16[384,768]{1,0:T(8,128)(2,1)}, bf16[384,768]{1,0:T(8,128)(2,1)S(1)}, u32[]{:S(2)}, u32[]{:S(2)}) collective-permute-start(bf16[384,768]{1,0:T(8,128)(2,1)} %shard_map.49.refs_0_), channel_id=1, source_target_pairs={{0,56},{8,0},{16,8},{24,16},{32,24},{40,32},{48,40},{56,48},{1,57}... | collective-permute-start | bytes 1769480 | tf_op jit(solution)/shard_map/z-1_589kB/ppermute | solution.py:26
  67.4 13.4 %collective-permute-start.3 = (bf16[384,768]{1,0:T(8,128)(2,1)S(1)}, bf16[384,768]{1,0:T(8,128)(2,1)S(1)}, u32[]{:S(2)}, u32[]{:S(2)}) collective-permute-start(bf16[384,768]{1,0:T(8,128)(2,1)S(1)} %collective-permute-done.1.refs_1_), channel_id=1, source_target_pairs={{0,8},{8,16},{16,24},{24,32},{32,40},{40,48},{48,56},{56,0},{1,9},... | collective-permute-start | bytes 1769480 | tf_op jit(solution)/shard_map/z1_589kB/ppermute | solution.py:26
  67.5 13.4 %collective-permute-start.4 = (bf16[384,768]{1,0:T(8,128)(2,1)S(1)}, bf16[384,768]{1,0:T(8,128)(2,1)S(1)}, u32[]{:S(2)}, u32[]{:S(2)}) collective-permute-start(bf16[384,768]{1,0:T(8,128)(2,1)S(1)} %collective-permute-done.2.refs_2_), channel_id=1, source_target_pairs={{0,56},{8,0},{16,8},{24,16},{32,24},{40,32},{48,40},{56,48},{1,57}... | collective-permute-start | bytes 1769480 | tf_op jit(solution)/shard_map/z-1_589kB/ppermute | solution.py:26
  80.8 13.1 %copy-start.5 = (bf16[384,768]{1,0:T(8,128)(2,1)}, bf16[384,768]{1,0:T(8,128)(2,1)S(1)}, u32[]{:S(2)}) copy-start(bf16[384,768]{1,0:T(8,128)(2,1)S(1)} %collective-permute-done.3.refs_3_) | copy-start | bytes 1769476
  80.8 12.3 %collective-permute-start.5 = (bf16[384,768]{1,0:T(8,128)(2,1)S(1)}, bf16[384,768]{1,0:T(8,128)(2,1)S(1)}, u32[]{:S(2)}, u32[]{:S(2)}) collective-permute-start(bf16[384,768]{1,0:T(8,128)(2,1)S(1)} %collective-permute-done.3.refs_3_), channel_id=1, source_target_pairs={{0,8},{8,16},{16,24},{24,32},{32,40},{40,48},{48,56},{56,0},{1,9},... | collective-permute-start | bytes 1769480 | tf_op jit(solution)/shard_map/z1_589kB/ppermute | solution.py:26
  80.9 13.5 %copy-start.7 = (bf16[384,768]{1,0:T(8,128)(2,1)}, bf16[384,768]{1,0:T(8,128)(2,1)S(1)}, u32[]{:S(2)}) copy-start(bf16[384,768]{1,0:T(8,128)(2,1)S(1)} %collective-permute-done.4.refs_4_) | copy-start | bytes 1769476
  80.9 12.1 %collective-permute-start.6 = (bf16[384,768]{1,0:T(8,128)(2,1)S(1)}, bf16[384,768]{1,0:T(8,128)(2,1)S(1)}, u32[]{:S(2)}, u32[]{:S(2)}) collective-permute-start(bf16[384,768]{1,0:T(8,128)(2,1)S(1)} %collective-permute-done.4.refs_4_), channel_id=1, source_target_pairs={{0,56},{8,0},{16,8},{24,16},{32,24},{40,32},{48,40},{56,48},{1,57}... | collective-permute-start | bytes 1769480 | tf_op jit(solution)/shard_map/z-1_589kB/ppermute | solution.py:26
  93.9 10.1 %collective-permute-start.7 = (bf16[384,384]{1,0:T(8,128)(2,1)}, bf16[384,384]{1,0:T(8,128)(2,1)S(1)}, u32[]{:S(2)}, u32[]{:S(2)}) collective-permute-start(bf16[384,384]{1,0:T(8,128)(2,1)} %get-tuple-element.38), channel_id=1, source_target_pairs={{0,8},{8,16},{16,24},{24,32},{32,40},{40,48},{48,56},{56,0},{1,9},... | collective-permute-start | bytes 884744 | tf_op jit(solution)/shard_map/z1_294kB/ppermute | solution.py:26
  94.5 9.5 %collective-permute-start.8 = (bf16[384,384]{1,0:T(8,128)(2,1)}, bf16[384,384]{1,0:T(8,128)(2,1)S(1)}, u32[]{:S(2)}, u32[]{:S(2)}) collective-permute-start(bf16[384,384]{1,0:T(8,128)(2,1)} %get-tuple-element.39), channel_id=1, source_target_pairs={{0,56},{8,0},{16,8},{24,16},{32,24},{40,32},{48,40},{56,48},{1,57}... | collective-permute-start | bytes 884744 | tf_op jit(solution)/shard_map/z-1_294kB/ppermute | solution.py:26
  97.2 1.7 %copy-start.3 = (bf16[384,3072]{1,0:T(8,128)(2,1)S(1)}, bf16[384,3072]{1,0:T(8,128)(2,1)}, u32[]{:S(2)}) copy-start(bf16[384,3072]{1,0:T(8,128)(2,1)} %all-gather.4.cloned.1.call-done.amps_ref) | copy-start | bytes 7077892
  98.9 1.1 copy-start.6
  100.0 1.1 copy-start.8
  104.0 5.0 %copy-start = (bf16[768,1536]{1,0:T(8,128)(2,1)S(1)}, bf16[768,1536]{1,0:T(8,128)(2,1)}, u32[]{:S(2)}) copy-start(bf16[768,1536]{1,0:T(8,128)(2,1)} %all-gather.6.cloned.1.call-done.other_ref.amps_ref) | copy-start | bytes 7077892
  105.7 11.2 %collective-permute-start.11 = (bf16[384,384]{1,0:T(8,128)(2,1)S(1)}, bf16[384,384]{1,0:T(8,128)(2,1)S(1)}, u32[]{:S(2)}, u32[]{:S(2)}) collective-permute-start(bf16[384,384]{1,0:T(8,128)(2,1)S(1)} %get-tuple-element.46), channel_id=1, source_target_pairs={{0,64},{64,128},{128,192},{192,0},{1,65},{65,129},{129,193},{193,1... | collective-permute-start | bytes 884744 | tf_op jit(solution)/shard_map/y1_294kB/ppermute | solution.py:26
  107.6 9.5 %collective-permute-start.13 = (bf16[384,384]{1,0:T(8,128)(2,1)S(1)}, bf16[384,384]{1,0:T(8,128)(2,1)S(1)}, u32[]{:S(2)}, u32[]{:S(2)}) collective-permute-start(bf16[384,384]{1,0:T(8,128)(2,1)S(1)} %get-tuple-element.48), channel_id=1, source_target_pairs={{0,192},{64,0},{128,64},{192,128},{1,193},{65,1},{129,65},{193,129... | collective-permute-start | bytes 884744 | tf_op jit(solution)/shard_map/y-1_294kB/ppermute | solution.py:26
  111.4 9.3 %collective-permute-start.10 = (bf16[384,384]{1,0:T(8,128)(2,1)S(1)}, bf16[384,384]{1,0:T(8,128)(2,1)S(1)}, u32[]{:S(2)}, u32[]{:S(2)}) collective-permute-start(bf16[384,384]{1,0:T(8,128)(2,1)S(1)} %get-tuple-element.44), channel_id=1, source_target_pairs={{0,64},{64,128},{128,192},{192,0},{1,65},{65,129},{129,193},{193,1... | collective-permute-start | bytes 884744 | tf_op jit(solution)/shard_map/y1_294kB/ppermute | solution.py:26
  112.0 8.7 %collective-permute-start.9 = (bf16[384,384]{1,0:T(8,128)(2,1)S(1)}, bf16[384,384]{1,0:T(8,128)(2,1)S(1)}, u32[]{:S(2)}, u32[]{:S(2)}) collective-permute-start(bf16[384,384]{1,0:T(8,128)(2,1)S(1)} %get-tuple-element.43), channel_id=1, source_target_pairs={{0,192},{64,0},{128,64},{192,128},{1,193},{65,1},{129,65},{193,129... | collective-permute-start | bytes 884744 | tf_op jit(solution)/shard_map/y-1_294kB/ppermute | solution.py:26
  117.0 8.7 %collective-permute-start.12 = (bf16[384,384]{1,0:T(8,128)(2,1)S(1)}, bf16[384,384]{1,0:T(8,128)(2,1)S(1)}, u32[]{:S(2)}, u32[]{:S(2)}) collective-permute-start(bf16[384,384]{1,0:T(8,128)(2,1)S(1)} %add_convert_fusion.3), channel_id=1, source_target_pairs={{0,64},{64,128},{128,192},{192,0},{1,65},{65,129},{129,193},{193,1... | collective-permute-start | bytes 884744 | tf_op jit(solution)/shard_map/y1_294kB/ppermute | solution.py:26
  117.2 8.5 %collective-permute-start.14 = (bf16[384,384]{1,0:T(8,128)(2,1)S(1)}, bf16[384,384]{1,0:T(8,128)(2,1)S(1)}, u32[]{:S(2)}, u32[]{:S(2)}) collective-permute-start(bf16[384,384]{1,0:T(8,128)(2,1)S(1)} %add_convert_fusion.2), channel_id=1, source_target_pairs={{0,192},{64,0},{128,64},{192,128},{1,193},{65,1},{129,65},{193,129... | collective-permute-start | bytes 884744 | tf_op jit(solution)/shard_map/y-1_294kB/ppermute | solution.py:26
  127.9 14.1 %collective-permute-start.17 = (bf16[96,1536]{1,0:T(8,128)(2,1)S(1)}, bf16[96,1536]{1,0:T(8,128)(2,1)S(1)}, u32[]{:S(2)}, u32[]{:S(2)}) collective-permute-start(bf16[96,1536]{1,0:T(8,128)(2,1)S(1)} %get-tuple-element.56), channel_id=1, source_target_pairs={{0,64},{64,128},{128,192},{192,0},{1,65},{65,129},{129,193},{193,1... | collective-permute-start | bytes 884744 | tf_op jit(solution)/shard_map/y1_294kB/ppermute | solution.py:26
  133.5 1.7 %copy-start.4 = (bf16[768,1536]{1,0:T(8,128)(2,1)S(1)}, bf16[768,1536]{1,0:T(8,128)(2,1)}, u32[]{:S(2)}) copy-start(bf16[768,1536]{1,0:T(8,128)(2,1)} %all-gather.8.cloned.1.call-done.amps_ref) | copy-start | bytes 7077892
  137.1 10.4 %collective-permute-start.19 = (bf16[96,1536]{1,0:T(8,128)(2,1)S(1)}, bf16[96,1536]{1,0:T(8,128)(2,1)S(1)}, u32[]{:S(2)}, u32[]{:S(2)}) collective-permute-start(bf16[96,1536]{1,0:T(8,128)(2,1)S(1)} %get-tuple-element.58), channel_id=1, source_target_pairs={{0,192},{64,0},{128,64},{192,128},{1,193},{65,1},{129,65},{193,129... | collective-permute-start | bytes 884744 | tf_op jit(solution)/shard_map/y-1_294kB/ppermute | solution.py:26
  140.0 12.8 %collective-permute-start.15 = (bf16[96,1536]{1,0:T(8,128)(2,1)S(1)}, bf16[96,1536]{1,0:T(8,128)(2,1)S(1)}, u32[]{:S(2)}, u32[]{:S(2)}) collective-permute-start(bf16[96,1536]{1,0:T(8,128)(2,1)S(1)} %get-tuple-element.53), channel_id=1, source_target_pairs={{0,192},{64,0},{128,64},{192,128},{1,193},{65,1},{129,65},{193,129... | collective-permute-start | bytes 884744 | tf_op jit(solution)/shard_map/y-1_294kB/ppermute | solution.py:26
  140.8 12.0 %collective-permute-start.16 = (bf16[96,1536]{1,0:T(8,128)(2,1)S(1)}, bf16[96,1536]{1,0:T(8,128)(2,1)S(1)}, u32[]{:S(2)}, u32[]{:S(2)}) collective-permute-start(bf16[96,1536]{1,0:T(8,128)(2,1)S(1)} %get-tuple-element.54), channel_id=1, source_target_pairs={{0,64},{64,128},{128,192},{192,0},{1,65},{65,129},{129,193},{193,1... | collective-permute-start | bytes 884744 | tf_op jit(solution)/shard_map/y1_294kB/ppermute | solution.py:26
  142.0 13.9 %copy-start.11 = (f32[1,96,3072]{2,1,0:T(8,128)S(1)}, f32[1,96,3072]{2,1,0:T(8,128)}, u32[]{:S(2)}) copy-start(f32[1,96,3072]{2,1,0:T(8,128)} %param.7) | copy-start | bytes 3538948
  142.1 11.5 %collective-permute-start.18 = (bf16[96,1536]{1,0:T(8,128)(2,1)S(1)}, bf16[96,1536]{1,0:T(8,128)(2,1)S(1)}, u32[]{:S(2)}, u32[]{:S(2)}) collective-permute-start(bf16[96,1536]{1,0:T(8,128)(2,1)S(1)} %add_convert_fusion.1), channel_id=1, source_target_pairs={{0,64},{64,128},{128,192},{192,0},{1,65},{65,129},{129,193},{193,1... | collective-permute-start | bytes 884744 | tf_op jit(solution)/shard_map/y1_294kB/ppermute | solution.py:26
  147.5 8.4 %collective-permute-start.20 = (bf16[96,1536]{1,0:T(8,128)(2,1)S(1)}, bf16[96,1536]{1,0:T(8,128)(2,1)S(1)}, u32[]{:S(2)}, u32[]{:S(2)}) collective-permute-start(bf16[96,1536]{1,0:T(8,128)(2,1)S(1)} %add_convert_fusion), channel_id=1, source_target_pairs={{0,192},{64,0},{128,64},{192,128},{1,193},{65,1},{129,65},{193,129... | collective-permute-start | bytes 884744 | tf_op jit(solution)/shard_map/y-1_294kB/ppermute | solution.py:26
Sparse Core Ops, SparseCore 0:
  9.1 44.5 all-gather.5
  55.5 34.3 all-gather.3
  91.7 41.7 all-gather.7
